TPU v7x, 32 devices: a whole 2x2x4 slice. The times are simulated.
32 devices in a mesh: groups: 2 (over x), refl: 8 (over z, y), freq: 2 (over core).
Axes of the slice: x: 2, y: 2, z: 4, core: 2. Of those that a mesh axis runs over, the one named last changes fastest.
Arguments:
- spectra: bfloat16 [2, 16, 1024, 8192], P(None, 'freq', 'groups', 'refl'), parts along dimension 2, may hold values from -9 to 9
- recorded: bfloat16 [8, 2, 64, 64, 256], P('refl', 'freq', 'groups'), parts along dimension 2, may hold values from -10 to 10
- initial_filters: float32 [8, 2, 2, 2, 33], P('refl', 'freq', 'groups'), parts along dimension 2, may hold values from -0.6 to 0.6
Outputs:
- primaries: bfloat16 [8, 2, 64, 64, 256], P('refl', 'freq', 'groups'), parts along dimension 2
- filters: float32 [8, 2, 2, 2, 33], P('refl', 'freq', 'groups'), parts along dimension 2
There are 2 independent parts, one for each index of `groups`. A program takes and returns all parts, laid end to end along the dimension named above; each array names one. Nothing has to cross between parts.
All inputs are finite; a program needn't handle non-finite values.
Results may differ from a plain program's by a relative error of at most 0.025.
Values may be sent and summed in bfloat16 or wider, within the bound.
No kernel may reach another device: no remote copies, remote signals or barrier semaphores. Data moves between devices by JAX's collectives and lax.ppermute only.
A program may use at most 128 MiB of HBM per device.

v0:
```python
import math

import jax
import jax.numpy as jnp
from jax import lax
from jax.sharding import PartitionSpec as P

NF = 16
K0 = 48
NT = 256
XR = 8192
WC = 32
WM = 4
TAPS = 33
ITERS = 3


EXACT_PRECISION = lax.Precision.HIGHEST


def passed_along(block, axis, distance):
    devices = range(lax.axis_size(axis))
    route = [((i - distance) % len(devices), i) for i in devices]
    return lax.ppermute(block, axis, route)


def time_table():
    frequency_bins = jnp.arange(NF, dtype=jnp.int32)
    samples = jnp.arange(NT, dtype=jnp.int32)
    phases = (K0 + frequency_bins)[:, None] * samples[None, :] % NT
    angles = 2.0 * math.pi / NT * phases.astype(jnp.float32)
    weight = math.sqrt(2.0 / NF)
    return jnp.stack([weight * jnp.cos(angles), -weight * jnp.sin(angles)], axis=1).astype(
        jnp.bfloat16
    )


def lag_sums(matrix):
    length = matrix.shape[-1]
    leading = matrix.shape[:-2]
    doubled = jnp.concatenate([matrix, matrix], axis=-1).reshape(leading + (2 * length * length,))
    padded = jnp.concatenate([doubled, jnp.zeros(leading + (length,), matrix.dtype)], axis=-1)
    skewed = padded.reshape(leading + (length, 2 * length + 1))
    return jnp.sum(skewed, axis=-2)[..., :length]


def solve_filters(gram_sums, cross_sums, initial):
    length = gram_sums.shape[-1]
    half_taps = (TAPS - 1) // 2
    lag_gram = lag_sums(gram_sums)[..., :TAPS]
    lag_cross = lag_sums(cross_sums)
    target = jnp.concatenate(
        [
            jnp.flip(lag_cross[..., : half_taps + 1], -1),
            jnp.flip(lag_cross[..., length - half_taps :], -1),
        ],
        -1,
    )
    row_bound = lag_gram[..., 0] + 2.0 * jnp.sum(jnp.abs(lag_gram[..., 1:]), -1)
    step_size = 0.5 / (row_bound + 1e-06)
    tap_index = jnp.arange(TAPS, dtype=jnp.int32)
    offset = jnp.abs(tap_index[:, None] - tap_index[None, :])
    select = (offset[:, :, None] == tap_index[None, None, :]).astype(jnp.float32)
    toeplitz = jnp.einsum("abk,...k->...ab", select, lag_gram, precision=EXACT_PRECISION)
    filters = initial
    for repeat in range(ITERS):
        applied = jnp.einsum("...ab,...b->...a", toeplitz, filters, precision=EXACT_PRECISION)
        filters = filters + step_size[..., None] * (target - applied)
    return filters


def conv_matrix(taps):
    half_taps = (TAPS - 1) // 2
    positions = jnp.arange(NT, dtype=jnp.int32)
    circular_shift = (positions[None, :] - positions[:, None]) % NT
    wanted = (jnp.arange(TAPS, dtype=jnp.int32) - half_taps) % NT
    select = (circular_shift[None] == wanted[:, None, None]).astype(jnp.float32)
    return jnp.einsum(
        "kut,...k->...ut", select, taps.astype(jnp.float32), precision=EXACT_PRECISION
    ).astype(jnp.bfloat16)


def to_time(exchanged):
    freq_count = exchanged.shape[1]
    item_count = exchanged.shape[2]
    half_width = exchanged.shape[4] // 2
    spectrum = exchanged.reshape(freq_count, item_count, 2, half_width)
    return jnp.einsum(
        "fsab,fat->sbt", spectrum, time_table(), preferred_element_type=jnp.float32
    ).astype(jnp.bfloat16)


def extend(multiples, recorded_tile):
    freq_blocks = lax.axis_size("freq")
    tile_columns = 4 * freq_blocks
    row_total = lax.axis_size("refl") * freq_blocks // tile_columns
    grid_index = (lax.axis_index(("refl", "freq")) + 2 * freq_blocks) % (row_total * tile_columns)
    column_index = grid_index % tile_columns
    row_index = grid_index // tile_columns
    margins = []
    for offset in (1, -1):
        if offset == 1:
            rim_multiples = multiples[:, -WM:]
            rim_recorded = recorded_tile[:, -WM:]
            allowed = column_index != 0
        else:
            rim_multiples = multiples[:, :WM]
            rim_recorded = recorded_tile[:, :WM]
            allowed = column_index != tile_columns - 1
        got_multiples, got_recorded = passed_along(
            (rim_multiples, rim_recorded), ("refl", "freq"), offset
        )
        margins.append(
            (
                jnp.where(allowed, got_multiples, jnp.zeros_like(got_multiples)),
                jnp.where(allowed, got_recorded, jnp.zeros_like(got_recorded)),
            )
        )
    wide_multiples = jnp.concatenate([margins[0][0], multiples, margins[1][0]], axis=1)
    wide_recorded = jnp.concatenate([margins[0][1], recorded_tile, margins[1][1]], axis=1)
    bands = []
    for offset in (tile_columns, -tile_columns):
        if offset > 0:
            rim_multiples = wide_multiples[-WM:]
            rim_recorded = wide_recorded[-WM:]
            allowed = row_index != 0
        else:
            rim_multiples = wide_multiples[:WM]
            rim_recorded = wide_recorded[:WM]
            allowed = row_index != row_total - 1
        got_multiples, got_recorded = passed_along(
            (rim_multiples, rim_recorded), ("refl", "freq"), offset
        )
        bands.append(
            (
                jnp.where(allowed, got_multiples, jnp.zeros_like(got_multiples)),
                jnp.where(allowed, got_recorded, jnp.zeros_like(got_recorded)),
            )
        )
    full_multiples = jnp.concatenate([bands[0][0], wide_multiples, bands[1][0]], axis=0)
    full_recorded = jnp.concatenate([bands[0][1], wide_recorded, bands[1][1]], axis=0)
    return (full_multiples, full_recorded)


def body(spectra, recorded, initial_filters):
    freq_blocks = lax.axis_size("freq")
    refl_devices = lax.axis_size("refl")
    freq_count = spectra.shape[1]
    tile_sources = recorded.shape[2]
    tile_receivers = recorded.shape[3]
    samples = recorded.shape[4]
    source_count = tile_sources * (refl_devices // 4)
    group_width = freq_blocks * tile_receivers
    amplitude = 1.0 / math.sqrt(2.0 * XR)
    real_part = spectra[0]
    imag_part = spectra[1]
    right_side = jnp.concatenate([real_part, imag_part], axis=2)
    left_side = jnp.stack(
        [
            jnp.concatenate([real_part[:, :source_count], -imag_part[:, :source_count]], axis=2),
            jnp.concatenate([imag_part[:, :source_count], real_part[:, :source_count]], axis=2),
        ],
        axis=1,
    )

    def single_tile(tile_index):
        grid_tile = (tile_index + 2) % refl_devices
        tile_rows = lax.dynamic_slice_in_dim(
            left_side, grid_tile // 4 * tile_sources, tile_sources, 2
        )
        tile_cols = lax.dynamic_slice_in_dim(
            right_side, grid_tile % 4 * group_width, group_width, 1
        )
        products = jnp.einsum(
            "fosk,frk->fosr", tile_rows, tile_cols, preferred_element_type=jnp.float32
        )
        products = products.reshape(freq_count, 2, tile_sources, freq_blocks, tile_receivers)
        products = jnp.transpose(products, (0, 2, 3, 1, 4))
        scaled = (
            amplitude * products.reshape(freq_count, tile_sources, freq_blocks, 2 * tile_receivers)
        ).astype(jnp.bfloat16)
        return lax.optimization_barrier(scaled).astype(jnp.float32)

    summed = lax.psum_scatter(
        jax.vmap(single_tile)(jnp.arange(1 * lax.axis_size("refl"), dtype=jnp.int32)).astype(
            jnp.bfloat16
        ),
        "refl",
        scatter_dimension=0,
        tiled=True,
    )
    multiples = to_time(lax.all_to_all(summed, "freq", split_axis=3, concat_axis=1, tiled=True))
    recorded_tile = recorded[0, 0]
    wide_multiples, wide_recorded = extend(multiples, recorded_tile)
    support_width = WC + 2 * WM
    wins_rows = tile_sources // WC
    wins_cols = tile_receivers // WC
    window_count = wins_rows * wins_cols
    window_ids = jnp.arange(window_count, dtype=jnp.int32)

    def support(window_index):
        anchor = (window_index // wins_cols * WC, window_index % wins_cols * WC, 0)
        return (
            lax.dynamic_slice(wide_multiples, anchor, (support_width, support_width, samples)),
            lax.dynamic_slice(wide_recorded, anchor, (support_width, support_width, samples)),
        )

    support_multiples, support_recorded = jax.vmap(support)(window_ids)
    flat_multiples = support_multiples.reshape(window_count, support_width * support_width, samples)
    flat_recorded = support_recorded.reshape(window_count, support_width * support_width, samples)
    stacked = jnp.stack([flat_multiples, flat_recorded], axis=1)
    statistics = jnp.einsum(
        "wajt,wju->watu", stacked, flat_multiples, preferred_element_type=jnp.float32
    )
    filters = solve_filters(
        statistics[:, 0], statistics[:, 1], initial_filters[0, 0].reshape(window_count, -1)
    )
    taps_matrix = conv_matrix(filters.astype(jnp.bfloat16))

    def cores(tile_array):
        grouped = tile_array.reshape(wins_rows, WC, wins_cols, WC, samples)
        return jnp.transpose(grouped, (0, 2, 1, 3, 4)).reshape(window_count, WC * WC, samples)

    predicted = jnp.einsum(
        "wju,wut->wjt", cores(multiples), taps_matrix, preferred_element_type=jnp.float32
    )
    cleaned = (cores(recorded_tile).astype(jnp.float32) - predicted).astype(jnp.bfloat16)
    cleaned = cleaned.reshape(wins_rows, wins_cols, WC, WC, samples)
    cleaned = jnp.transpose(cleaned, (0, 2, 1, 3, 4)).reshape(
        1, 1, tile_sources, tile_receivers, samples
    )
    return (cleaned, filters.reshape(1, 1, wins_rows, wins_cols, -1))


def solution(mesh):
    placed = (
        P(None, "freq", "groups", "refl"),
        P("refl", "freq", "groups", None, None),
        P("refl", "freq", "groups", None, None),
    )
    return jax.shard_map(
        body,
        mesh=mesh,
        in_specs=placed,
        out_specs=(
            P("refl", "freq", "groups", None, None),
            P("refl", "freq", "groups", None, None),
        ),
        check_vma=False,
    )
```

profile of v0, /device:TPU:0, one launch (start us, length us, event | category | flops | bytes accessed | tf_op | source)
XLA Modules:
  0.0 276.7 jit_solution(4154786635678017595)
XLA Ops:
  7.2 6.8 %slice_bitcast_fusion = (bf16[8,512,1024]{2,1,0:T(8,128)(2,1)S(1)}, bf16[8,512,1024]{2,1,0:T(8,128)(2,1)S(1)}) fusion(bf16[2,8,512,1024]{3,2,1,0:T(8,128)(2,1)} %param.3), kind=kLoop, calls=%fused_computation.13 | loop fusion | bytes 33554432 | tf_op jit(solution)/shard_map/squeeze | solution.py:156
  14.3 6.8 %pad_maximum_fusion = bf16[8,512,2048]{2,1,0:T(8,128)(2,1)} fusion(bf16[8,512,1024]{2,1,0:T(8,128)(2,1)S(1)} %get-tuple-element.46, bf16[8,512,1024]{2,1,0:T(8,128)(2,1)S(1)} %get-tuple-element.47), kind=kLoop, calls=%fused_computation.10 | loop fusion | flops 33554432 | bytes 33554432 | tf_op jit(solution)/shard_map/concatenate | solution.py:157
  23.9 41.9 %while.2 = (s32[]{:T(128)}, bf16[8,2,64,2048]{3,2,0,1:T(8,128)(2,1)}, s32[8,4]{0,1:T(4,128)S(1)}, bf16[8,8,2,32,2048]{4,3,2,1,0:T(8,128)(2,1)}, s32[]{:T(128)}) while((s32[]{:T(128)}, bf16[8,2,64,2048]{3,2,0,1:T(8,128)(2,1)}, s32[8,4]{0,1:T(4,128)S(1)}, bf16[8,8,2,32,2048]{4,3,2,1,0:T(8,128)(2,1)}, s32[]{:T(128)}) %tuple.44), condition=%wide.while_cond, body=%wide.while_body.sunk | while | flops 2 | bytes 4195433 | solution.py:168
  24.5 4.6 %fusion.66 = bf16[8,8,2,32,2048]{4,3,2,1,0:T(8,128)(2,1)} fusion(bf16[8,8,2,32,2048]{4,3,2,1,0:T(8,128)(2,1)} %get-tuple-element.124, s32[]{:T(128)} %get-tuple-element.121, bf16[8,2,64,2048]{3,2,0,1:T(8,128)(2,1)} %get-tuple-element.127, s32[]{:T(128)} %bitcast.112), kind=kLoop, calls=%fused_computation.3.clone.1 | loop fusion | bytes 4195328 | tf_op jit(solution)/shard_map/vmap()/gather
  29.8 4.7 %fusion.66 = bf16[8,8,2,32,2048]{4,3,2,1,0:T(8,128)(2,1)} fusion(bf16[8,8,2,32,2048]{4,3,2,1,0:T(8,128)(2,1)} %get-tuple-element.124, s32[]{:T(128)} %get-tuple-element.121, bf16[8,2,64,2048]{3,2,0,1:T(8,128)(2,1)} %get-tuple-element.127, s32[]{:T(128)} %bitcast.112), kind=kLoop, calls=%fused_computation.3.clone.1 | loop fusion | bytes 4195328 | tf_op jit(solution)/shard_map/vmap()/gather
  45.5 4.5 %fusion.66 = bf16[8,8,2,32,2048]{4,3,2,1,0:T(8,128)(2,1)} fusion(bf16[8,8,2,32,2048]{4,3,2,1,0:T(8,128)(2,1)} %get-tuple-element.124, s32[]{:T(128)} %get-tuple-element.121, bf16[8,2,64,2048]{3,2,0,1:T(8,128)(2,1)} %get-tuple-element.127, s32[]{:T(128)} %bitcast.112), kind=kLoop, calls=%fused_computation.3.clone.1 | loop fusion | bytes 4195328 | tf_op jit(solution)/shard_map/vmap()/gather
  55.9 4.7 %fusion.66 = bf16[8,8,2,32,2048]{4,3,2,1,0:T(8,128)(2,1)} fusion(bf16[8,8,2,32,2048]{4,3,2,1,0:T(8,128)(2,1)} %get-tuple-element.124, s32[]{:T(128)} %get-tuple-element.121, bf16[8,2,64,2048]{3,2,0,1:T(8,128)(2,1)} %get-tuple-element.127, s32[]{:T(128)} %bitcast.112), kind=kLoop, calls=%fused_computation.3.clone.1 | loop fusion | bytes 4195328 | tf_op jit(solution)/shard_map/vmap()/gather
  61.2 4.6 %fusion.66 = bf16[8,8,2,32,2048]{4,3,2,1,0:T(8,128)(2,1)} fusion(bf16[8,8,2,32,2048]{4,3,2,1,0:T(8,128)(2,1)} %get-tuple-element.124, s32[]{:T(128)} %get-tuple-element.121, bf16[8,2,64,2048]{3,2,0,1:T(8,128)(2,1)} %get-tuple-element.127, s32[]{:T(128)} %bitcast.112), kind=kLoop, calls=%fused_computation.3.clone.1 | loop fusion | bytes 4195328 | tf_op jit(solution)/shard_map/vmap()/gather
  65.8 54.9 %while.3 = (s32[]{:T(128)}, bf16[8,512,2048]{2,1,0:T(8,128)(2,1)}, s32[8,3]{0,1:T(4,128)S(1)}, bf16[8,8,128,2048]{3,2,1,0:T(8,128)(2,1)}, s32[]{:T(128)}) while((s32[]{:T(128)}, bf16[8,512,2048]{2,1,0:T(8,128)(2,1)}, s32[8,3]{0,1:T(4,128)S(1)}, bf16[8,8,128,2048]{3,2,1,0:T(8,128)(2,1)}, s32[]{:T(128)}) %tuple.47), condition=%wide.while_cond.1, body=%wide.while_body.1.sunk | while | flops 2 | bytes 8389729 | solution.py:171
  66.4 6.3 %bitcast_dynamic-update-slice_fusion.2 = bf16[8,8,128,2048]{3,2,1,0:T(8,128)(2,1)} fusion(bf16[8,8,128,2048]{3,2,1,0:T(8,128)(2,1)} %get-tuple-element.139, s32[]{:T(128)} %get-tuple-element.136, bf16[8,512,2048]{2,1,0:T(8,128)(2,1)} %get-tuple-element.142, s32[]{:T(128)} %bitcast.114), kind=kLoop, calls=%fused_computation.6.clone.1 | loop fusion | bytes 8389632 | tf_op jit(solution)/shard_map/vmap()/gather
  73.3 6.2 %bitcast_dynamic-update-slice_fusion.2 = bf16[8,8,128,2048]{3,2,1,0:T(8,128)(2,1)} fusion(bf16[8,8,128,2048]{3,2,1,0:T(8,128)(2,1)} %get-tuple-element.139, s32[]{:T(128)} %get-tuple-element.136, bf16[8,512,2048]{2,1,0:T(8,128)(2,1)} %get-tuple-element.142, s32[]{:T(128)} %bitcast.114), kind=kLoop, calls=%fused_computation.6.clone.1 | loop fusion | bytes 8389632 | tf_op jit(solution)/shard_map/vmap()/gather
  80.1 6.3 %bitcast_dynamic-update-slice_fusion.2 = bf16[8,8,128,2048]{3,2,1,0:T(8,128)(2,1)} fusion(bf16[8,8,128,2048]{3,2,1,0:T(8,128)(2,1)} %get-tuple-element.139, s32[]{:T(128)} %get-tuple-element.136, bf16[8,512,2048]{2,1,0:T(8,128)(2,1)} %get-tuple-element.142, s32[]{:T(128)} %bitcast.114), kind=kLoop, calls=%fused_computation.6.clone.1 | loop fusion | bytes 8389632 | tf_op jit(solution)/shard_map/vmap()/gather
  87.0 6.3 %bitcast_dynamic-update-slice_fusion.2 = bf16[8,8,128,2048]{3,2,1,0:T(8,128)(2,1)} fusion(bf16[8,8,128,2048]{3,2,1,0:T(8,128)(2,1)} %get-tuple-element.139, s32[]{:T(128)} %get-tuple-element.136, bf16[8,512,2048]{2,1,0:T(8,128)(2,1)} %get-tuple-element.142, s32[]{:T(128)} %bitcast.114), kind=kLoop, calls=%fused_computation.6.clone.1 | loop fusion | bytes 8389632 | tf_op jit(solution)/shard_map/vmap()/gather
  93.9 6.3 %bitcast_dynamic-update-slice_fusion.2 = bf16[8,8,128,2048]{3,2,1,0:T(8,128)(2,1)} fusion(bf16[8,8,128,2048]{3,2,1,0:T(8,128)(2,1)} %get-tuple-element.139, s32[]{:T(128)} %get-tuple-element.136, bf16[8,512,2048]{2,1,0:T(8,128)(2,1)} %get-tuple-element.142, s32[]{:T(128)} %bitcast.114), kind=kLoop, calls=%fused_computation.6.clone.1 | loop fusion | bytes 8389632 | tf_op jit(solution)/shard_map/vmap()/gather
  100.7 6.2 %bitcast_dynamic-update-slice_fusion.2 = bf16[8,8,128,2048]{3,2,1,0:T(8,128)(2,1)} fusion(bf16[8,8,128,2048]{3,2,1,0:T(8,128)(2,1)} %get-tuple-element.139, s32[]{:T(128)} %get-tuple-element.136, bf16[8,512,2048]{2,1,0:T(8,128)(2,1)} %get-tuple-element.142, s32[]{:T(128)} %bitcast.114), kind=kLoop, calls=%fused_computation.6.clone.1 | loop fusion | bytes 8389632 | tf_op jit(solution)/shard_map/vmap()/gather
  107.6 6.3 %bitcast_dynamic-update-slice_fusion.2 = bf16[8,8,128,2048]{3,2,1,0:T(8,128)(2,1)} fusion(bf16[8,8,128,2048]{3,2,1,0:T(8,128)(2,1)} %get-tuple-element.139, s32[]{:T(128)} %get-tuple-element.136, bf16[8,512,2048]{2,1,0:T(8,128)(2,1)} %get-tuple-element.142, s32[]{:T(128)} %bitcast.114), kind=kLoop, calls=%fused_computation.6.clone.1 | loop fusion | bytes 8389632 | tf_op jit(solution)/shard_map/vmap()/gather
  114.5 6.3 %bitcast_dynamic-update-slice_fusion.2 = bf16[8,8,128,2048]{3,2,1,0:T(8,128)(2,1)} fusion(bf16[8,8,128,2048]{3,2,1,0:T(8,128)(2,1)} %get-tuple-element.139, s32[]{:T(128)} %get-tuple-element.136, bf16[8,512,2048]{2,1,0:T(8,128)(2,1)} %get-tuple-element.142, s32[]{:T(128)} %bitcast.114), kind=kLoop, calls=%fused_computation.6.clone.1 | loop fusion | bytes 8389632 | tf_op jit(solution)/shard_map/vmap()/gather
  120.7 19.1 %multiply_convert_fusion = bf16[8,8,2,32,128]{4,3,2,1,0:T(8,128)(2,1)S(1)} fusion(bf16[8,8,2,32,2048]{4,3,2,1,0:T(8,128)(2,1)} %get-tuple-element.9, bf16[8,8,128,2048]{3,2,1,0:T(8,128)(2,1)} %get-tuple-element.17), kind=kOutput, calls=%fused_computation.27 | convolution fusion | flops 2148532224 | bytes 51380224 | tf_op jit(solution)/shard_map/vmap(fosk,frk->fosr)/dot_general | solution.py:174
  144.2 4.8 %convert_element_type.65 = bf16[8,8,32,2,128]{4,2,3,1,0:T(8,128)(2,1)} reshape(bf16[8,8,32,2,2,64]{5,4,2,3,1,0:T(2,128)(2,1)} %bitcast.121) | data formatting | bytes 2097152 | tf_op jit(solution)/shard_map/vmap()/convert_element_type | solution.py:181
  149.2 5.5 %collective-permute-start.5 = (bf16[32,4,256]{2,1,0:T(4,128)(2,1)S(1)}, bf16[32,4,256]{2,1,0:T(4,128)(2,1)S(1)}, u32[]{:S(2)}, u32[]{:S(2)}) collective-permute-start(bf16[32,4,256]{2,1,0:T(4,128)(2,1)S(1)} %get-tuple-element.57), channel_id=1, source_target_pairs={{1,0},{2,1},{3,2},{4,3},{5,4},{6,5},{7,6},{8,7},{9,8},{10,9},{11,1... | collective-permute-start | bytes 196616 | tf_op jit(solution)/shard_map/ppermute | solution.py:24
  156.6 4.6 %collective-permute-done.4 = bf16[32,4,256]{2,1,0:T(4,128)(2,1)S(1)} collective-permute-done((bf16[32,4,256]{2,1,0:T(4,128)(2,1)S(1)}, bf16[32,4,256]{2,1,0:T(4,128)(2,1)S(1)}, u32[]{:S(2)}, u32[]{:S(2)}) %collective-permute-start.4) | collective-permute-done | bytes 65568 | tf_op jit(solution)/shard_map/ppermute | solution.py:24
  166.7 7.5 %collective-permute-done.7 = bf16[4,72,256]{2,1,0:T(8,128)(2,1)S(1)} collective-permute-done((bf16[4,72,256]{2,1,0:T(8,128)(2,1)S(1)}, bf16[4,72,256]{2,1,0:T(8,128)(2,1)S(1)}, u32[]{:S(2)}, u32[]{:S(2)}) %collective-permute-start.7) | collective-permute-done | bytes 147488 | tf_op jit(solution)/shard_map/ppermute | solution.py:24
  174.2 46.3 %reduce-scatter.2.cloned.1.call-done = bf16[1,8,32,2,128]{4,2,3,1,0:T(8,128)(2,1)} async-done(((bf16[8,8,32,2,128]{4,2,3,1,0:T(8,128)(2,1)}), bf16[1,8,32,2,128]{4,2,3,1,0:T(8,128)(2,1)}) %reduce-scatter.2.cloned.1.call-update) | async-done | bytes 131088 | tf_op jit(solution)/shard_map/reduce_scatter | solution.py:184
  242.7 6.9 %collective-permute-done.3 = bf16[4,72,256]{2,1,0:T(8,128)(2,1)S(1)} collective-permute-done((bf16[4,72,256]{2,1,0:T(8,128)(2,1)S(1)}, bf16[4,72,256]{2,1,0:T(8,128)(2,1)S(1)}, u32[]{:S(2)}, u32[]{:S(2)}) %collective-permute-start.3) | collective-permute-done | bytes 147488 | tf_op jit(solution)/shard_map/ppermute | solution.py:24
  (139 shorter events, 80.4 us)
Async XLA Ops:
  7.2 213.4 %reduce-scatter.2.cloned.1.call-start = ((), (), s32[]{:S(2)}) async-start(), calls=%async_computation.2 | async-start | bytes 1179648 | tf_op jit(solution)/shard_map/reduce_scatter | solution.py:184
  144.2 4.9 %copy-start = (bf16[1,1,32,64,256]{4,3,2,1,0:T(8,128)(2,1)S(1)}, bf16[1,1,32,64,256]{4,3,2,1,0:T(8,128)(2,1)}, u32[]{:S(2)}) copy-start(bf16[1,1,32,64,256]{4,3,2,1,0:T(8,128)(2,1)} %param.4) | copy-start | bytes 3145732
  149.2 7.4 %collective-permute-start.5 = (bf16[32,4,256]{2,1,0:T(4,128)(2,1)S(1)}, bf16[32,4,256]{2,1,0:T(4,128)(2,1)S(1)}, u32[]{:S(2)}, u32[]{:S(2)}) collective-permute-start(bf16[32,4,256]{2,1,0:T(4,128)(2,1)S(1)} %get-tuple-element.57), channel_id=1, source_target_pairs={{1,0},{2,1},{3,2},{4,3},{5,4},{6,5},{7,6},{8,7},{9,8},{10,9},{11,1... | collective-permute-start | bytes 196616 | tf_op jit(solution)/shard_map/ppermute | solution.py:24
  154.7 6.5 %collective-permute-start.4 = (bf16[32,4,256]{2,1,0:T(4,128)(2,1)S(1)}, bf16[32,4,256]{2,1,0:T(4,128)(2,1)S(1)}, u32[]{:S(2)}, u32[]{:S(2)}) collective-permute-start(bf16[32,4,256]{2,1,0:T(4,128)(2,1)S(1)} %get-tuple-element.56), channel_id=1, source_target_pairs={{15,0},{0,1},{1,2},{2,3},{3,4},{4,5},{5,6},{6,7},{7,8},{8,9},{9,10... | collective-permute-start | bytes 196616 | tf_op jit(solution)/shard_map/ppermute | solution.py:24
  161.3 12.9 %collective-permute-start.7 = (bf16[4,72,256]{2,1,0:T(8,128)(2,1)S(1)}, bf16[4,72,256]{2,1,0:T(8,128)(2,1)S(1)}, u32[]{:S(2)}, u32[]{:S(2)}) collective-permute-start(bf16[4,72,256]{2,1,0:T(8,128)(2,1)S(1)} %get-tuple-element.51), channel_id=1, source_target_pairs={{8,0},{9,1},{10,2},{11,3},{12,4},{13,5},{14,6},{15,7},{0,8},{1,9},... | collective-permute-start | bytes 442376 | tf_op jit(solution)/shard_map/ppermute | solution.py:24
  163.8 62.4 %collective-permute-start.6 = (bf16[4,72,256]{2,1,0:T(8,128)(2,1)S(1)}, bf16[4,72,256]{2,1,0:T(8,128)(2,1)S(1)}, u32[]{:S(2)}, u32[]{:S(2)}) collective-permute-start(bf16[4,72,256]{2,1,0:T(8,128)(2,1)S(1)} %get-tuple-element.50), channel_id=1, source_target_pairs={{8,0},{9,1},{10,2},{11,3},{12,4},{13,5},{14,6},{15,7},{0,8},{1,9},... | collective-permute-start | bytes 442376 | tf_op jit(solution)/shard_map/ppermute | solution.py:24
  226.0 6.4 %collective-permute-start = (bf16[32,4,256]{2,1,0:T(4,128)(2,1)S(1)}, bf16[32,4,256]{2,1,0:T(4,128)(2,1)S(1)}, u32[]{:S(2)}, u32[]{:S(2)}) collective-permute-start(bf16[32,4,256]{2,1,0:T(4,128)(2,1)S(1)} %get-tuple-element.58), channel_id=1, source_target_pairs={{15,0},{0,1},{1,2},{2,3},{3,4},{4,5},{5,6},{6,7},{7,8},{8,9},{9,10... | collective-permute-start | bytes 196616 | tf_op jit(solution)/shard_map/ppermute | solution.py:24
  226.3 6.4 %collective-permute-start.1 = (bf16[32,4,256]{2,1,0:T(4,128)(2,1)S(1)}, bf16[32,4,256]{2,1,0:T(4,128)(2,1)S(1)}, u32[]{:S(2)}, u32[]{:S(2)}) collective-permute-start(bf16[32,4,256]{2,1,0:T(4,128)(2,1)S(1)} %get-tuple-element.59), channel_id=1, source_target_pairs={{1,0},{2,1},{3,2},{4,3},{5,4},{6,5},{7,6},{8,7},{9,8},{10,9},{11,1... | collective-permute-start | bytes 196616 | tf_op jit(solution)/shard_map/ppermute | solution.py:24
  232.8 9.8 %collective-permute-start.2 = (bf16[4,72,256]{2,1,0:T(8,128)(2,1)S(1)}, bf16[4,72,256]{2,1,0:T(8,128)(2,1)S(1)}, u32[]{:S(2)}, u32[]{:S(2)}) collective-permute-start(bf16[4,72,256]{2,1,0:T(8,128)(2,1)S(1)} %get-tuple-element.52), channel_id=1, source_target_pairs={{8,0},{9,1},{10,2},{11,3},{12,4},{13,5},{14,6},{15,7},{0,8},{1,9},... | collective-permute-start | bytes 442376 | tf_op jit(solution)/shard_map/ppermute | solution.py:24
  239.7 9.9 %collective-permute-start.3 = (bf16[4,72,256]{2,1,0:T(8,128)(2,1)S(1)}, bf16[4,72,256]{2,1,0:T(8,128)(2,1)S(1)}, u32[]{:S(2)}, u32[]{:S(2)}) collective-permute-start(bf16[4,72,256]{2,1,0:T(8,128)(2,1)S(1)} %get-tuple-element.53), channel_id=1, source_target_pairs={{8,0},{9,1},{10,2},{11,3},{12,4},{13,5},{14,6},{15,7},{0,8},{1,9},... | collective-permute-start | bytes 442376 | tf_op jit(solution)/shard_map/ppermute | solution.py:24
  251.3 1.4 copy-start.3
  258.6 6.1 %copy-start.4 = (f32[1,1,1,2,33]{4,3,2,1,0:T(2,128)S(1)}, f32[1,1,1,2,33]{4,3,2,1,0:T(2,128)}, u32[]{:S(2)}) copy-start(f32[1,1,1,2,33]{4,3,2,1,0:T(2,128)} %param.5) | copy-start | bytes 796
  259.8 8.5 %copy-start.1 = (f32[1,32,2,32,256]{4,3,1,2,0:T(8,128)S(1)}, f32[1,32,2,32,256]{4,3,1,2,0:T(8,128)}, u32[]{:S(2)}) copy-start(f32[1,32,2,32,256]{4,3,1,2,0:T(8,128)} %copy.29) | copy-start | bytes 6291460
  262.9 5.4 %copy-start.2 = (bf16[1,2,32,32,256]{4,3,2,1,0:T(8,128)(2,1)S(1)}, bf16[1,2,32,32,256]{4,3,2,1,0:T(8,128)(2,1)}, u32[]{:S(2)}) copy-start(bf16[1,2,32,32,256]{4,3,2,1,0:T(8,128)(2,1)} %copy.34) | copy-start | bytes 3145732
  265.5 3.2 %copy-start.5 = (f32[2,33]{1,0:T(2,128)}, f32[2,33]{1,0:T(2,128)S(1)}, u32[]{:S(2)}) copy-start(f32[2,33]{1,0:T(2,128)S(1)} %multiply_add_fusion) | copy-start | bytes 796
Sparse Core Ops, SparseCore 0:
  149.2 71.3 reduce-scatter.1
where the time goes:
time: 278 us; the launch traced here: 277 us
  local copies, waits for them, and re-layouts  134 us (48%)
  waiting for transfers between devices  69 us (25%)
  matrix products  25.8 us (9%)
  starting transfers between devices  16.2 us (6%)
  between operations  14.4 us (5%)
  other arithmetic  13.3 us (5%)
  blocking collectives  3.84 us (1%)
    gather x48, local copies, waits for them, and re-layouts  96.8 us
    reduce_scatter x1, waiting for transfers between devices, body(): lax.psum_scatter(jax.vmap(single_tile)(jnp.arange(1 * lax.axis_size('refl...  46.3 us
    ppermute x8, waiting for transfers between devices, passed_along(): return lax.ppermute(block, axis, route)  22.6 us
    dot_general x1, matrix products, single_tile(): jnp.einsum('fosk,frk->fosr', tile_rows, tile_cols, preferred_element_type...  19.1 us
    ppermute x8, starting transfers between devices, passed_along(): return lax.ppermute(block, axis, route)  16.2 us
    convert_element_type x3, local copies, waits for them, and re-layouts, single_tile(): scaled = (amplitude * products.reshape(freq_count, tile_sources, freq_blo...  9.19 us
    squeeze x1, local copies, waits for them, and re-layouts, body(): imag_part = spectra[1]  6.85 us
    concatenate x1, other arithmetic, body(): right_side = jnp.concatenate([real_part, imag_part], axis=2)  6.77 us
  transfers between devices with their start and end apart: 9, of which 7 were waited for; matrix products, arithmetic and copies ran while one was open for 4% of the time, Pallas kernels for 0%

commit v1 on v0

v1 whole, which is shorter than its diff:
```python
import functools
import math

import jax
import jax.numpy as jnp
import numpy as np
from jax import lax
from jax.experimental import pallas as pl
from jax.experimental.pallas import tpu as pltpu
from jax.sharding import PartitionSpec as P

NF = 16
K0 = 48
NT = 256
XR = 8192
WC = 32
WM = 4
TAPS = 33
ITERS = 3
HALF = (TAPS - 1) // 2
COLS = 4
LANES = 128
HF = 8
EXACT = lax.Precision.HIGHEST
F32 = jnp.float32
BF16 = jnp.bfloat16
VMEM = pltpu.CompilerParams(vmem_limit_bytes=32 * 1024 * 1024)


def tables():
    f = np.arange(NF)
    t = np.arange(NT)
    w = 2.0 * np.pi * (K0 + f) / NT
    angle = 2.0 * np.pi * (((K0 + f)[:, None] * t[None, :]) % NT) / NT
    weight = math.sqrt(2.0 / NF)
    table = np.stack([weight * np.cos(angle), -weight * np.sin(angle)], 1)
    table = table.astype(np.float32).astype(jnp.bfloat16).astype(np.float32)
    halves = table.reshape(2, HF, 2, NT).transpose(0, 2, 1, 3)
    time = halves.reshape(2, 2 * HF, NT)
    turned = np.stack([-halves[:, 1], halves[:, 0]], 1).reshape(2, 2 * HF, NT)
    lane = np.arange(LANES)
    held = lane < TAPS
    tap = lane - HALF
    cos_k = np.where(held, np.cos(w[:, None] * tap), 0.0).reshape(2, HF, LANES)
    sin_k = np.where(held, np.sin(w[:, None] * tap), 0.0).reshape(2, HF, LANES)
    lag = np.where(held, 16.0 * np.cos(w[:, None] * lane), 0.0).reshape(2, HF, LANES)
    zero = np.zeros_like(lag)
    to_lag = np.concatenate([lag, zero, zero, zero], 1)
    to_target = np.concatenate([zero, cos_k, sin_k, zero], 1)
    lags = np.concatenate([to_lag, to_target], 2)
    cos_rows = np.concatenate([cos_k, cos_k], 1)
    sin_rows = np.concatenate([sin_k, sin_k], 1)
    as32 = lambda x: np.asarray(x, np.float32)
    return time, as32(turned), as32(lags), as32(cos_rows), as32(sin_rows)


def lanes_of(rows):
    return lax.broadcasted_iota(jnp.int32, (rows, LANES), 1)


def band_rows(p, rows):
    if rows == 2:
        return [WC if p == 0 else WC - WM]
    return [p * WC - WM if p > 0 else None, (p + 1) * WC if p < rows - 1 else None]


def terms_kernel(rows, s_ref, *rest):
    refl = rows * COLS
    outs, (blocks, bands, sides) = rest[:refl], rest[refl:]
    f = pl.program_id(0)
    sources = rows * WC
    width = s_ref.shape[-1]
    amplitude = 1.0 / math.sqrt(2.0 * XR)
    left = s_ref[:, 0, :sources, :].reshape(2 * sources, width)
    parts = [[], []]
    for c in range(COLS):
        right = s_ref[:, 0, c * LANES : (c + 1) * LANES, :].reshape(2 * LANES, width)
        got = lax.dot_general(left, right, (((1,), (1,)), ((), ())), preferred_element_type=F32)
        parts[0].append(amplitude * (got[:sources, :LANES] - got[sources:, LANES:]))
        parts[1].append(amplitude * (got[:sources, LANES:] + got[sources:, :LANES]))
    low = lanes_of(WC // 2) < LANES // 2
    nb = len(band_rows(0, rows))
    for c in range(COLS):
        for p in range(rows):
            g = p * COLS + c
            for part in range(2):
                x = parts[part][c][p * WC : (p + 1) * WC]
                a, b = x[: WC // 2], x[WC // 2 :]
                first = jnp.where(low, a, pltpu.roll(b, LANES // 2, 1))
                second = jnp.where(low, pltpu.roll(a, LANES // 2, 1), b)
                at = pl.multiple_of(part * HF * WC + f * WC, WC)
                blocks[g, pl.ds(at, WC), :] = jnp.concatenate([first, second], 0).astype(BF16)
            for n, start in enumerate(band_rows(p, rows)):
                if start is None:
                    band = jnp.zeros((2 * WM, LANES), F32)
                else:
                    band = jnp.concatenate([x[c][start : start + WM] for x in parts], 0)
                bands[g, pl.ds(pl.multiple_of(n * HF * 8 + f * 8, 8), 8), :] = band
    lane = lanes_of(sources)
    zero = jnp.zeros((sources, LANES), F32)
    for c in range(COLS):
        for part in range(2):
            x = parts[part]
            before = x[c - 1] if c > 0 else zero
            after = x[c + 1] if c < COLS - 1 else zero
            base = f * 16 + part * 8
            moved = pltpu.roll(jnp.where(lane >= LANES // 2, before, after), base + WM, 1)
            here = (lane >= base) & (lane < base + 8)
            sides[c] = jnp.where(here, moved, sides[c])

    @pl.when(f == HF - 1)
    def _():
        me = lax.axis_index("refl")
        main = 2 * HF * WC
        for p in range(rows):
            for c in range(COLS):
                g = p * COLS + c
                blocks[g, main : main + nb * 64, :] = bands[g].astype(BF16)
                side = [sides[c, p * WC : (p + 1) * WC, :]]
                for start in band_rows(p, rows):
                    side.append(
                        jnp.zeros((WM, LANES), F32)
                        if start is None
                        else sides[c, start : start + WM, :]
                    )
                side.append(jnp.zeros((16 - nb * WM, LANES), F32))
                blocks[g, main + nb * 64 :, :] = jnp.concatenate(side, 0).astype(BF16)
        for k in range(refl):
            outs[k][...] = blocks[((me ^ k) + 2) % refl]


def block_terms(spectra, rows):
    refl = rows * COLS
    freqs, receivers, width = spectra.shape[1:]
    nb = len(band_rows(0, rows))
    size = 2 * HF * WC + nb * 64 + 48
    out = jax.ShapeDtypeStruct((size, LANES), BF16)
    spec = pl.BlockSpec((size, LANES), lambda f: (0, 0))
    return pl.pallas_call(
        functools.partial(terms_kernel, rows),
        grid=(freqs,),
        in_specs=[pl.BlockSpec((2, 1, receivers, width), lambda f: (0, f, 0, 0))],
        out_specs=[spec] * refl,
        out_shape=[out] * refl,
        scratch_shapes=[
            pltpu.VMEM((refl, size, LANES), BF16),
            pltpu.VMEM((refl, nb * 64, LANES), F32),
            pltpu.VMEM((COLS, rows * WC, LANES), F32),
        ],
        compiler_params=VMEM,
        name="block_terms",
    )(spectra)


def project_kernel(r_ref, t_ref, keep_ref, send_ref):
    j = lax.axis_index("freq")
    table = jnp.concatenate([t_ref[j], t_ref[1 - j]], 0)
    half = WC // 2
    for s in range(half):
        pair = jnp.concatenate([r_ref[s], r_ref[half + s]], 0)
        got = lax.dot_general(table, pair, (((1,), (1,)), ((), ())), preferred_element_type=F32)
        keep_ref[s] = got[: 2 * HF]
        send_ref[s] = got[2 * HF :]


def project(recorded, table):
    shape = jax.ShapeDtypeStruct((WC // 2, 2 * HF, LANES), F32)
    return pl.pallas_call(
        project_kernel, out_shape=[shape, shape], compiler_params=VMEM, name="project"
    )(recorded, table)


def grid_place(rows):
    g = (lax.axis_index("refl") + 2) % (rows * COLS)
    return g // COLS, g % COLS


def band_kernel(rows, keep_ref, other_ref, *outs):
    j = lax.axis_index("freq")
    p, _ = grid_place(rows)
    half = WC // 2
    low = lanes_of(HF) < LANES // 2

    def build(out_ref, first, upper):
        for s in range(WM):
            for part in range(2):
                rows_of = pl.ds(part * HF, HF)
                kept = keep_ref[first + s, rows_of, :]
                other = other_ref[first + s, rows_of, :]
                a = jnp.where(j == 0, kept, other)
                b = jnp.where(j == 0, other, kept)
                plain = jnp.where(low, a, pltpu.roll(b, LANES // 2, 1))
                shifted = jnp.where(low, pltpu.roll(a, LANES // 2, 1), b)
                band = jnp.where(upper, shifted, plain)
                out_ref[pl.ds(part * WM + s, HF, stride=8), :] = band

    if rows == 2:
        build(outs[0], jnp.where(p == 0, half - WM, 0), p == 0)
    else:
        build(outs[0], half - WM, True)
        build(outs[1], 0, False)


def band_projections(keep, other, rows):
    shape = jax.ShapeDtypeStruct((64, LANES), F32)
    return pl.pallas_call(
        functools.partial(band_kernel, rows),
        out_shape=[shape] * len(band_rows(0, rows)),
        name="band_projections",
    )(keep, other)


def side_kernel(keep_ref, other_ref, *rest):
    bands, out_ref = rest[:-1], rest[-1]
    j = lax.axis_index("freq")
    half = WC // 2
    keep = keep_ref[...].reshape(half * 2 * HF, LANES)
    other = other_ref[...].reshape(half * 2 * HF, LANES)
    left = jnp.where(j == 0, keep, other)
    right = jnp.where(j == 0, other, keep)
    row = lax.broadcasted_iota(jnp.int32, (LANES, LANES), 0)
    lane = lax.broadcasted_iota(jnp.int32, (LANES, LANES), 1)
    r = lane % 8
    dot = functools.partial(jnp.dot, precision=EXACT, preferred_element_type=F32)

    def picked(at_left, at_right):
        take_right = ((row == at_right + r) & (r < WM)).astype(F32)
        take_left = ((row == at_left + r - WM) & (r >= WM)).astype(F32)
        return take_left, take_right

    at = lax.broadcasted_iota(jnp.int32, (half, 2 * HF, LANES), 1)
    l3 = lax.broadcasted_iota(jnp.int32, (half, 2 * HF, LANES), 2)
    mine = (l3 // 16 == at % HF) & ((l3 // 8) % 2 == at // HF)
    for sh in range(2):
        take_left, take_right = picked(sh * 64, sh * 64 + 60)
        x = (dot(left, take_left) + dot(right, take_right)).reshape(half, 2 * HF, LANES)
        out_ref[sh * half : (sh + 1) * half, :] = jnp.sum(jnp.where(mine, x, 0.0), 1)
    take_left, take_right = picked(0, LANES - WM)
    b_row = lax.broadcasted_iota(jnp.int32, (HF, 8, LANES), 1)
    b_f = lax.broadcasted_iota(jnp.int32, (HF, 8, LANES), 0)
    b_l = lax.broadcasted_iota(jnp.int32, (HF, 8, LANES), 2)
    mine = (b_l // 16 == b_f) & ((b_l // 8) % 2 == b_row // WM)
    out_ref[WC:, :] = jnp.zeros((16, LANES), F32)
    for n, band in enumerate(bands):
        x = dot(band[...], take_left + take_right).reshape(HF, 8, LANES)
        x = jnp.sum(jnp.where(mine, x, 0.0), 0)
        out_ref[WC + n * WM : WC + (n + 1) * WM, :] = x[:WM] + x[WM:]


def side_projections(keep, other, bands):
    return pl.pallas_call(
        side_kernel,
        out_shape=jax.ShapeDtypeStruct((48, LANES), F32),
        name="side_projections",
    )(keep, other, *bands)


def statistics_kernel(rows, *refs):
    refl = rows * COLS
    nb = len(band_rows(0, rows))
    blocks, refs = refs[:refl], refs[refl:]
    keep_ref, other_ref, near_ref, far_ref, lags_ref = refs[:5]
    bands, refs = refs[5 : 5 + nb], refs[5 + nb :]
    own_ref, send_ref, lag_ref, spectrum = refs
    j = lax.axis_index("freq")
    _, c = grid_place(rows)
    half = WC // 2

    def summed(start, size):
        total = blocks[0][start : start + size, :].astype(F32)
        for block in blocks[1:]:
            total = total + block[start : start + size, :].astype(F32)
        return total.astype(BF16).astype(F32)

    for fp in range(2 * HF):
        x = summed(fp * WC, WC)
        for tile in range(2):
            spectrum[pl.ds(tile * half * 16 + fp, half, stride=16), :] = x[
                tile * half : (tile + 1) * half
            ]
    count = half * 16
    here = pl.multiple_of(j * count, count)
    there = pl.multiple_of((1 - j) * count, count)
    own_ref[...] = spectrum[pl.ds(here, count), :].astype(BF16)
    send_ref[...] = spectrum[pl.ds(there, count), :].astype(BF16)
    sums = []
    for at, q_ref in ((here, keep_ref), (there, other_ref)):
        power = in_phase = turned = jnp.zeros((HF, LANES), F32)
        for s in range(half):
            a = spectrum[pl.ds(at + s * 16, HF), :]
            b = spectrum[pl.ds(at + s * 16 + HF, HF), :]
            qc, qs = q_ref[s, :HF, :], q_ref[s, HF:, :]
            power = power + (a * a + b * b)
            in_phase = in_phase + (a * qc + b * qs)
            turned = turned + (b * qc - a * qs)
        sums.append([power, in_phase, turned])
    total = None
    sub = lax.broadcasted_iota(jnp.int32, (HF, 8, LANES), 1)
    for n in range(nb):
        x = summed(2 * HF * WC + n * 64, 64).reshape(HF, 8, LANES)
        q = bands[n][...].reshape(HF, 8, LANES)
        partner = jnp.where(sub < WM, -1.0, 1.0) * pltpu.roll(q, WM, 1)
        here_sums = [jnp.sum(x * y, 1) for y in (x, q, partner)]
        total = here_sums if total is None else [a + b for a, b in zip(total, here_sums)]
    sums.append(total)

    window = lax.broadcasted_iota(jnp.int32, (8, LANES), 0)
    lane = lanes_of(8)
    window = jnp.where(window < 4, (window + 2 * j) % 4, 8)
    starts = window * WC - WM

    def mask(receiver):
        return ((receiver >= starts) & (receiver < starts + WC + 2 * WM)).astype(F32)

    dot = functools.partial(lax.dot_general, precision=EXACT, preferred_element_type=F32)
    stats = jnp.zeros((8, 32), F32)
    receivers = (j * 64 + lane % 64, (1 - j) * 64 + lane % 64, lane)
    for x, receiver in zip(sums, receivers):
        x = jnp.concatenate(x + [jnp.zeros((HF, LANES), F32)], 0)
        stats = stats + dot(mask(receiver), x, (((1,), (1,)), ((), ())))
    x = summed(2 * HF * WC + nb * 64, 48)
    l48 = lanes_of(48)
    from_near = ((l48 % 8) < WM) == ((c % 2) == 1)
    q = jnp.where(from_near, near_ref[...], far_ref[...])
    first_part = (l48 // 8) % 2 == 0
    partner = jnp.where(first_part, -pltpu.roll(q, LANES - 8, 1), pltpu.roll(q, 8, 1))
    row = lax.broadcasted_iota(jnp.int32, (LANES, 32), 0)
    column = lax.broadcasted_iota(jnp.int32, (LANES, 32), 1)
    at_side = ((window == 0) & (lane % 8 < WM)) | ((window == 3) & (lane % 8 >= WM))
    for n, y in enumerate((x, q, partner)):
        z = jnp.sum(x * y, 0, keepdims=True)
        z = jnp.where(at_side, jnp.broadcast_to(z, (8, LANES)), 0.0)
        to = (column == n * HF + row // 16).astype(F32)
        stats = stats + dot(z, to, (((1,), (0,)), ((), ())))
    lag_ref[...] = dot(stats, lags_ref[j], (((1,), (0,)), ((), ())))


def statistics(blocks, keep, other, near, far, lags, bands, rows):
    count = WC // 2 * 2 * HF
    return pl.pallas_call(
        functools.partial(statistics_kernel, rows),
        out_shape=[
            jax.ShapeDtypeStruct((count, LANES), BF16),
            jax.ShapeDtypeStruct((count, LANES), BF16),
            jax.ShapeDtypeStruct((8, 2 * LANES), F32),
        ],
        scratch_shapes=[pltpu.VMEM((2 * count, LANES), F32)],
        compiler_params=VMEM,
        name="statistics",
    )(*blocks, keep, other, near, far, lags, *bands)


def subtract_kernel(
    steps,
    lag_ref,
    lag_got_ref,
    start_ref,
    time_ref,
    turned_ref,
    cos_ref,
    sin_ref,
    own_ref,
    got_ref,
    r_low_ref,
    r_high_ref,
    clean_ref,
    filters_ref,
    wavelets,
):
    step = pl.program_id(0)
    j = lax.axis_index("freq")
    half = WC // 2

    @pl.when(step == 0)
    def _():
        total = lag_ref[0:2, :] + lag_got_ref[2:4, :]
        lag, target = total[:, :LANES], total[:, LANES:]
        lane = lanes_of(2)
        held = lane < TAPS
        magnitude = jnp.where(held, jnp.abs(lag), 0.0)
        zero_lag = jnp.sum(jnp.where(lane == 0, lag, 0.0), 1, keepdims=True)
        others = jnp.sum(jnp.where(lane >= 1, magnitude, 0.0), 1, keepdims=True)
        step_size = 0.5 / (zero_lag + 2.0 * others + 1e-06)
        filters = jnp.concatenate(
            [start_ref[...], jnp.zeros((2, LANES - TAPS), F32)], 1
        )
        spread = [jnp.broadcast_to(lag[:, d : d + 1], (2, LANES)) for d in range(TAPS)]
        for repeat in range(ITERS):
            applied = spread[0] * filters
            for d in range(1, TAPS):
                applied = applied + spread[d] * (
                    pltpu.roll(filters, d, 1) + pltpu.roll(filters, LANES - d, 1)
                )
            filters = jnp.where(held, filters + step_size * (target - applied), 0.0)
        filters_ref[...] = filters[:, :TAPS]
        taps = filters.astype(BF16).astype(F32)
        for w in range(2):
            for n, h in enumerate((j, 1 - j)):
                tap = taps[w : w + 1, :]
                hc = jnp.sum(cos_ref[h] * tap, 1, keepdims=True)
                hs = jnp.sum(sin_ref[h] * tap, 1, keepdims=True)
                at = w * 32 + n * 16
                wavelets[at : at + 16, :] = (hc * time_ref[h] + hs * turned_ref[h]).astype(BF16)

    table = wavelets[...]
    lane = lax.broadcasted_iota(jnp.int32, (32, LANES), 1)
    first = (lane % 64) < WC
    zero = jnp.zeros((32, LANES), BF16)
    for s in range(half // steps):
        x = jnp.concatenate([own_ref[s * 16 : s * 16 + 16, :], got_ref[s * 16 : s * 16 + 16, :]], 0)
        both = jnp.concatenate([jnp.where(first, x, zero), jnp.where(first, zero, x)], 0)
        predicted = lax.dot_general(
            both, table, (((0,), (0,)), ((), ())), preferred_element_type=F32
        )
        clean_ref[0, s] = (r_low_ref[0, s].astype(F32) - predicted[:64]).astype(BF16)
        clean_ref[1, s] = (r_high_ref[0, s].astype(F32) - predicted[64:]).astype(BF16)


def subtract(lag, lag_got, start, time, turned, cos_rows, sin_rows, own, got, recorded):
    steps = 4
    half = WC // 2
    each = half // steps
    recorded = recorded.reshape(2, half, 64, NT)
    whole = lambda x: pl.BlockSpec(x.shape, lambda i: (0,) * x.ndim)
    small = (lag, lag_got, start, time, turned, cos_rows, sin_rows)
    rows_spec = pl.BlockSpec((each * 16, LANES), lambda i: (i, 0))
    return pl.pallas_call(
        functools.partial(subtract_kernel, steps),
        grid=(steps,),
        in_specs=[whole(x) for x in small]
        + [
            rows_spec,
            rows_spec,
            pl.BlockSpec((1, each, 64, NT), lambda i: (0, i, 0, 0)),
            pl.BlockSpec((1, each, 64, NT), lambda i: (1, i, 0, 0)),
        ],
        out_specs=[
            pl.BlockSpec((2, each, 64, NT), lambda i: (0, i, 0, 0)),
            pl.BlockSpec((2, TAPS), lambda i: (0, 0)),
        ],
        out_shape=[
            jax.ShapeDtypeStruct((2, half, 64, NT), BF16),
            jax.ShapeDtypeStruct((2, TAPS), F32),
        ],
        scratch_shapes=[pltpu.VMEM((64, NT), BF16)],
        compiler_params=VMEM,
        name="subtract",
    )(*small, own, got, recorded, recorded)


def body(spectra, recorded, initial_filters):
    refl = lax.axis_size("refl")
    rows = refl // COLS
    time, turned, lags, cos_rows, sin_rows = (jnp.asarray(x) for x in tables())
    core_swap = [(0, 1), (1, 0)]

    def place(p, c):
        return (p * COLS + c - 2) % refl

    blocks = block_terms(spectra, rows)
    got = [blocks[0]]
    for k in range(1, refl):
        got.append(lax.ppermute(blocks[k], "refl", [(i, i ^ k) for i in range(refl)]))

    tile = recorded[0, 0]
    keep, send = project(tile, time.astype(BF16))
    other = lax.ppermute(send, "freq", core_swap)
    bands = band_projections(keep, other, rows)
    if rows == 2:
        routes = [[(place(p, c), place(1 - p, c)) for p in range(2) for c in range(COLS)]]
    else:
        routes = [
            [(place(p, c), place(p + 1, c)) for p in range(rows - 1) for c in range(COLS)],
            [(place(p + 1, c), place(p, c)) for p in range(rows - 1) for c in range(COLS)],
        ]
    bands = [lax.ppermute(x, "refl", route) for x, route in zip(bands, routes)]
    sides = side_projections(keep, other, bands)
    near = lax.ppermute(
        sides, "refl", [(place(p, c), place(p, c ^ 1)) for p in range(rows) for c in range(COLS)]
    )
    far = lax.ppermute(
        sides, "refl", [(place(p, c), place(p, 3 - c)) for p in range(rows) for c in (1, 2)]
    )
    own, away, lag = statistics(got, keep, other, near, far, lags, bands, rows)
    came = lax.ppermute(away, "freq", core_swap)
    lag_got = lax.ppermute(lag, "freq", core_swap)
    clean, filters = subtract(
        lag,
        lag_got,
        initial_filters.reshape(2, TAPS),
        time,
        turned,
        cos_rows,
        sin_rows,
        own,
        came,
        tile,
    )
    return (clean.reshape(recorded.shape), filters.reshape(initial_filters.shape))


def solution(mesh):
    placed = (
        P(None, "freq", "groups", "refl"),
        P("refl", "freq", "groups", None, None),
        P("refl", "freq", "groups", None, None),
    )
    return jax.shard_map(
        body,
        mesh=mesh,
        in_specs=placed,
        out_specs=(
            P("refl", "freq", "groups", None, None),
            P("refl", "freq", "groups", None, None),
        ),
        check_vma=False,
    )
```

time: 278 us -> 65.8 us (0.24)
  local copies, waits for them, and re-layouts: 134 us -> 10.7 us
  waiting for transfers between devices: 69 us -> 15.6 us
  matrix products: 25.8 us -> 0 us
  Pallas kernels: 0 us -> 16.8 us
  between operations: 14.4 us -> 0.73 us
  other arithmetic: 13.3 us -> 0 us
  starting transfers between devices: 16.2 us -> 21.5 us
  blocking collectives: 3.84 us -> 0 us
    gather x52 -> x0, local copies, waits for them, and re-layouts: 103 us -> none
    reduce_scatter x1 -> x0, waiting for transfers between devices: 46.3 us -> none  [body(): lax.psum_scatter(jax.vmap(single_tile)(jnp.arange(1 * lax.axis_size('refl...]
    dot_general x9 -> x0, matrix products: 25.8 us -> none  [the longest x1 19.1 us: single_tile(): jnp.einsum('fosk,frk->fosr', tile_rows, tile_cols, preferred_element_type...]
    pallas_call x0 -> x6, Pallas kernels: none -> 16.8 us  [the longest x1 8.9 us: block_terms(): pl.pallas_call(functools.partial(terms_kernel, rows), grid=(freqs,), in_s...]
    convert_element_type x4 -> x0, local copies, waits for them, and re-layouts: 10.8 us -> none  [the longest x3 9.19 us: single_tile(): scaled = (amplitude * products.reshape(freq_count, tile_sources, freq_blo...]
    concatenate x7 -> x0, other arithmetic: 8.42 us -> none  [the longest x1 6.77 us: body(): right_side = jnp.concatenate([real_part, imag_part], axis=2)]
    unnamed x14 -> x32, local copies, waits for them, and re-layouts: 2.73 us -> 10.7 us
    ppermute x8 -> x13, waiting for transfers between devices: 22.6 us -> 15.6 us  [the longest x7 10.4 us: body(): lax.ppermute(blocks[k], 'refl', [(i, i ^ k) for i in range(refl)])]
  transfers between devices with their start and end apart: 9 -> 13, of which waited for: 7 -> 4; matrix products, arithmetic and copies ran while one was open for 4% -> 0% of each run, Pallas kernels for 0% -> 19%
where the time goes in v1:
time: 65.8 us; the launch traced here: 65.4 us
  starting transfers between devices  21.5 us (33%)
  Pallas kernels  16.8 us (26%)
  waiting for transfers between devices  15.6 us (24%)
  local copies, waits for them, and re-layouts  10.7 us (16%)
  between operations  0.73 us (1%)
    ppermute x7, starting transfers between devices, body(): lax.ppermute(blocks[k], 'refl', [(i, i ^ k) for i in range(refl)])  12.2 us
    unnamed x32, local copies, waits for them, and re-layouts  10.7 us
    ppermute x7, waiting for transfers between devices, body(): lax.ppermute(blocks[k], 'refl', [(i, i ^ k) for i in range(refl)])  10.4 us
    pallas_call x1, Pallas kernels, block_terms(): pl.pallas_call(functools.partial(terms_kernel, rows), grid=(freqs,), in_s...  8.9 us
    ppermute x1, waiting for transfers between devices, body(): lax.ppermute(sides, 'refl', [(place(p, c), place(p, 3 - c)) for p in rang...  4.34 us
    ppermute x1, starting transfers between devices, body(): lax.ppermute(sides, 'refl', [(place(p, c), place(p, 3 - c)) for p in rang...  4.2 us
    pallas_call x1, Pallas kernels, subtract(): pl.pallas_call(functools.partial(subtract_kernel, steps), grid=(steps,),...  2.88 us
    ppermute x1, starting transfers between devices, body(): bands = [lax.ppermute(x, 'refl', route) for x, route in zip(bands, routes)]  2.59 us
  transfers between devices with their start and end apart: 13, of which 4 were waited for; matrix products, arithmetic and copies ran while one was open for 0% of the time, Pallas kernels for 19%

profile of v1, /device:TPU:0, one launch (start us, length us, event | category | flops | bytes accessed | tf_op | source)
XLA Modules:
  0.0 65.4 jit_solution(7692731063673716343)
XLA Ops:
  0.6 1.2 %copy-done.1 = bf16[1,1,32,64,256]{4,3,2,1,0:T(8,128)(2,1)S(1)} copy-done((bf16[1,1,32,64,256]{4,3,2,1,0:T(8,128)(2,1)S(1)}, bf16[1,1,32,64,256]{4,3,2,1,0:T(8,128)(2,1)}, u32[]{:S(2)}) %copy-start.1) | copy-done | bytes 1048600
  1.9 0.7 %copy-done.14 = bf16[2,16,256]{2,1,0:T(8,128)(2,1)S(1)} copy-done((bf16[2,16,256]{2,1,0:T(8,128)(2,1)S(1)}, bf16[2,16,256]{2,1,0:T(8,128)(2,1)}, u32[]{:S(2)}) %copy-start.14) | copy-done | bytes 16408
  3.0 0.7 %copy-done.3 = f32[16,16,128]{2,1,0:T(8,128)} copy-done((f32[16,16,128]{2,1,0:T(8,128)}, f32[16,16,128]{2,1,0:T(8,128)S(1)}, u32[]{:S(2)}) %copy-start.3) | copy-done | bytes 131096
  4.2 5.8 %copy-done = bf16[2,8,512,1024]{3,2,1,0:T(8,128)(2,1)S(1)} copy-done((bf16[2,8,512,1024]{3,2,1,0:T(8,128)(2,1)S(1)}, bf16[2,8,512,1024]{3,2,1,0:T(8,128)(2,1)}, u32[]{:S(2)}) %copy-start) | copy-done | bytes 16777240
  10.0 8.9 %block_terms.1 = (bf16[624,128]{1,0:T(8,128)(2,1)S(1)}, bf16[624,128]{1,0:T(8,128)(2,1)S(1)}, bf16[624,128]{1,0:T(8,128)(2,1)S(1)}, bf16[624,128]{1,0:T(8,128)(2...) custom-call(bf16[2,8,512,1024]{3,2,1,0:T(8,128)(2,1)S(1)} %copy-done), custom_call_target="tpu_custom_call" | custom-call | tf_op jit(solution)/shard_map/block_terms/pallas_call | solution.py:139
  18.9 2.6 %collective-permute-start = (bf16[624,128]{1,0:T(8,128)(2,1)S(1)}, bf16[624,128]{1,0:T(8,128)(2,1)S(1)}, u32[]{:S(2)}, u32[]{:S(2)}) collective-permute-start(bf16[624,128]{1,0:T(8,128)(2,1)S(1)} %get-tuple-element.18), channel_id=1, source_target_pairs={{0,2},{2,0},{4,6},{6,4},{8,10},{10,8},{12,14},{14,12},{1,3},{3,1},... | collective-permute-start | bytes 479240 | tf_op jit(solution)/shard_map/ppermute | solution.py:463
  21.4 1.6 %collective-permute-start.1 = (bf16[624,128]{1,0:T(8,128)(2,1)S(1)}, bf16[624,128]{1,0:T(8,128)(2,1)S(1)}, u32[]{:S(2)}, u32[]{:S(2)}) collective-permute-start(bf16[624,128]{1,0:T(8,128)(2,1)S(1)} %get-tuple-element.19), channel_id=1, source_target_pairs={{0,4},{2,6},{4,0},{6,2},{8,12},{10,14},{12,8},{14,10},{1,5},{3,7},... | collective-permute-start | bytes 479240 | tf_op jit(solution)/shard_map/ppermute | solution.py:463
  23.0 0.7 copy-done.5
  23.7 1.7 %band_projections.1 = f32[64,128]{1,0:T(8,128)} custom-call(f32[16,16,128]{2,1,0:T(8,128)} %copy-done.3, f32[16,16,128]{2,1,0:T(8,128)} %copy-done.5), custom_call_target="tpu_custom_call" | custom-call | tf_op jit(solution)/shard_map/band_projections/pallas_call | solution.py:206
  25.3 2.6 %collective-permute-start.8 = (f32[64,128]{1,0:T(8,128)}, f32[64,128]{1,0:T(8,128)S(1)}, u32[]{:S(2)}, u32[]{:S(2)}) collective-permute-start(f32[64,128]{1,0:T(8,128)} %band_projections.1), channel_id=1, source_target_pairs={{12,4},{14,6},{0,8},{2,10},{4,12},{6,14},{8,0},{10,2},{13,5},{15,7... | collective-permute-start | bytes 98312 | tf_op jit(solution)/shard_map/ppermute | solution.py:476
  28.3 3.9 %collective-permute-start.4 = (bf16[624,128]{1,0:T(8,128)(2,1)S(1)}, bf16[624,128]{1,0:T(8,128)(2,1)S(1)}, u32[]{:S(2)}, u32[]{:S(2)}) collective-permute-start(bf16[624,128]{1,0:T(8,128)(2,1)S(1)} %get-tuple-element.22), channel_id=1, source_target_pairs={{0,10},{2,8},{4,14},{6,12},{8,2},{10,0},{12,6},{14,4},{1,11},{3,9}... | collective-permute-start | bytes 479240 | tf_op jit(solution)/shard_map/ppermute | solution.py:463
  32.2 1.3 %collective-permute-start.5 = (bf16[624,128]{1,0:T(8,128)(2,1)S(1)}, bf16[624,128]{1,0:T(8,128)(2,1)S(1)}, u32[]{:S(2)}, u32[]{:S(2)}) collective-permute-start(bf16[624,128]{1,0:T(8,128)(2,1)S(1)} %get-tuple-element.23), channel_id=1, source_target_pairs={{0,12},{2,14},{4,8},{6,10},{8,4},{10,6},{12,0},{14,2},{1,13},{3,15... | collective-permute-start | bytes 479240 | tf_op jit(solution)/shard_map/ppermute | solution.py:463
  33.6 2.4 %collective-permute-start.6 = (bf16[624,128]{1,0:T(8,128)(2,1)S(1)}, bf16[624,128]{1,0:T(8,128)(2,1)S(1)}, u32[]{:S(2)}, u32[]{:S(2)}) collective-permute-start(bf16[624,128]{1,0:T(8,128)(2,1)S(1)} %get-tuple-element.24), channel_id=1, source_target_pairs={{0,14},{2,12},{4,10},{6,8},{8,6},{10,4},{12,2},{14,0},{1,15},{3,13... | collective-permute-start | bytes 479240 | tf_op jit(solution)/shard_map/ppermute | solution.py:463
  36.0 2.2 %side_projections.1 = f32[48,128]{1,0:T(8,128)} custom-call(f32[16,16,128]{2,1,0:T(8,128)} %copy-done.3, f32[16,16,128]{2,1,0:T(8,128)} %copy-done.5, f32[64,128]{1,0:T(8,128)} %copy-done.7), custom_call_target="tpu_custom_call" | custom-call | tf_op jit(solution)/shard_map/side_projections/pallas_call | solution.py:251
  38.2 1.5 %collective-permute-start.9 = (f32[48,128]{1,0:T(8,128)}, f32[48,128]{1,0:T(8,128)S(1)}, u32[]{:S(2)}, u32[]{:S(2)}) collective-permute-start(f32[48,128]{1,0:T(8,128)} %side_projections.1), channel_id=1, source_target_pairs={{12,14},{14,12},{0,2},{2,0},{4,6},{6,4},{8,10},{10,8},{13,15},{15,... | collective-permute-start | bytes 73736 | tf_op jit(solution)/shard_map/ppermute | solution.py:478
  39.7 10.3 %collective-permute-done.3.refs_4_ = bf16[624,128]{1,0:T(8,128)(2,1)S(1)} collective-permute-done((bf16[624,128]{1,0:T(8,128)(2,1)S(1)}, bf16[624,128]{1,0:T(8,128)(2,1)S(1)}, u32[]{:S(2)}, u32[]{:S(2)}) %collective-permute-start.3) | collective-permute-done | bytes 159776 | tf_op jit(solution)/shard_map/ppermute | solution.py:463
  50.0 4.2 %collective-permute-start.10 = (f32[48,128]{1,0:T(8,128)}, f32[48,128]{1,0:T(8,128)S(1)}, u32[]{:S(2)}, u32[]{:S(2)}) collective-permute-start(f32[48,128]{1,0:T(8,128)} %side_projections.1), channel_id=1, source_target_pairs={{14,0},{0,14},{6,8},{8,6},{15,1},{1,15},{7,9},{9,7},{30,16},{16,30... | collective-permute-start | bytes 73736 | tf_op jit(solution)/shard_map/ppermute | solution.py:481
  54.3 4.3 %collective-permute-done.10.refs_11_ = f32[48,128]{1,0:T(8,128)S(1)} collective-permute-done((f32[48,128]{1,0:T(8,128)}, f32[48,128]{1,0:T(8,128)S(1)}, u32[]{:S(2)}, u32[]{:S(2)}) %collective-permute-start.10) | collective-permute-done | bytes 24608 | tf_op jit(solution)/shard_map/ppermute | solution.py:481
  58.7 0.9 %copy-done.6 = f32[16,16,128]{2,1,0:T(8,128)S(1)} copy-done((f32[16,16,128]{2,1,0:T(8,128)S(1)}, f32[16,16,128]{2,1,0:T(8,128)}, u32[]{:S(2)}) %copy-start.6) | copy-done | bytes 131096
  59.6 0.8 %copy-done.8 = f32[64,128]{1,0:T(8,128)S(1)} copy-done((f32[64,128]{1,0:T(8,128)S(1)}, f32[64,128]{1,0:T(8,128)}, u32[]{:S(2)}) %copy-start.8) | copy-done | bytes 32792
  60.3 0.8 %statistics.1 = (bf16[256,128]{1,0:T(8,128)(2,1)S(1)}, bf16[256,128]{1,0:T(8,128)(2,1)S(1)}, f32[8,256]{1,0:T(8,128)S(1)}) custom-call(bf16[624,128]{1,0:T(8,128)(2,1)S(1)} %get-tuple-element.17.refs_0_, bf16[624,128]{1,0:T(8,128)(2,1)S(1)} %collective-permute-done.refs_1_, bf16[624,128]{1,0:T(8,128)(2,1)S(1)} %collective-permute-done.1.refs_2_, ...), custom_call_target="tpu_custom_call" | custom-call | tf_op jit(solution)/shard_map/statistics/pallas_call | solution.py:340
  61.1 0.5 collective-permute-start.11
  61.7 0.8 %collective-permute-done.11.lag_got_ref = f32[8,256]{1,0:T(8,128)S(1)} collective-permute-done((f32[8,256]{1,0:T(8,128)S(1)}, f32[8,256]{1,0:T(8,128)S(1)}, u32[]{:S(2)}, u32[]{:S(2)}) %collective-permute-start.11) | collective-permute-done | bytes 8224 | tf_op jit(solution)/shard_map/ppermute | solution.py:486
  62.5 2.9 %subtract.1 = (bf16[2,16,64,256]{3,2,1,0:T(8,128)(2,1)}, f32[2,33]{1,0:T(2,128)}) custom-call(f32[8,256]{1,0:T(8,128)S(1)} %get-tuple-element.27.lag_ref, f32[8,256]{1,0:T(8,128)S(1)} %collective-permute-done.11.lag_got_ref, f32[2,33]{1,0:T(2,128)S(1)} %bitcast.8, f32[2,16,256]{2,1,0:T(8,128)S(1)} %copy-done.10, f32[2,16,256]{2,1,0:T(8,128)S(1)} %copy-done.11, ...), custom_call_target="tpu_custom_call" | custom-call | tf_op jit(solution)/shard_map/subtract/pallas_call | solution.py:427
  (40 shorter events, 1.5 us)
Async XLA Ops:
  0.6 61.9 %copy-start.15 = (f32[1,1,1,2,33]{4,3,2,1,0:T(2,128)S(1)}, f32[1,1,1,2,33]{4,3,2,1,0:T(2,128)}, u32[]{:S(2)}) copy-start(f32[1,1,1,2,33]{4,3,2,1,0:T(2,128)} %param.10) | copy-start | bytes 796
  0.6 1.2 %copy-start.1 = (bf16[1,1,32,64,256]{4,3,2,1,0:T(8,128)(2,1)S(1)}, bf16[1,1,32,64,256]{4,3,2,1,0:T(8,128)(2,1)}, u32[]{:S(2)}) copy-start(bf16[1,1,32,64,256]{4,3,2,1,0:T(8,128)(2,1)} %param.9) | copy-start | bytes 3145732
  2.6 59.9 %copy-start.2 = (bf16[1,1,32,64,256]{4,3,2,1,0:T(8,128)(2,1)S(1)}, bf16[1,1,32,64,256]{4,3,2,1,0:T(8,128)(2,1)}, u32[]{:S(2)}) copy-start(bf16[1,1,32,64,256]{4,3,2,1,0:T(8,128)(2,1)} %param.9) | copy-start | bytes 3145732
  2.6 59.9 %copy-start.12 = (f32[2,16,128]{2,1,0:T(8,128)S(1)}, f32[2,16,128]{2,1,0:T(8,128)}, u32[]{:S(2)}) copy-start(f32[2,16,128]{2,1,0:T(8,128)} %constant.13.clone.cos_ref) | copy-start | bytes 49156
  3.7 19.3 %collective-permute-start.7 = (f32[16,16,128]{2,1,0:T(8,128)S(1)}, f32[16,16,128]{2,1,0:T(8,128)S(1)}, u32[]{:S(2)}, u32[]{:S(2)}) collective-permute-start(f32[16,16,128]{2,1,0:T(8,128)S(1)} %get-tuple-element.26), channel_id=1, source_target_pairs={{0,1},{1,0},{2,3},{3,2},{4,5},{5,4},{6,7},{7,6},{8,9},{9,8},{10,11... | collective-permute-start | bytes 393224 | tf_op jit(solution)/shard_map/ppermute | solution.py:467
  4.2 5.8 %copy-start = (bf16[2,8,512,1024]{3,2,1,0:T(8,128)(2,1)S(1)}, bf16[2,8,512,1024]{3,2,1,0:T(8,128)(2,1)}, u32[]{:S(2)}) copy-start(bf16[2,8,512,1024]{3,2,1,0:T(8,128)(2,1)} %s_ref.1) | copy-start | bytes 50331652
  9.9 48.7 %copy-start.4 = (f32[16,16,128]{2,1,0:T(8,128)S(1)}, f32[16,16,128]{2,1,0:T(8,128)}, u32[]{:S(2)}) copy-start(f32[16,16,128]{2,1,0:T(8,128)} %copy-done.3) | copy-start | bytes 393220
  9.9 48.7 %copy-start.9 = (f32[2,32,256]{2,1,0:T(8,128)S(1)}, f32[2,32,256]{2,1,0:T(8,128)}, u32[]{:S(2)}) copy-start(f32[2,32,256]{2,1,0:T(8,128)} %constant.12.clone.refs_12_) | copy-start | bytes 196612
  9.9 52.6 %copy-start.10 = (f32[2,16,256]{2,1,0:T(8,128)S(1)}, f32[2,16,256]{2,1,0:T(8,128)}, u32[]{:S(2)}) copy-start(f32[2,16,256]{2,1,0:T(8,128)} %constant.10.clone.time_ref) | copy-start | bytes 98308
  9.9 52.6 %copy-start.11 = (f32[2,16,256]{2,1,0:T(8,128)S(1)}, f32[2,16,256]{2,1,0:T(8,128)}, u32[]{:S(2)}) copy-start(f32[2,16,256]{2,1,0:T(8,128)} %constant.11.clone.turned_ref) | copy-start | bytes 98308
  9.9 52.6 %copy-start.13 = (f32[2,16,128]{2,1,0:T(8,128)S(1)}, f32[2,16,128]{2,1,0:T(8,128)}, u32[]{:S(2)}) copy-start(f32[2,16,128]{2,1,0:T(8,128)} %constant.14.clone.sin_ref) | copy-start | bytes 49156
  18.9 9.5 %collective-permute-start = (bf16[624,128]{1,0:T(8,128)(2,1)S(1)}, bf16[624,128]{1,0:T(8,128)(2,1)S(1)}, u32[]{:S(2)}, u32[]{:S(2)}) collective-permute-start(bf16[624,128]{1,0:T(8,128)(2,1)S(1)} %get-tuple-element.18), channel_id=1, source_target_pairs={{0,2},{2,0},{4,6},{6,4},{8,10},{10,8},{12,14},{14,12},{1,3},{3,1},... | collective-permute-start | bytes 479240 | tf_op jit(solution)/shard_map/ppermute | solution.py:463
  21.4 10.8 %collective-permute-start.1 = (bf16[624,128]{1,0:T(8,128)(2,1)S(1)}, bf16[624,128]{1,0:T(8,128)(2,1)S(1)}, u32[]{:S(2)}, u32[]{:S(2)}) collective-permute-start(bf16[624,128]{1,0:T(8,128)(2,1)S(1)} %get-tuple-element.19), channel_id=1, source_target_pairs={{0,4},{2,6},{4,0},{6,2},{8,12},{10,14},{12,8},{14,10},{1,5},{3,7},... | collective-permute-start | bytes 479240 | tf_op jit(solution)/shard_map/ppermute | solution.py:463
  25.3 8.2 %collective-permute-start.8 = (f32[64,128]{1,0:T(8,128)}, f32[64,128]{1,0:T(8,128)S(1)}, u32[]{:S(2)}, u32[]{:S(2)}) collective-permute-start(f32[64,128]{1,0:T(8,128)} %band_projections.1), channel_id=1, source_target_pairs={{12,4},{14,6},{0,8},{2,10},{4,12},{6,14},{8,0},{10,2},{13,5},{15,7... | collective-permute-start | bytes 98312 | tf_op jit(solution)/shard_map/ppermute | solution.py:476
  27.9 10.2 %collective-permute-start.2 = (bf16[624,128]{1,0:T(8,128)(2,1)S(1)}, bf16[624,128]{1,0:T(8,128)(2,1)S(1)}, u32[]{:S(2)}, u32[]{:S(2)}) collective-permute-start(bf16[624,128]{1,0:T(8,128)(2,1)S(1)} %get-tuple-element.20), channel_id=1, source_target_pairs={{0,6},{2,4},{4,2},{6,0},{8,14},{10,12},{12,10},{14,8},{1,7},{3,5},... | collective-permute-start | bytes 479240 | tf_op jit(solution)/shard_map/ppermute | solution.py:463
  28.3 21.6 %collective-permute-start.3 = (bf16[624,128]{1,0:T(8,128)(2,1)S(1)}, bf16[624,128]{1,0:T(8,128)(2,1)S(1)}, u32[]{:S(2)}, u32[]{:S(2)}) collective-permute-start(bf16[624,128]{1,0:T(8,128)(2,1)S(1)} %get-tuple-element.21), channel_id=1, source_target_pairs={{0,8},{2,10},{4,12},{6,14},{8,0},{10,2},{12,4},{14,6},{1,9},{3,11}... | collective-permute-start | bytes 479240 | tf_op jit(solution)/shard_map/ppermute | solution.py:463
  28.3 26.0 %collective-permute-start.4 = (bf16[624,128]{1,0:T(8,128)(2,1)S(1)}, bf16[624,128]{1,0:T(8,128)(2,1)S(1)}, u32[]{:S(2)}, u32[]{:S(2)}) collective-permute-start(bf16[624,128]{1,0:T(8,128)(2,1)S(1)} %get-tuple-element.22), channel_id=1, source_target_pairs={{0,10},{2,8},{4,14},{6,12},{8,2},{10,0},{12,6},{14,4},{1,11},{3,9}... | collective-permute-start | bytes 479240 | tf_op jit(solution)/shard_map/ppermute | solution.py:463
  32.2 22.1 %collective-permute-start.5 = (bf16[624,128]{1,0:T(8,128)(2,1)S(1)}, bf16[624,128]{1,0:T(8,128)(2,1)S(1)}, u32[]{:S(2)}, u32[]{:S(2)}) collective-permute-start(bf16[624,128]{1,0:T(8,128)(2,1)S(1)} %get-tuple-element.23), channel_id=1, source_target_pairs={{0,12},{2,14},{4,8},{6,10},{8,4},{10,6},{12,0},{14,2},{1,13},{3,15... | collective-permute-start | bytes 479240 | tf_op jit(solution)/shard_map/ppermute | solution.py:463
  33.6 2.4 %copy-start.7 = (f32[64,128]{1,0:T(8,128)}, f32[64,128]{1,0:T(8,128)S(1)}, u32[]{:S(2)}) copy-start(f32[64,128]{1,0:T(8,128)S(1)} %collective-permute-done.8.rest_0_.refs_13_) | copy-start | bytes 98308
  33.6 20.8 %collective-permute-start.6 = (bf16[624,128]{1,0:T(8,128)(2,1)S(1)}, bf16[624,128]{1,0:T(8,128)(2,1)S(1)}, u32[]{:S(2)}, u32[]{:S(2)}) collective-permute-start(bf16[624,128]{1,0:T(8,128)(2,1)S(1)} %get-tuple-element.24), channel_id=1, source_target_pairs={{0,14},{2,12},{4,10},{6,8},{8,6},{10,4},{12,2},{14,0},{1,15},{3,13... | collective-permute-start | bytes 479240 | tf_op jit(solution)/shard_map/ppermute | solution.py:463
  38.2 16.2 %collective-permute-start.9 = (f32[48,128]{1,0:T(8,128)}, f32[48,128]{1,0:T(8,128)S(1)}, u32[]{:S(2)}, u32[]{:S(2)}) collective-permute-start(f32[48,128]{1,0:T(8,128)} %side_projections.1), channel_id=1, source_target_pairs={{12,14},{14,12},{0,2},{2,0},{4,6},{6,4},{8,10},{10,8},{13,15},{15,... | collective-permute-start | bytes 73736 | tf_op jit(solution)/shard_map/ppermute | solution.py:478
  50.0 8.7 %collective-permute-start.10 = (f32[48,128]{1,0:T(8,128)}, f32[48,128]{1,0:T(8,128)S(1)}, u32[]{:S(2)}, u32[]{:S(2)}) collective-permute-start(f32[48,128]{1,0:T(8,128)} %side_projections.1), channel_id=1, source_target_pairs={{14,0},{0,14},{6,8},{8,6},{15,1},{1,15},{7,9},{9,7},{30,16},{16,30... | collective-permute-start | bytes 73736 | tf_op jit(solution)/shard_map/ppermute | solution.py:481
  61.1 1.4 %collective-permute-start.12 = (bf16[256,128]{1,0:T(8,128)(2,1)S(1)}, bf16[256,128]{1,0:T(8,128)(2,1)S(1)}, u32[]{:S(2)}, u32[]{:S(2)}) collective-permute-start(bf16[256,128]{1,0:T(8,128)(2,1)S(1)} %get-tuple-element.29), channel_id=1, source_target_pairs={{0,1},{1,0},{2,3},{3,2},{4,5},{5,4},{6,7},{7,6},{8,9},{9,8},{10,11... | collective-permute-start | bytes 196616 | tf_op jit(solution)/shard_map/ppermute | solution.py:485
  61.1 1.4 %collective-permute-start.11 = (f32[8,256]{1,0:T(8,128)S(1)}, f32[8,256]{1,0:T(8,128)S(1)}, u32[]{:S(2)}, u32[]{:S(2)}) collective-permute-start(f32[8,256]{1,0:T(8,128)S(1)} %get-tuple-element.27.lag_ref), channel_id=1, source_target_pairs={{0,1},{1,0},{2,3},{3,2},{4,5},{5,4},{6,7},{7,6},{8,9},{9,8},{10,11... | collective-permute-start | bytes 24584 | tf_op jit(solution)/shard_map/ppermute | solution.py:486
  (5 other events, 3.7 us)

commit v2 on v1

v2 whole, which is shorter than its diff:
```python
import functools
import math

import jax
import jax.numpy as jnp
import numpy as np
from jax import lax
from jax.experimental import pallas as pl
from jax.experimental.pallas import tpu as pltpu
from jax.sharding import PartitionSpec as P

NF = 16
K0 = 48
NT = 256
XR = 8192
WC = 32
WM = 4
TAPS = 33
ITERS = 3
HALF = (TAPS - 1) // 2
COLS = 4
LANES = 128
HF = 8
TERMS_VMEM = 48 * 1024 * 1024
AHEAD = 3
EXACT = lax.Precision.HIGHEST
F32 = jnp.float32
BF16 = jnp.bfloat16
VMEM = pltpu.CompilerParams(vmem_limit_bytes=12 * 1024 * 1024)


def tables():
    f = np.arange(NF)
    t = np.arange(NT)
    w = 2.0 * np.pi * (K0 + f) / NT
    angle = 2.0 * np.pi * (((K0 + f)[:, None] * t[None, :]) % NT) / NT
    weight = math.sqrt(2.0 / NF)
    table = np.stack([weight * np.cos(angle), -weight * np.sin(angle)], 1)
    table = table.astype(np.float32).astype(jnp.bfloat16).astype(np.float32)
    halves = table.reshape(2, HF, 2, NT).transpose(0, 2, 1, 3)
    time = halves.reshape(2, 2 * HF, NT)
    turned = np.stack([-halves[:, 1], halves[:, 0]], 1).reshape(2, 2 * HF, NT)
    lane = np.arange(LANES)
    held = lane < TAPS
    tap = lane - HALF
    cos_k = np.where(held, np.cos(w[:, None] * tap), 0.0).reshape(2, HF, LANES)
    sin_k = np.where(held, np.sin(w[:, None] * tap), 0.0).reshape(2, HF, LANES)
    lag = np.where(held, 16.0 * np.cos(w[:, None] * lane), 0.0).reshape(2, HF, LANES)
    zero = np.zeros_like(lag)
    to_lag = np.concatenate([lag, zero, zero, zero], 1)
    to_target = np.concatenate([zero, cos_k, sin_k, zero], 1)
    lags = np.concatenate([to_lag, to_target], 2)
    trig = np.concatenate([np.concatenate([cos_k, cos_k], 1), np.concatenate([sin_k, sin_k], 1)], 2)
    return np.concatenate([time, turned, lags, trig], 1).astype(np.float32)


TIME, TURNED, LAGS, TRIG = (slice(0, 16), slice(16, 32), slice(32, 64), slice(64, 80))


def lanes_of(rows):
    return lax.broadcasted_iota(jnp.int32, (rows, LANES), 1)


def band_rows(p, rows):
    if rows == 2:
        return [WC if p == 0 else WC - WM]
    return [p * WC - WM if p > 0 else None, (p + 1) * WC if p < rows - 1 else None]


def terms_kernel(rows, s_hbm, *rest):
    refl = rows * COLS
    outs, (buffer, blocks, bands, sides, arrived) = rest[:-5], rest[-5:]
    sources = rows * WC
    freqs, _, _, width = buffer.shape
    amplitude = 1.0 / math.sqrt(2.0 * XR)
    nb = len(band_rows(0, rows))
    main = 2 * HF * WC

    def fetch(f, part):
        return pltpu.make_async_copy(s_hbm.at[part, f], buffer.at[f, part], arrived.at[f, part])

    for f in range(AHEAD):
        for part in range(2):
            fetch(f, part).start()

    def products(f):
        if f + AHEAD < freqs:
            for part in range(2):
                fetch(f + AHEAD, part).start()
        for part in range(2):
            fetch(f, part).wait()
        left = buffer[f, :, :sources, :].reshape(2 * sources, width)
        parts = [[], []]
        for c in range(COLS):
            right = buffer[f, :, c * LANES : (c + 1) * LANES, :].reshape(2 * LANES, width)
            got = lax.dot_general(left, right, (((1,), (1,)), ((), ())), preferred_element_type=F32)
            parts[0].append(amplitude * (got[:sources, :LANES] - got[sources:, LANES:]))
            parts[1].append(amplitude * (got[:sources, LANES:] + got[sources:, :LANES]))
        return parts

    def place(f, parts):
        for c in range(COLS):
            for p in range(rows):
                g = p * COLS + c
                for part in range(2):
                    at = part * HF * WC + f * WC
                    x = parts[part][c][p * WC : (p + 1) * WC]
                    blocks[g, at : at + WC, :] = x.astype(BF16)
                for n, start in enumerate(band_rows(p, rows)):
                    if start is None:
                        band = jnp.zeros((2 * WM, LANES), F32)
                    else:
                        band = jnp.concatenate([x[c][start : start + WM] for x in parts], 0)
                    bands[g, n * HF * 8 + f * 8 : n * HF * 8 + f * 8 + 8, :] = band
        lane = lanes_of(sources)
        base = f * 16
        first = (lane >= base) & (lane < base + 8)
        second = (lane >= base + 8) & (lane < base + 16)
        zero = jnp.zeros((sources, LANES), F32)
        for c in range(COLS):
            side = sides[c]
            for part, here in enumerate((first, second)):
                x = parts[part]
                before = x[c - 1] if c > 0 else zero
                after = x[c + 1] if c < COLS - 1 else zero
                moved = jnp.where(lane >= LANES // 2, before, after)
                moved = pltpu.roll(moved, (base + part * 8 + WM) % LANES, 1)
                side = jnp.where(here, moved, side)
            sides[c] = side

    before = None
    for f in range(freqs):
        parts = products(f)
        if before is not None:
            place(f - 1, before)
        before = parts
    place(freqs - 1, before)
    me = lax.axis_index("refl")
    for p in range(rows):
        for c in range(COLS):
            g = p * COLS + c
            blocks[g, main : main + nb * 64, :] = bands[g].astype(BF16)
            side = [sides[c, p * WC : (p + 1) * WC, :]]
            for start in band_rows(p, rows):
                side.append(
                    jnp.zeros((WM, LANES), F32)
                    if start is None
                    else sides[c, start : start + WM, :]
                )
            side.append(jnp.zeros((16 - nb * WM, LANES), F32))
            blocks[g, main + nb * 64 :, :] = jnp.concatenate(side, 0).astype(BF16)
    for out, k in zip(outs, parcels(refl)):
        out[...] = blocks[((me ^ k) + 2) % refl]


def parcels(refl):
    places = list(range(refl - 2, -1, -2))
    return [k ^ 1 for k in places] + places


def block_terms(spectra, rows):
    refl = rows * COLS
    freqs, receivers, width = spectra.shape[1:]
    nb = len(band_rows(0, rows))
    size = 2 * HF * WC + nb * 64 + 48
    return pl.pallas_call(
        functools.partial(terms_kernel, rows),
        in_specs=[pl.BlockSpec(memory_space=pl.ANY)],
        out_shape=[jax.ShapeDtypeStruct((size, LANES), BF16)] * refl,
        scratch_shapes=[
            pltpu.VMEM((freqs, 2, receivers, width), BF16),
            pltpu.VMEM((refl, size, LANES), BF16),
            pltpu.VMEM((refl, nb * 64, LANES), F32),
            pltpu.VMEM((COLS, rows * WC, LANES), F32),
            pltpu.SemaphoreType.DMA((freqs, 2)),
        ],
        compiler_params=pltpu.CompilerParams(vmem_limit_bytes=TERMS_VMEM),
        name="block_terms",
    )(spectra)


def project_kernel(r_ref, t_ref, keep_ref, send_ref):
    j = lax.axis_index("freq")
    table = jnp.concatenate([t_ref[j, TIME], t_ref[1 - j, TIME]], 0).astype(BF16)
    half = WC // 2
    for s in range(half):
        pair = jnp.concatenate([r_ref[s], r_ref[half + s]], 0)
        got = lax.dot_general(table, pair, (((1,), (1,)), ((), ())), preferred_element_type=F32)
        keep_ref[s] = got[: 2 * HF]
        send_ref[s] = got[2 * HF :]


def project(recorded, table):
    shape = jax.ShapeDtypeStruct((WC // 2, 2 * HF, LANES), F32)
    return pl.pallas_call(
        project_kernel, out_shape=[shape, shape], compiler_params=VMEM, name="project"
    )(recorded, table)


def grid_place(rows):
    g = (lax.axis_index("refl") + 2) % (rows * COLS)
    return g // COLS, g % COLS


def edge_kernel(rows, keep_ref, other_ref, *outs):
    bands, sides_ref = outs[:-1], outs[-1]
    j = lax.axis_index("freq")
    p, _ = grid_place(rows)
    half = WC // 2
    low = lanes_of(HF) < LANES // 2

    def build(out_ref, first, upper):
        for s in range(WM):
            for part in range(2):
                rows_of = pl.ds(part * HF, HF)
                kept = keep_ref[first + s, rows_of, :]
                other = other_ref[first + s, rows_of, :]
                a = jnp.where(j == 0, kept, other)
                b = jnp.where(j == 0, other, kept)
                plain = jnp.where(low, a, pltpu.roll(b, LANES // 2, 1))
                shifted = jnp.where(low, pltpu.roll(a, LANES // 2, 1), b)
                band = jnp.where(upper, shifted, plain)
                out_ref[pl.ds(part * WM + s, HF, stride=8), :] = band

    if rows == 2:
        build(bands[0], jnp.where(p == 0, half - WM, 0), p == 0)
    else:
        build(bands[0], half - WM, True)
        build(bands[1], 0, False)

    keep = keep_ref[...].reshape(half * 2 * HF, LANES)
    other = other_ref[...].reshape(half * 2 * HF, LANES)
    left = jnp.where(j == 0, keep, other).astype(BF16)
    right = jnp.where(j == 0, other, keep).astype(BF16)
    row = lax.broadcasted_iota(jnp.int32, (LANES, LANES), 0)
    r = lax.broadcasted_iota(jnp.int32, (LANES, LANES), 1) % 8
    at = lax.broadcasted_iota(jnp.int32, (half, 2 * HF, LANES), 1)
    lane = lax.broadcasted_iota(jnp.int32, (half, 2 * HF, LANES), 2)
    mine = (lane // 16 == at % HF) & ((lane // 8) % 2 == at // HF)
    for upper in range(2):
        from_right = ((row == upper * 64 + 60 + r) & (r < WM)).astype(F32).astype(BF16)
        from_left = ((row == upper * 64 + r - WM) & (r >= WM)).astype(F32).astype(BF16)
        x = jnp.dot(left, from_left, preferred_element_type=F32)
        x = x + jnp.dot(right, from_right, preferred_element_type=F32)
        x = jnp.where(mine, x.reshape(half, 2 * HF, LANES), 0.0)
        sides_ref[upper * half : (upper + 1) * half, :] = jnp.sum(x, 1)


def edge_projections(keep, other, rows):
    nb = len(band_rows(0, rows))
    return pl.pallas_call(
        functools.partial(edge_kernel, rows),
        out_shape=[jax.ShapeDtypeStruct((64, LANES), F32)] * nb
        + [jax.ShapeDtypeStruct((WC, LANES), F32)],
        compiler_params=VMEM,
        name="edge_projections",
    )(keep, other)


def statistics_kernel(rows, *refs):
    nb = len(band_rows(0, rows))
    count = rows * COLS // 2 + 1
    blocks, refs = refs[:count], refs[count:]
    keep_ref, other_ref, lags_ref = refs[:3]
    bands, refs = refs[3 : 3 + nb], refs[3 + nb :]
    nears, refs = refs[: 1 + nb], refs[1 + nb :]
    fars, refs = refs[: 1 + nb], refs[1 + nb :]
    own_ref, send_ref, lag_ref, spectrum = refs
    j = lax.axis_index("freq")
    p, c = grid_place(rows)
    half = WC // 2

    def summed(start, size):
        total = blocks[0][start : start + size, :].astype(F32)
        for block in blocks[1:]:
            total = total + block[start : start + size, :].astype(F32)
        return total.astype(BF16).astype(F32)

    low = lanes_of(half) < LANES // 2
    for fp in range(2 * HF):
        x = summed(fp * WC, WC)
        a, b = x[:half], x[half:]
        first = jnp.where(low, a, pltpu.roll(b, LANES // 2, 1))
        second = jnp.where(low, pltpu.roll(a, LANES // 2, 1), b)
        spectrum[pl.ds(fp, half, stride=16), :] = first
        spectrum[pl.ds(half * 16 + fp, half, stride=16), :] = second
    count = half * 16
    here = pl.multiple_of(j * count, count)
    there = pl.multiple_of((1 - j) * count, count)
    own_ref[...] = spectrum[pl.ds(here, count), :].astype(BF16)
    send_ref[...] = spectrum[pl.ds(there, count), :].astype(BF16)
    sums = []
    for at, q_ref in ((here, keep_ref), (there, other_ref)):
        power = in_phase = turned = jnp.zeros((HF, LANES), F32)
        for s in range(half):
            a = spectrum[pl.ds(at + s * 16, HF), :]
            b = spectrum[pl.ds(at + s * 16 + HF, HF), :]
            qc, qs = q_ref[s, :HF, :], q_ref[s, HF:, :]
            power = power + (a * a + b * b)
            in_phase = in_phase + (a * qc + b * qs)
            turned = turned + (b * qc - a * qs)
        sums.append([power, in_phase, turned])
    total = None
    sub = lax.broadcasted_iota(jnp.int32, (HF, 8, LANES), 1)
    for n in range(nb):
        x = summed(2 * HF * WC + n * 64, 64).reshape(HF, 8, LANES)
        q = bands[n][...].reshape(HF, 8, LANES)
        partner = jnp.where(sub < WM, -1.0, 1.0) * pltpu.roll(q, WM, 1)
        here_sums = [jnp.sum(x * y, 1) for y in (x, q, partner)]
        total = here_sums if total is None else [a + b for a, b in zip(total, here_sums)]
    sums.append(total)

    window = lax.broadcasted_iota(jnp.int32, (8, LANES), 0)
    lane = lanes_of(8)
    window = jnp.where(window < 4, (window + 2 * j) % 4, 8)
    starts = window * WC - WM

    def mask(receiver):
        return ((receiver >= starts) & (receiver < starts + WC + 2 * WM)).astype(F32)

    dot = functools.partial(lax.dot_general, precision=EXACT, preferred_element_type=F32)
    stats = jnp.zeros((8, 32), F32)
    receivers = (j * 64 + lane % 64, (1 - j) * 64 + lane % 64, lane)
    for x, receiver in zip(sums, receivers):
        x = jnp.concatenate(x + [jnp.zeros((HF, LANES), F32)], 0)
        stats = stats + dot(mask(receiver), x, (((1,), (1,)), ((), ())))
    x = summed(2 * HF * WC + nb * 64, 48)
    l48 = lanes_of(48)
    from_near = ((l48 % 8) < WM) == ((c % 2) == 1)
    q = []
    for sides in (nears, fars):
        pieces = [sides[0][...]]
        for n, side in enumerate(sides[1:]):
            top, bottom = side[:WM, :], side[WC - WM :, :]
            pieces.append(jnp.where(p == 0, top, bottom) if nb == 1 else (bottom, top)[n])
        pieces.append(jnp.zeros((16 - nb * WM, LANES), F32))
        q.append(jnp.concatenate(pieces, 0))
    q = jnp.where(from_near, q[0], q[1])
    first_part = (l48 // 8) % 2 == 0
    partner = jnp.where(first_part, -pltpu.roll(q, LANES - 8, 1), pltpu.roll(q, 8, 1))
    row = lax.broadcasted_iota(jnp.int32, (LANES, 32), 0)
    column = lax.broadcasted_iota(jnp.int32, (LANES, 32), 1)
    at_side = ((window == 0) & (lane % 8 < WM)) | ((window == 3) & (lane % 8 >= WM))
    for n, y in enumerate((x, q, partner)):
        z = jnp.sum(x * y, 0, keepdims=True)
        z = jnp.where(at_side, jnp.broadcast_to(z, (8, LANES)), 0.0)
        to = (column == n * HF + row // 16).astype(F32)
        stats = stats + dot(z, to, (((1,), (0,)), ((), ())))
    lag_ref[...] = dot(stats, lags_ref[j, LAGS], (((1,), (0,)), ((), ())))


def statistics(blocks, keep, other, table, bands, nears, fars, rows):
    count = WC // 2 * 2 * HF
    return pl.pallas_call(
        functools.partial(statistics_kernel, rows),
        out_shape=[
            jax.ShapeDtypeStruct((count, LANES), BF16),
            jax.ShapeDtypeStruct((count, LANES), BF16),
            jax.ShapeDtypeStruct((8, 2 * LANES), F32),
        ],
        scratch_shapes=[pltpu.VMEM((2 * count, LANES), F32)],
        compiler_params=VMEM,
        name="statistics",
    )(*blocks, keep, other, table, *bands, *nears, *fars)


def subtract_kernel(
    steps,
    lag_ref,
    lag_got_ref,
    start_ref,
    table_ref,
    own_ref,
    got_ref,
    r_low_ref,
    r_high_ref,
    clean_ref,
    filters_ref,
    wavelets,
):
    step = pl.program_id(0)
    j = lax.axis_index("freq")
    half = WC // 2

    @pl.when(step == 0)
    def _():
        total = lag_ref[0:2, :] + lag_got_ref[2:4, :]
        lag, target = total[:, :LANES], total[:, LANES:]
        lane = lanes_of(2)
        held = lane < TAPS
        magnitude = jnp.where(held, jnp.abs(lag), 0.0)
        zero_lag = jnp.sum(jnp.where(lane == 0, lag, 0.0), 1, keepdims=True)
        others = jnp.sum(jnp.where(lane >= 1, magnitude, 0.0), 1, keepdims=True)
        step_size = 0.5 / (zero_lag + 2.0 * others + 1e-06)
        filters = jnp.concatenate(
            [start_ref[...], jnp.zeros((2, LANES - TAPS), F32)], 1
        )
        spread = [jnp.broadcast_to(lag[:, d : d + 1], (2, LANES)) for d in range(TAPS)]
        for repeat in range(ITERS):
            applied = spread[0] * filters
            for d in range(1, TAPS):
                applied = applied + spread[d] * (
                    pltpu.roll(filters, d, 1) + pltpu.roll(filters, LANES - d, 1)
                )
            filters = jnp.where(held, filters + step_size * (target - applied), 0.0)
        filters_ref[...] = filters[:, :TAPS]
        taps = filters.astype(BF16).astype(F32)
        for w in range(2):
            for n, h in enumerate((j, 1 - j)):
                tap = taps[w : w + 1, :]
                hc = jnp.sum(table_ref[h, TRIG, :LANES] * tap, 1, keepdims=True)
                hs = jnp.sum(table_ref[h, TRIG, LANES:] * tap, 1, keepdims=True)
                wave = hc * table_ref[h, TIME] + hs * table_ref[h, TURNED]
                at = w * 32 + n * 16
                wavelets[at : at + 16, :] = wave.astype(BF16)

    table = wavelets[...]
    lane = lax.broadcasted_iota(jnp.int32, (32, LANES), 1)
    first = (lane % 64) < WC
    zero = jnp.zeros((32, LANES), BF16)
    for s in range(half // steps):
        x = jnp.concatenate([own_ref[s * 16 : s * 16 + 16, :], got_ref[s * 16 : s * 16 + 16, :]], 0)
        both = jnp.concatenate([jnp.where(first, x, zero), jnp.where(first, zero, x)], 0)
        predicted = lax.dot_general(
            both, table, (((0,), (0,)), ((), ())), preferred_element_type=F32
        )
        clean_ref[0, s] = (r_low_ref[0, s].astype(F32) - predicted[:64]).astype(BF16)
        clean_ref[1, s] = (r_high_ref[0, s].astype(F32) - predicted[64:]).astype(BF16)


def subtract(lag, lag_got, start, table, own, got, recorded):
    steps = 4
    half = WC // 2
    each = half // steps
    recorded = recorded.reshape(2, half, 64, NT)
    whole = lambda x: pl.BlockSpec(x.shape, lambda i: (0,) * x.ndim)
    small = (lag, lag_got, start, table)
    rows_spec = pl.BlockSpec((each * 16, LANES), lambda i: (i, 0))
    return pl.pallas_call(
        functools.partial(subtract_kernel, steps),
        grid=(steps,),
        in_specs=[whole(x) for x in small]
        + [
            rows_spec,
            rows_spec,
            pl.BlockSpec((1, each, 64, NT), lambda i: (0, i, 0, 0)),
            pl.BlockSpec((1, each, 64, NT), lambda i: (1, i, 0, 0)),
        ],
        out_specs=[
            pl.BlockSpec((2, each, 64, NT), lambda i: (0, i, 0, 0)),
            pl.BlockSpec((2, TAPS), lambda i: (0, 0)),
        ],
        out_shape=[
            jax.ShapeDtypeStruct((2, half, 64, NT), BF16),
            jax.ShapeDtypeStruct((2, TAPS), F32),
        ],
        scratch_shapes=[pltpu.VMEM((64, NT), BF16)],
        compiler_params=VMEM,
        name="subtract",
    )(*small, own, got, recorded, recorded)


def body(spectra, recorded, initial_filters):
    refl = lax.axis_size("refl")
    rows = refl // COLS
    table = jnp.asarray(tables())
    core_swap = [(0, 1), (1, 0)]

    def place(p, c):
        return (p * COLS + c - 2) % refl

    def swap(x, k):
        return lax.ppermute(x, "refl", [(i, i ^ k) for i in range(refl)])

    def add(x, y):
        return (x.astype(F32) + y.astype(F32)).astype(BF16)

    after = lax.optimization_barrier
    blocks = block_terms(spectra, rows)
    pairs = refl // 2
    sent, kept = list(blocks[:pairs]), blocks[pairs:]
    came = [swap(sent[0], 1)]
    tile, sent[1] = after((recorded[0, 0], sent[1]))
    keep, send = project(tile, table)
    other = lax.ppermute(send, "freq", core_swap)
    *bands, sides = edge_projections(keep, other, rows)
    sent[1], sides, *bands = after((sent[1], sides, *bands))
    came.append(swap(sent[1], 1))
    if rows == 2:
        near = swap(sides, 1)
    got = []
    for n, k in enumerate(range(refl - 2, 0, -2)):
        total = add(kept[n], came[n])
        if n + 2 < pairs:
            total, sent[n + 2] = after((total, sent[n + 2]))
            came.append(swap(sent[n + 2], 1))
        if rows == 2 and n == 0:
            total, near, bands[0] = after((total, near, bands[0]))
        came[n + 1], total = after((came[n + 1], total))
        got.append(swap(total, k))
        if rows == 2 and n == 1:
            bands = [swap(bands[0], k)]
    got = [kept[-1], came[-1]] + got
    if rows == 2:
        nears, fars = [near, swap(near, 4)], [swap(near, 6), swap(near, 2)]
    else:

        def shift(x, rise, across):
            route = [
                (place(p, c), place(p + rise, across[c]))
                for p in range(rows)
                for c in range(COLS)
                if 0 <= p + rise < rows and across[c] is not None
            ]
            return lax.ppermute(x, "refl", route)

        bands = [shift(x, rise, (0, 1, 2, 3)) for x, rise in zip(bands, (1, -1))]
        nears = [shift(sides, rise, (1, 0, 3, 2)) for rise in (0, 1, -1)]
        fars = [shift(sides, rise, (None, 2, 1, None)) for rise in (0, 1, -1)]
    own, away, lag = statistics(got, keep, other, table, bands, nears, fars, rows)
    away_got = lax.ppermute(away, "freq", core_swap)
    lag_got = lax.ppermute(lag, "freq", core_swap)
    clean, filters = subtract(
        lag,
        lag_got,
        initial_filters.reshape(2, TAPS),
        table,
        own,
        away_got,
        tile,
    )
    return (clean.reshape(recorded.shape), filters.reshape(initial_filters.shape))


def solution(mesh):
    placed = (
        P(None, "freq", "groups", "refl"),
        P("refl", "freq", "groups", None, None),
        P("refl", "freq", "groups", None, None),
    )
    return jax.shard_map(
        body,
        mesh=mesh,
        in_specs=placed,
        out_specs=(
            P("refl", "freq", "groups", None, None),
            P("refl", "freq", "groups", None, None),
        ),
        check_vma=False,
    )
```

time: 65.8 us -> 49.7 us (0.76)
  local copies, waits for them, and re-layouts: 10.7 us -> 0.02 us
  waiting for transfers between devices: 15.6 us -> 11.4 us
  Pallas kernels: 16.8 us -> 12.9 us
  starting transfers between devices: 21.5 us -> 24.3 us
    unnamed x32 -> x6, local copies, waits for them, and re-layouts: 10.7 us -> 0.02 us
    ppermute x11 -> x13, waiting for transfers between devices: 14.8 us -> 9.23 us  [the longest x12 9.23 us: swap(): return lax.ppermute(x, 'refl', [(i, i ^ k) for i in range(refl)])]
    pallas_call x3 -> x2, Pallas kernels: 12.7 us -> 8.87 us  [the longest x1 8.65 us: block_terms(): pl.pallas_call(functools.partial(terms_kernel, rows), in_specs=[pl.BlockS...]
    ppermute x11 -> x13, starting transfers between devices: 20.5 us -> 23.8 us  [the longest x12 23.8 us: swap(): return lax.ppermute(x, 'refl', [(i, i ^ k) for i in range(refl)])]
    ppermute x1, waiting for transfers between devices: 0.01 us -> 1.33 us  [body(): other = lax.ppermute(send, 'freq', core_swap)]
  transfers between devices with their start and end apart: 13 -> 15, of which waited for: 4 -> 5; matrix products, arithmetic and copies ran while one was open for 0% -> 0% of each run, Pallas kernels for 19% -> 1%
where the time goes in v2:
time: 49.7 us; the launch traced here: 49.5 us
  starting transfers between devices  24.3 us (49%)
  Pallas kernels  12.9 us (26%)
  waiting for transfers between devices  11.4 us (23%)
  between operations  0.72 us (1%)
    ppermute x12, starting transfers between devices, swap(): return lax.ppermute(x, 'refl', [(i, i ^ k) for i in range(refl)])  23.8 us
    ppermute x12, waiting for transfers between devices, swap(): return lax.ppermute(x, 'refl', [(i, i ^ k) for i in range(refl)])  9.23 us
    pallas_call x1, Pallas kernels, block_terms(): pl.pallas_call(functools.partial(terms_kernel, rows), in_specs=[pl.BlockS...  8.65 us
    pallas_call x1, Pallas kernels, subtract(): pl.pallas_call(functools.partial(subtract_kernel, steps), grid=(steps,),...  2.83 us
    ppermute x1, waiting for transfers between devices, body(): other = lax.ppermute(send, 'freq', core_swap)  1.33 us
  transfers between devices with their start and end apart: 15, of which 5 were waited for; matrix products, arithmetic and copies ran while one was open for 0% of the time, Pallas kernels for 1%

profile of v2, /device:TPU:0, one launch (start us, length us, event | category | flops | bytes accessed | tf_op | source)
XLA Modules:
  0.0 49.5 jit_solution(12746272031468079904)
XLA Ops:
  0.7 8.6 %block_terms.1 = (bf16[624,128]{1,0:T(8,128)(2,1)S(1)}, bf16[624,128]{1,0:T(8,128)(2,1)S(1)}, bf16[624,128]{1,0:T(8,128)(2,1)S(1)}, bf16[624,128]{1,0:T(8,128)(2...) custom-call(bf16[2,8,512,1024]{3,2,1,0:T(8,128)(2,1)} %s_hbm.1), custom_call_target="tpu_custom_call" | custom-call | tf_op jit(solution)/shard_map/block_terms/pallas_call | solution.py:166
  9.3 3.0 %collective-permute-start.2 = (bf16[624,128]{1,0:T(8,128)(2,1)S(1)}, bf16[624,128]{1,0:T(8,128)(2,1)S(1)}, u32[]{:S(2)}, u32[]{:S(2)}) collective-permute-start(bf16[624,128]{1,0:T(8,128)(2,1)S(1)} %get-tuple-element.48), channel_id=1, source_target_pairs={{0,2},{2,0},{4,6},{6,4},{8,10},{10,8},{12,14},{14,12},{1,3},{3,1},... | collective-permute-start | bytes 479240 | tf_op jit(solution)/shard_map/ppermute | solution.py:473
  12.4 0.4 project.1
  12.8 0.0 collective-permute-start
  12.9 1.3 %collective-permute-done.other_ref.refs_6_ = f32[16,16,128]{2,1,0:T(8,128)S(1)} collective-permute-done((f32[16,16,128]{2,1,0:T(8,128)S(1)}, f32[16,16,128]{2,1,0:T(8,128)S(1)}, u32[]{:S(2)}, u32[]{:S(2)}) %collective-permute-start) | collective-permute-done | bytes 131104 | tf_op jit(solution)/shard_map/ppermute | solution.py:485
  14.2 0.2 edge_projections.1
  14.4 0.1 collective-permute-start.3
  14.5 2.0 %collective-permute-start.1 = (bf16[624,128]{1,0:T(8,128)(2,1)S(1)}, bf16[624,128]{1,0:T(8,128)(2,1)S(1)}, u32[]{:S(2)}, u32[]{:S(2)}) collective-permute-start(bf16[624,128]{1,0:T(8,128)(2,1)S(1)} %get-tuple-element.46), channel_id=1, source_target_pairs={{0,2},{2,0},{4,6},{6,4},{8,10},{10,8},{12,14},{14,12},{1,3},{3,1},... | collective-permute-start | bytes 479240 | tf_op jit(solution)/shard_map/ppermute | solution.py:473
  16.6 1.9 %collective-permute-start.5 = (bf16[624,128]{1,0:T(8,128)(2,1)S(1)}, bf16[624,128]{1,0:T(8,128)(2,1)S(1)}, u32[]{:S(2)}, u32[]{:S(2)}) collective-permute-start(bf16[624,128]{1,0:T(8,128)(2,1)S(1)} %get-tuple-element.58), channel_id=1, source_target_pairs={{0,2},{2,0},{4,6},{6,4},{8,10},{10,8},{12,14},{14,12},{1,3},{3,1},... | collective-permute-start | bytes 479240 | tf_op jit(solution)/shard_map/ppermute | solution.py:473
  18.5 3.3 %collective-permute-done.1 = bf16[624,128]{1,0:T(8,128)(2,1)S(1)} collective-permute-done((bf16[624,128]{1,0:T(8,128)(2,1)S(1)}, bf16[624,128]{1,0:T(8,128)(2,1)S(1)}, u32[]{:S(2)}, u32[]{:S(2)}) %collective-permute-start.1) | collective-permute-done | bytes 159776 | tf_op jit(solution)/shard_map/ppermute | solution.py:473
  21.8 1.8 %collective-permute-start.4 = (bf16[624,128]{1,0:T(8,128)(2,1)S(1)}, bf16[624,128]{1,0:T(8,128)(2,1)S(1)}, u32[]{:S(2)}, u32[]{:S(2)}) collective-permute-start(bf16[624,128]{1,0:T(8,128)(2,1)S(1)} %get-tuple-element.56), channel_id=1, source_target_pairs={{0,2},{2,0},{4,6},{6,4},{8,10},{10,8},{12,14},{14,12},{1,3},{3,1},... | collective-permute-start | bytes 479240 | tf_op jit(solution)/shard_map/ppermute | solution.py:473
  23.6 3.6 %collective-permute-start.6 = (bf16[624,128]{1,0:T(8,128)(2,1)S(1)}, bf16[624,128]{1,0:T(8,128)(2,1)S(1)}, u32[]{:S(2)}, u32[]{:S(2)}) collective-permute-start(bf16[624,128]{1,0:T(8,128)(2,1)S(1)} %add_convert_fusion.2), channel_id=1, source_target_pairs={{0,12},{2,14},{4,8},{6,10},{8,4},{10,6},{12,0},{14,2},{1,13},{3,15... | collective-permute-start | bytes 479240 | tf_op jit(solution)/shard_map/ppermute | solution.py:473
  27.3 0.8 %collective-permute-start.7 = (bf16[624,128]{1,0:T(8,128)(2,1)S(1)}, bf16[624,128]{1,0:T(8,128)(2,1)S(1)}, u32[]{:S(2)}, u32[]{:S(2)}) collective-permute-start(bf16[624,128]{1,0:T(8,128)(2,1)S(1)} %add_convert_fusion.1), channel_id=1, source_target_pairs={{0,8},{2,10},{4,12},{6,14},{8,0},{10,2},{12,4},{14,6},{1,9},{3,11}... | collective-permute-start | bytes 479240 | tf_op jit(solution)/shard_map/ppermute | solution.py:473
  28.1 1.6 %collective-permute-start.8 = (bf16[624,128]{1,0:T(8,128)(2,1)S(1)}, bf16[624,128]{1,0:T(8,128)(2,1)S(1)}, u32[]{:S(2)}, u32[]{:S(2)}) collective-permute-start(bf16[624,128]{1,0:T(8,128)(2,1)S(1)} %add_convert_fusion), channel_id=1, source_target_pairs={{0,4},{2,6},{4,0},{6,2},{8,12},{10,14},{12,8},{14,10},{1,5},{3,7},... | collective-permute-start | bytes 479240 | tf_op jit(solution)/shard_map/ppermute | solution.py:473
  29.7 0.4 collective-permute-start.12
  30.2 3.4 %collective-permute-start.11 = (f32[32,128]{1,0:T(8,128)S(1)}, f32[32,128]{1,0:T(8,128)S(1)}, u32[]{:S(2)}, u32[]{:S(2)}) collective-permute-start(f32[32,128]{1,0:T(8,128)S(1)} %collective-permute-done.3.refs_9_), channel_id=1, source_target_pairs={{0,12},{2,14},{4,8},{6,10},{8,4},{10,6},{12,0},{14,2},{1,13},{3,15... | collective-permute-start | bytes 49160 | tf_op jit(solution)/shard_map/ppermute | solution.py:473
  33.5 2.7 %collective-permute-done.12.refs_12_ = f32[32,128]{1,0:T(8,128)S(1)} collective-permute-done((f32[32,128]{1,0:T(8,128)S(1)}, f32[32,128]{1,0:T(8,128)S(1)}, u32[]{:S(2)}, u32[]{:S(2)}) %collective-permute-start.12) | collective-permute-done | bytes 16416 | tf_op jit(solution)/shard_map/ppermute | solution.py:473
  36.3 3.6 %collective-permute-start.9 = (f32[64,128]{1,0:T(8,128)S(1)}, f32[64,128]{1,0:T(8,128)S(1)}, u32[]{:S(2)}, u32[]{:S(2)}) collective-permute-start(f32[64,128]{1,0:T(8,128)S(1)} %get-tuple-element.65), channel_id=1, source_target_pairs={{0,8},{2,10},{4,12},{6,14},{8,0},{10,2},{12,4},{14,6},{1,9},{3,11}... | collective-permute-start | bytes 98312 | tf_op jit(solution)/shard_map/ppermute | solution.py:473
  39.9 1.5 %collective-permute-start.10 = (f32[32,128]{1,0:T(8,128)S(1)}, f32[32,128]{1,0:T(8,128)S(1)}, u32[]{:S(2)}, u32[]{:S(2)}) collective-permute-start(f32[32,128]{1,0:T(8,128)S(1)} %collective-permute-done.3.refs_9_), channel_id=1, source_target_pairs={{0,8},{2,10},{4,12},{6,14},{8,0},{10,2},{12,4},{14,6},{1,9},{3,11}... | collective-permute-start | bytes 49160 | tf_op jit(solution)/shard_map/ppermute | solution.py:473
  41.3 3.2 %collective-permute-done.10.refs_10_ = f32[32,128]{1,0:T(8,128)S(1)} collective-permute-done((f32[32,128]{1,0:T(8,128)S(1)}, f32[32,128]{1,0:T(8,128)S(1)}, u32[]{:S(2)}, u32[]{:S(2)}) %collective-permute-start.10) | collective-permute-done | bytes 16416 | tf_op jit(solution)/shard_map/ppermute | solution.py:473
  44.6 0.8 %statistics.1 = (bf16[256,128]{1,0:T(8,128)(2,1)S(1)}, bf16[256,128]{1,0:T(8,128)(2,1)S(1)}, f32[8,256]{1,0:T(8,128)S(1)}) custom-call(bf16[624,128]{1,0:T(8,128)(2,1)S(1)} %get-tuple-element.37.refs_0_, bf16[624,128]{1,0:T(8,128)(2,1)S(1)} %collective-permute-done.4.refs_1_, bf16[624,128]{1,0:T(8,128)(2,1)S(1)} %collective-permute-done.6.refs_2_, ...), custom_call_target="tpu_custom_call" | custom-call | tf_op jit(solution)/shard_map/statistics/pallas_call | solution.py:354
  45.3 0.5 %collective-permute-start.13 = (f32[8,256]{1,0:T(8,128)S(1)}, f32[8,256]{1,0:T(8,128)S(1)}, u32[]{:S(2)}, u32[]{:S(2)}) collective-permute-start(f32[8,256]{1,0:T(8,128)S(1)} %get-tuple-element.67.lag_ref), channel_id=1, source_target_pairs={{0,1},{1,0},{2,3},{3,2},{4,5},{5,4},{6,7},{7,6},{8,9},{9,8},{10,11... | collective-permute-start | bytes 24584 | tf_op jit(solution)/shard_map/ppermute | solution.py:522
  45.9 0.8 %collective-permute-done.13.lag_got_ref = f32[8,256]{1,0:T(8,128)S(1)} collective-permute-done((f32[8,256]{1,0:T(8,128)S(1)}, f32[8,256]{1,0:T(8,128)S(1)}, u32[]{:S(2)}, u32[]{:S(2)}) %collective-permute-start.13) | collective-permute-done | bytes 8224 | tf_op jit(solution)/shard_map/ppermute | solution.py:522
  46.7 2.8 %subtract.1 = (bf16[2,16,64,256]{3,2,1,0:T(8,128)(2,1)}, f32[2,33]{1,0:T(2,128)}) custom-call(f32[8,256]{1,0:T(8,128)S(1)} %get-tuple-element.67.lag_ref, f32[8,256]{1,0:T(8,128)S(1)} %collective-permute-done.13.lag_got_ref, f32[2,33]{1,0:T(2,128)S(1)} %bitcast.8, f32[2,80,256]{2,1,0:T(8,128)S(1)} %copy-done.1, ...), custom_call_target="tpu_custom_call" | custom-call | tf_op jit(solution)/shard_map/subtract/pallas_call | solution.py:439
  (20 shorter events, 0.2 us)
Async XLA Ops:
  0.6 11.7 %copy-start.1 = (f32[2,80,256]{2,1,0:T(8,128)S(1)}, f32[2,80,256]{2,1,0:T(8,128)}, u32[]{:S(2)}) copy-start(f32[2,80,256]{2,1,0:T(8,128)} %constant.2.clone.t_ref.refs_7_.table_ref) | copy-start | bytes 491524
  0.6 11.7 %copy-start = (bf16[1,1,32,64,256]{4,3,2,1,0:T(8,128)(2,1)S(1)}, bf16[1,1,32,64,256]{4,3,2,1,0:T(8,128)(2,1)}, u32[]{:S(2)}) copy-start(bf16[1,1,32,64,256]{4,3,2,1,0:T(8,128)(2,1)} %param.5) | copy-start | bytes 3145732
  0.7 46.0 %copy-start.2 = (f32[1,1,1,2,33]{4,3,2,1,0:T(2,128)S(1)}, f32[1,1,1,2,33]{4,3,2,1,0:T(2,128)}, u32[]{:S(2)}) copy-start(f32[1,1,1,2,33]{4,3,2,1,0:T(2,128)} %param.6) | copy-start | bytes 796
  9.3 7.2 %collective-permute-start.2 = (bf16[624,128]{1,0:T(8,128)(2,1)S(1)}, bf16[624,128]{1,0:T(8,128)(2,1)S(1)}, u32[]{:S(2)}, u32[]{:S(2)}) collective-permute-start(bf16[624,128]{1,0:T(8,128)(2,1)S(1)} %get-tuple-element.48), channel_id=1, source_target_pairs={{0,2},{2,0},{4,6},{6,4},{8,10},{10,8},{12,14},{14,12},{1,3},{3,1},... | collective-permute-start | bytes 479240 | tf_op jit(solution)/shard_map/ppermute | solution.py:473
  12.8 1.4 %collective-permute-start = (f32[16,16,128]{2,1,0:T(8,128)S(1)}, f32[16,16,128]{2,1,0:T(8,128)S(1)}, u32[]{:S(2)}, u32[]{:S(2)}) collective-permute-start(f32[16,16,128]{2,1,0:T(8,128)S(1)} %get-tuple-element.43), channel_id=1, source_target_pairs={{0,1},{1,0},{2,3},{3,2},{4,5},{5,4},{6,7},{7,6},{8,9},{9,8},{10,11... | collective-permute-start | bytes 393224 | tf_op jit(solution)/shard_map/ppermute | solution.py:485
  14.4 4.1 %collective-permute-start.3 = (f32[32,128]{1,0:T(8,128)S(1)}, f32[32,128]{1,0:T(8,128)S(1)}, u32[]{:S(2)}, u32[]{:S(2)}) collective-permute-start(f32[32,128]{1,0:T(8,128)S(1)} %get-tuple-element.51), channel_id=1, source_target_pairs={{0,2},{2,0},{4,6},{6,4},{8,10},{10,8},{12,14},{14,12},{1,3},{3,1},... | collective-permute-start | bytes 49160 | tf_op jit(solution)/shard_map/ppermute | solution.py:473
  14.5 7.3 %collective-permute-start.1 = (bf16[624,128]{1,0:T(8,128)(2,1)S(1)}, bf16[624,128]{1,0:T(8,128)(2,1)S(1)}, u32[]{:S(2)}, u32[]{:S(2)}) collective-permute-start(bf16[624,128]{1,0:T(8,128)(2,1)S(1)} %get-tuple-element.46), channel_id=1, source_target_pairs={{0,2},{2,0},{4,6},{6,4},{8,10},{10,8},{12,14},{14,12},{1,3},{3,1},... | collective-permute-start | bytes 479240 | tf_op jit(solution)/shard_map/ppermute | solution.py:473
  16.6 10.7 %collective-permute-start.5 = (bf16[624,128]{1,0:T(8,128)(2,1)S(1)}, bf16[624,128]{1,0:T(8,128)(2,1)S(1)}, u32[]{:S(2)}, u32[]{:S(2)}) collective-permute-start(bf16[624,128]{1,0:T(8,128)(2,1)S(1)} %get-tuple-element.58), channel_id=1, source_target_pairs={{0,2},{2,0},{4,6},{6,4},{8,10},{10,8},{12,14},{14,12},{1,3},{3,1},... | collective-permute-start | bytes 479240 | tf_op jit(solution)/shard_map/ppermute | solution.py:473
  21.8 6.2 %collective-permute-start.4 = (bf16[624,128]{1,0:T(8,128)(2,1)S(1)}, bf16[624,128]{1,0:T(8,128)(2,1)S(1)}, u32[]{:S(2)}, u32[]{:S(2)}) collective-permute-start(bf16[624,128]{1,0:T(8,128)(2,1)S(1)} %get-tuple-element.56), channel_id=1, source_target_pairs={{0,2},{2,0},{4,6},{6,4},{8,10},{10,8},{12,14},{14,12},{1,3},{3,1},... | collective-permute-start | bytes 479240 | tf_op jit(solution)/shard_map/ppermute | solution.py:473
  23.6 20.9 %collective-permute-start.6 = (bf16[624,128]{1,0:T(8,128)(2,1)S(1)}, bf16[624,128]{1,0:T(8,128)(2,1)S(1)}, u32[]{:S(2)}, u32[]{:S(2)}) collective-permute-start(bf16[624,128]{1,0:T(8,128)(2,1)S(1)} %add_convert_fusion.2), channel_id=1, source_target_pairs={{0,12},{2,14},{4,8},{6,10},{8,4},{10,6},{12,0},{14,2},{1,13},{3,15... | collective-permute-start | bytes 479240 | tf_op jit(solution)/shard_map/ppermute | solution.py:473
  27.3 17.3 %collective-permute-start.7 = (bf16[624,128]{1,0:T(8,128)(2,1)S(1)}, bf16[624,128]{1,0:T(8,128)(2,1)S(1)}, u32[]{:S(2)}, u32[]{:S(2)}) collective-permute-start(bf16[624,128]{1,0:T(8,128)(2,1)S(1)} %add_convert_fusion.1), channel_id=1, source_target_pairs={{0,8},{2,10},{4,12},{6,14},{8,0},{10,2},{12,4},{14,6},{1,9},{3,11}... | collective-permute-start | bytes 479240 | tf_op jit(solution)/shard_map/ppermute | solution.py:473
  28.1 16.5 %collective-permute-start.8 = (bf16[624,128]{1,0:T(8,128)(2,1)S(1)}, bf16[624,128]{1,0:T(8,128)(2,1)S(1)}, u32[]{:S(2)}, u32[]{:S(2)}) collective-permute-start(bf16[624,128]{1,0:T(8,128)(2,1)S(1)} %add_convert_fusion), channel_id=1, source_target_pairs={{0,4},{2,6},{4,0},{6,2},{8,12},{10,14},{12,8},{14,10},{1,5},{3,7},... | collective-permute-start | bytes 479240 | tf_op jit(solution)/shard_map/ppermute | solution.py:473
  29.7 6.6 %collective-permute-start.12 = (f32[32,128]{1,0:T(8,128)S(1)}, f32[32,128]{1,0:T(8,128)S(1)}, u32[]{:S(2)}, u32[]{:S(2)}) collective-permute-start(f32[32,128]{1,0:T(8,128)S(1)} %collective-permute-done.3.refs_9_), channel_id=1, source_target_pairs={{0,4},{2,6},{4,0},{6,2},{8,12},{10,14},{12,8},{14,10},{1,5},{3,7},... | collective-permute-start | bytes 49160 | tf_op jit(solution)/shard_map/ppermute | solution.py:473
  30.2 9.7 %collective-permute-start.11 = (f32[32,128]{1,0:T(8,128)S(1)}, f32[32,128]{1,0:T(8,128)S(1)}, u32[]{:S(2)}, u32[]{:S(2)}) collective-permute-start(f32[32,128]{1,0:T(8,128)S(1)} %collective-permute-done.3.refs_9_), channel_id=1, source_target_pairs={{0,12},{2,14},{4,8},{6,10},{8,4},{10,6},{12,0},{14,2},{1,13},{3,15... | collective-permute-start | bytes 49160 | tf_op jit(solution)/shard_map/ppermute | solution.py:473
  36.3 8.3 %collective-permute-start.9 = (f32[64,128]{1,0:T(8,128)S(1)}, f32[64,128]{1,0:T(8,128)S(1)}, u32[]{:S(2)}, u32[]{:S(2)}) collective-permute-start(f32[64,128]{1,0:T(8,128)S(1)} %get-tuple-element.65), channel_id=1, source_target_pairs={{0,8},{2,10},{4,12},{6,14},{8,0},{10,2},{12,4},{14,6},{1,9},{3,11}... | collective-permute-start | bytes 98312 | tf_op jit(solution)/shard_map/ppermute | solution.py:473
  39.9 4.6 %collective-permute-start.10 = (f32[32,128]{1,0:T(8,128)S(1)}, f32[32,128]{1,0:T(8,128)S(1)}, u32[]{:S(2)}, u32[]{:S(2)}) collective-permute-start(f32[32,128]{1,0:T(8,128)S(1)} %collective-permute-done.3.refs_9_), channel_id=1, source_target_pairs={{0,8},{2,10},{4,12},{6,14},{8,0},{10,2},{12,4},{14,6},{1,9},{3,11}... | collective-permute-start | bytes 49160 | tf_op jit(solution)/shard_map/ppermute | solution.py:473
  45.3 1.4 %collective-permute-start.14 = (bf16[256,128]{1,0:T(8,128)(2,1)S(1)}, bf16[256,128]{1,0:T(8,128)(2,1)S(1)}, u32[]{:S(2)}, u32[]{:S(2)}) collective-permute-start(bf16[256,128]{1,0:T(8,128)(2,1)S(1)} %get-tuple-element.69), channel_id=1, source_target_pairs={{0,1},{1,0},{2,3},{3,2},{4,5},{5,4},{6,7},{7,6},{8,9},{9,8},{10,11... | collective-permute-start | bytes 196616 | tf_op jit(solution)/shard_map/ppermute | solution.py:521
  45.3 1.4 %collective-permute-start.13 = (f32[8,256]{1,0:T(8,128)S(1)}, f32[8,256]{1,0:T(8,128)S(1)}, u32[]{:S(2)}, u32[]{:S(2)}) collective-permute-start(f32[8,256]{1,0:T(8,128)S(1)} %get-tuple-element.67.lag_ref), channel_id=1, source_target_pairs={{0,1},{1,0},{2,3},{3,2},{4,5},{5,4},{6,7},{7,6},{8,9},{9,8},{10,11... | collective-permute-start | bytes 24584 | tf_op jit(solution)/shard_map/ppermute | solution.py:522

commit v3 on v2

--- a/solution.py
+++ b/solution.py
@@ -153,9 +153,13 @@
         out[...] = blocks[((me ^ k) + 2) % refl]
 
 
+def far_places(refl):
+    return list(range(4, refl, 2))
+
+
 def parcels(refl):
-    places = list(range(refl - 2, -1, -2))
-    return [k ^ 1 for k in places] + places
+    far = far_places(refl)
+    return [k ^ 1 for k in far] + far + [0, 1, 2, 3]
 
 
 def block_terms(spectra, rows):
@@ -259,12 +263,13 @@
 
 def statistics_kernel(rows, *refs):
     nb = len(band_rows(0, rows))
-    count = rows * COLS // 2 + 1
+    count = rows * COLS // 2 + 2
     blocks, refs = refs[:count], refs[count:]
     keep_ref, other_ref, lags_ref = refs[:3]
-    bands, refs = refs[3 : 3 + nb], refs[3 + nb :]
-    nears, refs = refs[: 1 + nb], refs[1 + nb :]
-    fars, refs = refs[: 1 + nb], refs[1 + nb :]
+    rims = [x[...] for x in refs[3 : 3 + nb * 3 + 2]]
+    bands, nears, fars = rims[:nb], rims[nb : 2 * nb + 1], rims[2 * nb + 1 :]
+    refs = refs[3 + nb * 3 + 2 :]
+    bands = [x.astype(F32) for x in bands]
     own_ref, send_ref, lag_ref, spectrum = refs
     j = lax.axis_index("freq")
     p, c = grid_place(rows)
@@ -304,7 +309,7 @@
     sub = lax.broadcasted_iota(jnp.int32, (HF, 8, LANES), 1)
     for n in range(nb):
         x = summed(2 * HF * WC + n * 64, 64).reshape(HF, 8, LANES)
-        q = bands[n][...].reshape(HF, 8, LANES)
+        q = bands[n].reshape(HF, 8, LANES)
         partner = jnp.where(sub < WM, -1.0, 1.0) * pltpu.roll(q, WM, 1)
         here_sums = [jnp.sum(x * y, 1) for y in (x, q, partner)]
         total = here_sums if total is None else [a + b for a, b in zip(total, here_sums)]
@@ -329,7 +334,8 @@
     from_near = ((l48 % 8) < WM) == ((c % 2) == 1)
     q = []
     for sides in (nears, fars):
-        pieces = [sides[0][...]]
+        sides = [x.astype(F32) for x in sides]
+        pieces = [sides[0]]
         for n, side in enumerate(sides[1:]):
             top, bottom = side[:WM, :], side[WC - WM :, :]
             pieces.append(jnp.where(p == 0, top, bottom) if nb == 1 else (bottom, top)[n])
@@ -429,7 +435,7 @@
 
 
 def subtract(lag, lag_got, start, table, own, got, recorded):
-    steps = 4
+    steps = 2
     half = WC // 2
     each = half // steps
     recorded = recorded.reshape(2, half, 64, NT)
@@ -477,32 +483,34 @@
 
     after = lax.optimization_barrier
     blocks = block_terms(spectra, rows)
-    pairs = refl // 2
-    sent, kept = list(blocks[:pairs]), blocks[pairs:]
+    far = far_places(refl)
+    sent, kept, close = list(blocks[: len(far)]), blocks[len(far) : -4], blocks[-4:]
     came = [swap(sent[0], 1)]
     tile, sent[1] = after((recorded[0, 0], sent[1]))
     keep, send = project(tile, table)
     other = lax.ppermute(send, "freq", core_swap)
     *bands, sides = edge_projections(keep, other, rows)
-    sent[1], sides, *bands = after((sent[1], sides, *bands))
-    came.append(swap(sent[1], 1))
+    extra = {}
     if rows == 2:
         near = swap(sides, 1)
-    got = []
-    for n, k in enumerate(range(refl - 2, 0, -2)):
-        total = add(kept[n], came[n])
-        if n + 2 < pairs:
-            total, sent[n + 2] = after((total, sent[n + 2]))
-            came.append(swap(sent[n + 2], 1))
-        if rows == 2 and n == 0:
-            total, near, bands[0] = after((total, near, bands[0]))
-        came[n + 1], total = after((came[n + 1], total))
-        got.append(swap(total, k))
-        if rows == 2 and n == 1:
-            bands = [swap(bands[0], k)]
-    got = [kept[-1], came[-1]] + got
+        extra = {6: [near], 4: [bands[0], near], 2: [near]}
+
+    def parcel(block, k):
+        return jnp.concatenate([block] + [x.astype(BF16) for x in extra.get(k, [])])
+
+    totals = [parcel(add(kept[0], came[0]), far[0])]
+    totals[0], *sent[1:] = after((totals[0], *sent[1:]))
+    came += [swap(x, 1) for x in sent[1:]]
+    totals += [parcel(add(kept[n], came[n]), far[n]) for n in range(1, len(far))]
+    got = [swap(x, k) for x, k in zip(totals, far)]
+    own, *close = close
+    (close[0], close[2]), _ = after(((close[0], close[2]), totals[1]))
+    close[1], _ = after((close[1], totals[0]))
+    close = [swap(parcel(x, k), k) for k, x in enumerate(close, 1)]
+    size = own.shape[0]
     if rows == 2:
-        nears, fars = [near, swap(near, 4)], [swap(near, 6), swap(near, 2)]
+        bands = [got[0][size : size + 64]]
+        nears, fars = [near, got[0][size + 64 :]], [got[1][size:], close[1][size:]]
     else:
 
         def shift(x, rise, across):
@@ -517,7 +525,7 @@
         bands = [shift(x, rise, (0, 1, 2, 3)) for x, rise in zip(bands, (1, -1))]
         nears = [shift(sides, rise, (1, 0, 3, 2)) for rise in (0, 1, -1)]
         fars = [shift(sides, rise, (None, 2, 1, None)) for rise in (0, 1, -1)]
-    own, away, lag = statistics(got, keep, other, table, bands, nears, fars, rows)
+    own, away, lag = statistics([own] + got + close, keep, other, table, bands, nears, fars, rows)
     away_got = lax.ppermute(away, "freq", core_swap)
     lag_got = lax.ppermute(lag, "freq", core_swap)
     clean, filters = subtract(

time: 49.7 us -> 43.2 us (0.87)
  starting transfers between devices: 24.3 us -> 13.1 us
  waiting for transfers between devices: 11.4 us -> 16.8 us
  Pallas kernels: 12.9 us -> 12.2 us
    ppermute x12 -> x8, starting transfers between devices: 23.8 us -> 12.5 us  [swap(): return lax.ppermute(x, 'refl', [(i, i ^ k) for i in range(refl)])]
    ppermute x12 -> x8, waiting for transfers between devices: 9.23 us -> 14.6 us  [swap(): return lax.ppermute(x, 'refl', [(i, i ^ k) for i in range(refl)])]
    pallas_call x1, Pallas kernels: 2.83 us -> 2.11 us  [subtract(): pl.pallas_call(functools.partial(subtract_kernel, steps), grid=(steps,),...]
  transfers between devices with their start and end apart: 15 -> 11, of which waited for: 5 -> 7; matrix products, arithmetic and copies ran while one was open for 0% -> 0% of each run, Pallas kernels for 1% -> 2%
where the time goes in v3:
time: 43.2 us; the launch traced here: 43 us
  waiting for transfers between devices  16.8 us (39%)
  starting transfers between devices  13.1 us (30%)
  Pallas kernels  12.2 us (28%)
  between operations  0.71 us (2%)
    ppermute x8, waiting for transfers between devices, swap(): return lax.ppermute(x, 'refl', [(i, i ^ k) for i in range(refl)])  14.6 us
    ppermute x8, starting transfers between devices, swap(): return lax.ppermute(x, 'refl', [(i, i ^ k) for i in range(refl)])  12.5 us
    pallas_call x1, Pallas kernels, block_terms(): pl.pallas_call(functools.partial(terms_kernel, rows), in_specs=[pl.BlockS...  8.64 us
    pallas_call x1, Pallas kernels, subtract(): pl.pallas_call(functools.partial(subtract_kernel, steps), grid=(steps,),...  2.11 us
    ppermute x1, waiting for transfers between devices, body(): other = lax.ppermute(send, 'freq', core_swap)  1.33 us
  transfers between devices with their start and end apart: 11, of which 7 were waited for; matrix products, arithmetic and copies ran while one was open for 0% of the time, Pallas kernels for 2%

profile of v3, /device:TPU:0, one launch (start us, length us, event | category | flops | bytes accessed | tf_op | source)
XLA Modules:
  0.0 43.0 jit_solution(11494752846302112775)
XLA Ops:
  0.6 0.0 copy-start.1
  0.7 8.6 %block_terms.1 = (bf16[624,128]{1,0:T(8,128)(2,1)S(1)}, bf16[624,128]{1,0:T(8,128)(2,1)S(1)}, bf16[624,128]{1,0:T(8,128)(2,1)S(1)}, bf16[624,128]{1,0:T(8,128)(2...) custom-call(bf16[2,8,512,1024]{3,2,1,0:T(8,128)(2,1)} %s_hbm.1), custom_call_target="tpu_custom_call" | custom-call | tf_op jit(solution)/shard_map/block_terms/pallas_call | solution.py:170
  9.3 3.0 %collective-permute-start = (bf16[624,128]{1,0:T(8,128)(2,1)S(1)}, bf16[624,128]{1,0:T(8,128)(2,1)S(1)}, u32[]{:S(2)}, u32[]{:S(2)}) collective-permute-start(bf16[624,128]{1,0:T(8,128)(2,1)S(1)} %get-tuple-element.28), channel_id=1, source_target_pairs={{0,2},{2,0},{4,6},{6,4},{8,10},{10,8},{12,14},{14,12},{1,3},{3,1},... | collective-permute-start | bytes 479240 | tf_op jit(solution)/shard_map/ppermute | solution.py:479
  12.4 0.4 %project.1 = (f32[16,16,128]{2,1,0:T(8,128)S(1)}, f32[16,16,128]{2,1,0:T(8,128)S(1)}) custom-call(bf16[32,64,256]{2,1,0:T(8,128)(2,1)S(1)} %bitcast.5, f32[2,80,256]{2,1,0:T(8,128)S(1)} %copy-done.1), custom_call_target="tpu_custom_call" | custom-call | tf_op jit(solution)/shard_map/project/pallas_call | solution.py:199
  12.8 0.0 collective-permute-start.1
  12.9 1.3 %collective-permute-done.1.other_ref.refs_7_ = f32[16,16,128]{2,1,0:T(8,128)S(1)} collective-permute-done((f32[16,16,128]{2,1,0:T(8,128)S(1)}, f32[16,16,128]{2,1,0:T(8,128)S(1)}, u32[]{:S(2)}, u32[]{:S(2)}) %collective-permute-start.1) | collective-permute-done | bytes 131104 | tf_op jit(solution)/shard_map/ppermute | solution.py:491
  14.2 0.2 edge_projections.1
  14.4 0.1 collective-permute-start.2
  14.5 3.7 %collective-permute-done.2.refs_10_ = f32[32,128]{1,0:T(8,128)S(1)} collective-permute-done((f32[32,128]{1,0:T(8,128)S(1)}, f32[32,128]{1,0:T(8,128)S(1)}, u32[]{:S(2)}, u32[]{:S(2)}) %collective-permute-start.2) | collective-permute-done | bytes 16416 | tf_op jit(solution)/shard_map/ppermute | solution.py:479
  18.3 0.4 collective-permute-start.4
  18.7 2.8 %collective-permute-start.3 = (bf16[720,128]{1,0:T(8,128)(2,1)S(1)}, bf16[720,128]{1,0:T(8,128)(2,1)S(1)}, u32[]{:S(2)}, u32[]{:S(2)}) collective-permute-start(bf16[720,128]{1,0:T(8,128)(2,1)S(1)} %pad_maximum_fusion.2), channel_id=1, source_target_pairs={{0,8},{2,10},{4,12},{6,14},{8,0},{10,2},{12,4},{14,6},{1,9},{3,11}... | collective-permute-start | bytes 552968 | tf_op jit(solution)/shard_map/ppermute | solution.py:479
  21.5 2.2 %collective-permute-done.4 = bf16[624,128]{1,0:T(8,128)(2,1)S(1)} collective-permute-done((bf16[624,128]{1,0:T(8,128)(2,1)S(1)}, bf16[624,128]{1,0:T(8,128)(2,1)S(1)}, u32[]{:S(2)}, u32[]{:S(2)}) %collective-permute-start.4) | collective-permute-done | bytes 159776 | tf_op jit(solution)/shard_map/ppermute | solution.py:479
  23.7 1.6 %collective-permute-start.7 = (bf16[656,128]{1,0:T(8,128)(2,1)S(1)}, bf16[656,128]{1,0:T(8,128)(2,1)S(1)}, u32[]{:S(2)}, u32[]{:S(2)}) collective-permute-start(bf16[656,128]{1,0:T(8,128)(2,1)S(1)} %get-tuple-element.50), channel_id=1, source_target_pairs={{0,4},{2,6},{4,0},{6,2},{8,12},{10,14},{12,8},{14,10},{1,5},{3,7},... | collective-permute-start | bytes 503816 | tf_op jit(solution)/shard_map/ppermute | solution.py:479
  25.4 2.5 %collective-permute-start.5 = (bf16[656,128]{1,0:T(8,128)(2,1)S(1)}, bf16[656,128]{1,0:T(8,128)(2,1)S(1)}, u32[]{:S(2)}, u32[]{:S(2)}) collective-permute-start(bf16[656,128]{1,0:T(8,128)(2,1)S(1)} %get-tuple-element.51), channel_id=1, source_target_pairs={{0,12},{2,14},{4,8},{6,10},{8,4},{10,6},{12,0},{14,2},{1,13},{3,15... | collective-permute-start | bytes 503816 | tf_op jit(solution)/shard_map/ppermute | solution.py:479
  27.9 0.8 %collective-permute-start.6 = (bf16[624,128]{1,0:T(8,128)(2,1)S(1)}, bf16[624,128]{1,0:T(8,128)(2,1)S(1)}, u32[]{:S(2)}, u32[]{:S(2)}) collective-permute-start(bf16[624,128]{1,0:T(8,128)(2,1)S(1)} %get-tuple-element.41), channel_id=1, source_target_pairs={{0,2},{2,0},{4,6},{6,4},{8,10},{10,8},{12,14},{14,12},{1,3},{3,1},... | collective-permute-start | bytes 479240 | tf_op jit(solution)/shard_map/ppermute | solution.py:479
  28.6 1.4 %collective-permute-start.8 = (bf16[624,128]{1,0:T(8,128)(2,1)S(1)}, bf16[624,128]{1,0:T(8,128)(2,1)S(1)}, u32[]{:S(2)}, u32[]{:S(2)}) collective-permute-start(bf16[624,128]{1,0:T(8,128)(2,1)S(1)} %get-tuple-element.44), channel_id=1, source_target_pairs={{0,6},{2,4},{4,2},{6,0},{8,14},{10,12},{12,10},{14,8},{1,7},{3,5},... | collective-permute-start | bytes 479240 | tf_op jit(solution)/shard_map/ppermute | solution.py:479
  30.0 2.5 %collective-permute-done.3.refs_1_ = bf16[720,128]{1,0:T(8,128)(2,1)S(1)} collective-permute-done((bf16[720,128]{1,0:T(8,128)(2,1)S(1)}, bf16[720,128]{1,0:T(8,128)(2,1)S(1)}, u32[]{:S(2)}, u32[]{:S(2)}) %collective-permute-start.3) | collective-permute-done | bytes 184352 | tf_op jit(solution)/shard_map/ppermute | solution.py:479
  32.5 4.0 %collective-permute-done.7.refs_4_ = bf16[656,128]{1,0:T(8,128)(2,1)S(1)} collective-permute-done((bf16[656,128]{1,0:T(8,128)(2,1)S(1)}, bf16[656,128]{1,0:T(8,128)(2,1)S(1)}, u32[]{:S(2)}, u32[]{:S(2)}) %collective-permute-start.7) | collective-permute-done | bytes 167968 | tf_op jit(solution)/shard_map/ppermute | solution.py:479
  36.5 2.3 %collective-permute-done.8.refs_5_ = bf16[624,128]{1,0:T(8,128)(2,1)S(1)} collective-permute-done((bf16[624,128]{1,0:T(8,128)(2,1)S(1)}, bf16[624,128]{1,0:T(8,128)(2,1)S(1)}, u32[]{:S(2)}, u32[]{:S(2)}) %collective-permute-start.8) | collective-permute-done | bytes 159776 | tf_op jit(solution)/shard_map/ppermute | solution.py:479
  38.8 0.8 %statistics.1 = (bf16[256,128]{1,0:T(8,128)(2,1)S(1)}, bf16[256,128]{1,0:T(8,128)(2,1)S(1)}, f32[8,256]{1,0:T(8,128)S(1)}) custom-call(bf16[624,128]{1,0:T(8,128)(2,1)S(1)} %get-tuple-element.26.refs_0_, bf16[720,128]{1,0:T(8,128)(2,1)S(1)} %collective-permute-done.3.refs_1_, bf16[656,128]{1,0:T(8,128)(2,1)S(1)} %collective-permute-done.5.refs_2_, ...), custom_call_target="tpu_custom_call" | custom-call | tf_op jit(solution)/shard_map/statistics/pallas_call | solution.py:360
  39.6 0.5 %collective-permute-start.9 = (f32[8,256]{1,0:T(8,128)S(1)}, f32[8,256]{1,0:T(8,128)S(1)}, u32[]{:S(2)}, u32[]{:S(2)}) collective-permute-start(f32[8,256]{1,0:T(8,128)S(1)} %get-tuple-element.45.lag_ref), channel_id=1, source_target_pairs={{0,1},{1,0},{2,3},{3,2},{4,5},{5,4},{6,7},{7,6},{8,9},{9,8},{10,11... | collective-permute-start | bytes 24584 | tf_op jit(solution)/shard_map/ppermute | solution.py:530
  40.1 0.8 %collective-permute-done.9.lag_got_ref = f32[8,256]{1,0:T(8,128)S(1)} collective-permute-done((f32[8,256]{1,0:T(8,128)S(1)}, f32[8,256]{1,0:T(8,128)S(1)}, u32[]{:S(2)}, u32[]{:S(2)}) %collective-permute-start.9) | collective-permute-done | bytes 8224 | tf_op jit(solution)/shard_map/ppermute | solution.py:530
  40.9 0.0 collective-permute-done.10.got_ref
  40.9 2.1 %subtract.1 = (bf16[2,16,64,256]{3,2,1,0:T(8,128)(2,1)}, f32[2,33]{1,0:T(2,128)}) custom-call(f32[8,256]{1,0:T(8,128)S(1)} %get-tuple-element.45.lag_ref, f32[8,256]{1,0:T(8,128)S(1)} %collective-permute-done.9.lag_got_ref, f32[2,33]{1,0:T(2,128)S(1)} %bitcast.8, f32[2,80,256]{2,1,0:T(8,128)S(1)} %copy-done.1, ...), custom_call_target="tpu_custom_call" | custom-call | tf_op jit(solution)/shard_map/subtract/pallas_call | solution.py:445
  (19 shorter events, 0.2 us)
Async XLA Ops:
  0.6 11.7 %copy-start.1 = (f32[2,80,256]{2,1,0:T(8,128)S(1)}, f32[2,80,256]{2,1,0:T(8,128)}, u32[]{:S(2)}) copy-start(f32[2,80,256]{2,1,0:T(8,128)} %constant.2.clone.t_ref.refs_8_.table_ref) | copy-start | bytes 491524
  0.6 11.7 %copy-start = (bf16[1,1,32,64,256]{4,3,2,1,0:T(8,128)(2,1)S(1)}, bf16[1,1,32,64,256]{4,3,2,1,0:T(8,128)(2,1)}, u32[]{:S(2)}) copy-start(bf16[1,1,32,64,256]{4,3,2,1,0:T(8,128)(2,1)} %param.5) | copy-start | bytes 3145732
  0.7 40.3 %copy-start.2 = (f32[1,1,1,2,33]{4,3,2,1,0:T(2,128)S(1)}, f32[1,1,1,2,33]{4,3,2,1,0:T(2,128)}, u32[]{:S(2)}) copy-start(f32[1,1,1,2,33]{4,3,2,1,0:T(2,128)} %param.6) | copy-start | bytes 796
  9.3 8.9 %collective-permute-start = (bf16[624,128]{1,0:T(8,128)(2,1)S(1)}, bf16[624,128]{1,0:T(8,128)(2,1)S(1)}, u32[]{:S(2)}, u32[]{:S(2)}) collective-permute-start(bf16[624,128]{1,0:T(8,128)(2,1)S(1)} %get-tuple-element.28), channel_id=1, source_target_pairs={{0,2},{2,0},{4,6},{6,4},{8,10},{10,8},{12,14},{14,12},{1,3},{3,1},... | collective-permute-start | bytes 479240 | tf_op jit(solution)/shard_map/ppermute | solution.py:479
  12.8 1.4 %collective-permute-start.1 = (f32[16,16,128]{2,1,0:T(8,128)S(1)}, f32[16,16,128]{2,1,0:T(8,128)S(1)}, u32[]{:S(2)}, u32[]{:S(2)}) collective-permute-start(f32[16,16,128]{2,1,0:T(8,128)S(1)} %get-tuple-element.32), channel_id=1, source_target_pairs={{0,1},{1,0},{2,3},{3,2},{4,5},{5,4},{6,7},{7,6},{8,9},{9,8},{10,11... | collective-permute-start | bytes 393224 | tf_op jit(solution)/shard_map/ppermute | solution.py:491
  14.4 3.8 %collective-permute-start.2 = (f32[32,128]{1,0:T(8,128)S(1)}, f32[32,128]{1,0:T(8,128)S(1)}, u32[]{:S(2)}, u32[]{:S(2)}) collective-permute-start(f32[32,128]{1,0:T(8,128)S(1)} %get-tuple-element.34), channel_id=1, source_target_pairs={{0,2},{2,0},{4,6},{6,4},{8,10},{10,8},{12,14},{14,12},{1,3},{3,1},... | collective-permute-start | bytes 49160 | tf_op jit(solution)/shard_map/ppermute | solution.py:479
  18.3 5.3 %collective-permute-start.4 = (bf16[624,128]{1,0:T(8,128)(2,1)S(1)}, bf16[624,128]{1,0:T(8,128)(2,1)S(1)}, u32[]{:S(2)}, u32[]{:S(2)}) collective-permute-start(bf16[624,128]{1,0:T(8,128)(2,1)S(1)} %get-tuple-element.38), channel_id=1, source_target_pairs={{0,2},{2,0},{4,6},{6,4},{8,10},{10,8},{12,14},{14,12},{1,3},{3,1},... | collective-permute-start | bytes 479240 | tf_op jit(solution)/shard_map/ppermute | solution.py:479
  18.7 13.8 %collective-permute-start.3 = (bf16[720,128]{1,0:T(8,128)(2,1)S(1)}, bf16[720,128]{1,0:T(8,128)(2,1)S(1)}, u32[]{:S(2)}, u32[]{:S(2)}) collective-permute-start(bf16[720,128]{1,0:T(8,128)(2,1)S(1)} %pad_maximum_fusion.2), channel_id=1, source_target_pairs={{0,8},{2,10},{4,12},{6,14},{8,0},{10,2},{12,4},{14,6},{1,9},{3,11}... | collective-permute-start | bytes 552968 | tf_op jit(solution)/shard_map/ppermute | solution.py:479
  23.7 12.7 %collective-permute-start.7 = (bf16[656,128]{1,0:T(8,128)(2,1)S(1)}, bf16[656,128]{1,0:T(8,128)(2,1)S(1)}, u32[]{:S(2)}, u32[]{:S(2)}) collective-permute-start(bf16[656,128]{1,0:T(8,128)(2,1)S(1)} %get-tuple-element.50), channel_id=1, source_target_pairs={{0,4},{2,6},{4,0},{6,2},{8,12},{10,14},{12,8},{14,10},{1,5},{3,7},... | collective-permute-start | bytes 503816 | tf_op jit(solution)/shard_map/ppermute | solution.py:479
  25.4 11.1 %collective-permute-start.5 = (bf16[656,128]{1,0:T(8,128)(2,1)S(1)}, bf16[656,128]{1,0:T(8,128)(2,1)S(1)}, u32[]{:S(2)}, u32[]{:S(2)}) collective-permute-start(bf16[656,128]{1,0:T(8,128)(2,1)S(1)} %get-tuple-element.51), channel_id=1, source_target_pairs={{0,12},{2,14},{4,8},{6,10},{8,4},{10,6},{12,0},{14,2},{1,13},{3,15... | collective-permute-start | bytes 503816 | tf_op jit(solution)/shard_map/ppermute | solution.py:479
  27.9 8.6 %collective-permute-start.6 = (bf16[624,128]{1,0:T(8,128)(2,1)S(1)}, bf16[624,128]{1,0:T(8,128)(2,1)S(1)}, u32[]{:S(2)}, u32[]{:S(2)}) collective-permute-start(bf16[624,128]{1,0:T(8,128)(2,1)S(1)} %get-tuple-element.41), channel_id=1, source_target_pairs={{0,2},{2,0},{4,6},{6,4},{8,10},{10,8},{12,14},{14,12},{1,3},{3,1},... | collective-permute-start | bytes 479240 | tf_op jit(solution)/shard_map/ppermute | solution.py:479
  28.6 10.1 %collective-permute-start.8 = (bf16[624,128]{1,0:T(8,128)(2,1)S(1)}, bf16[624,128]{1,0:T(8,128)(2,1)S(1)}, u32[]{:S(2)}, u32[]{:S(2)}) collective-permute-start(bf16[624,128]{1,0:T(8,128)(2,1)S(1)} %get-tuple-element.44), channel_id=1, source_target_pairs={{0,6},{2,4},{4,2},{6,0},{8,14},{10,12},{12,10},{14,8},{1,7},{3,5},... | collective-permute-start | bytes 479240 | tf_op jit(solution)/shard_map/ppermute | solution.py:479
  39.6 1.4 %collective-permute-start.10 = (bf16[256,128]{1,0:T(8,128)(2,1)S(1)}, bf16[256,128]{1,0:T(8,128)(2,1)S(1)}, u32[]{:S(2)}, u32[]{:S(2)}) collective-permute-start(bf16[256,128]{1,0:T(8,128)(2,1)S(1)} %get-tuple-element.47), channel_id=1, source_target_pairs={{0,1},{1,0},{2,3},{3,2},{4,5},{5,4},{6,7},{7,6},{8,9},{9,8},{10,11... | collective-permute-start | bytes 196616 | tf_op jit(solution)/shard_map/ppermute | solution.py:529
  39.6 1.4 %collective-permute-start.9 = (f32[8,256]{1,0:T(8,128)S(1)}, f32[8,256]{1,0:T(8,128)S(1)}, u32[]{:S(2)}, u32[]{:S(2)}) collective-permute-start(f32[8,256]{1,0:T(8,128)S(1)} %get-tuple-element.45.lag_ref), channel_id=1, source_target_pairs={{0,1},{1,0},{2,3},{3,2},{4,5},{5,4},{6,7},{7,6},{8,9},{9,8},{10,11... | collective-permute-start | bytes 24584 | tf_op jit(solution)/shard_map/ppermute | solution.py:530

commit v4 on v3

--- a/solution.py
+++ b/solution.py
@@ -493,7 +493,7 @@
     extra = {}
     if rows == 2:
         near = swap(sides, 1)
-        extra = {6: [near], 4: [bands[0], near], 2: [near]}
+        extra = {6: [near], 4: [bands[0], near], 3: [sides]}
 
     def parcel(block, k):
         return jnp.concatenate([block] + [x.astype(BF16) for x in extra.get(k, [])])
@@ -504,13 +504,13 @@
     totals += [parcel(add(kept[n], came[n]), far[n]) for n in range(1, len(far))]
     got = [swap(x, k) for x, k in zip(totals, far)]
     own, *close = close
-    (close[0], close[2]), _ = after(((close[0], close[2]), totals[1]))
-    close[1], _ = after((close[1], totals[0]))
+    (close[0], close[1]), _ = after(((close[0], close[1]), totals[1]))
+    close[2], _ = after((close[2], totals[0]))
     close = [swap(parcel(x, k), k) for k, x in enumerate(close, 1)]
     size = own.shape[0]
     if rows == 2:
         bands = [got[0][size : size + 64]]
-        nears, fars = [near, got[0][size + 64 :]], [got[1][size:], close[1][size:]]
+        nears, fars = [near, got[0][size + 64 :]], [got[1][size:], close[2][size:]]
     else:
 
         def shift(x, rise, across):

time: 43.2 us -> 41.7 us (0.965)
  waiting for transfers between devices: 16.8 us -> 12 us
  starting transfers between devices: 13.1 us -> 16.5 us
    ppermute x8, waiting for transfers between devices: 14.6 us -> 9.8 us  [swap(): return lax.ppermute(x, 'refl', [(i, i ^ k) for i in range(refl)])]
    ppermute x8, starting transfers between devices: 12.5 us -> 15.9 us  [swap(): return lax.ppermute(x, 'refl', [(i, i ^ k) for i in range(refl)])]
where the time goes in v4:
time: 41.7 us; the launch traced here: 41.6 us
  starting transfers between devices  16.5 us (40%)
  Pallas kernels  12.2 us (29%)
  waiting for transfers between devices  12 us (29%)
  between operations  0.73 us (2%)
    ppermute x8, starting transfers between devices, swap(): return lax.ppermute(x, 'refl', [(i, i ^ k) for i in range(refl)])  15.9 us
    ppermute x8, waiting for transfers between devices, swap(): return lax.ppermute(x, 'refl', [(i, i ^ k) for i in range(refl)])  9.8 us
    pallas_call x1, Pallas kernels, block_terms(): pl.pallas_call(functools.partial(terms_kernel, rows), in_specs=[pl.BlockS...  8.64 us
    pallas_call x1, Pallas kernels, subtract(): pl.pallas_call(functools.partial(subtract_kernel, steps), grid=(steps,),...  2.11 us
    ppermute x1, waiting for transfers between devices, body(): other = lax.ppermute(send, 'freq', core_swap)  1.33 us
  transfers between devices with their start and end apart: 11, of which 7 were waited for; matrix products, arithmetic and copies ran while one was open for 0% of the time, Pallas kernels for 2%

profile of v4, /device:TPU:0, one launch (start us, length us, event | category | flops | bytes accessed | tf_op | source)
XLA Modules:
  0.0 41.6 jit_solution(102357185643401825)
XLA Ops:
  0.6 0.0 copy-start.1
  0.7 8.6 %block_terms.1 = (bf16[624,128]{1,0:T(8,128)(2,1)S(1)}, bf16[624,128]{1,0:T(8,128)(2,1)S(1)}, bf16[624,128]{1,0:T(8,128)(2,1)S(1)}, bf16[624,128]{1,0:T(8,128)(2...) custom-call(bf16[2,8,512,1024]{3,2,1,0:T(8,128)(2,1)} %s_hbm.1), custom_call_target="tpu_custom_call" | custom-call | tf_op jit(solution)/shard_map/block_terms/pallas_call | solution.py:170
  9.3 3.0 %collective-permute-start = (bf16[624,128]{1,0:T(8,128)(2,1)S(1)}, bf16[624,128]{1,0:T(8,128)(2,1)S(1)}, u32[]{:S(2)}, u32[]{:S(2)}) collective-permute-start(bf16[624,128]{1,0:T(8,128)(2,1)S(1)} %get-tuple-element.28), channel_id=1, source_target_pairs={{0,2},{2,0},{4,6},{6,4},{8,10},{10,8},{12,14},{14,12},{1,3},{3,1},... | collective-permute-start | bytes 479240 | tf_op jit(solution)/shard_map/ppermute | solution.py:479
  12.4 0.4 %project.1 = (f32[16,16,128]{2,1,0:T(8,128)S(1)}, f32[16,16,128]{2,1,0:T(8,128)S(1)}) custom-call(bf16[32,64,256]{2,1,0:T(8,128)(2,1)S(1)} %bitcast.5, f32[2,80,256]{2,1,0:T(8,128)S(1)} %copy-done.1), custom_call_target="tpu_custom_call" | custom-call | tf_op jit(solution)/shard_map/project/pallas_call | solution.py:199
  12.8 0.0 collective-permute-start.1
  12.9 1.3 %collective-permute-done.1.other_ref.refs_7_ = f32[16,16,128]{2,1,0:T(8,128)S(1)} collective-permute-done((f32[16,16,128]{2,1,0:T(8,128)S(1)}, f32[16,16,128]{2,1,0:T(8,128)S(1)}, u32[]{:S(2)}, u32[]{:S(2)}) %collective-permute-start.1) | collective-permute-done | bytes 131104 | tf_op jit(solution)/shard_map/ppermute | solution.py:491
  14.2 0.2 edge_projections.1
  14.4 0.1 collective-permute-start.2
  14.5 3.7 %collective-permute-done.2.refs_10_ = f32[32,128]{1,0:T(8,128)S(1)} collective-permute-done((f32[32,128]{1,0:T(8,128)S(1)}, f32[32,128]{1,0:T(8,128)S(1)}, u32[]{:S(2)}, u32[]{:S(2)}) %collective-permute-start.2) | collective-permute-done | bytes 16416 | tf_op jit(solution)/shard_map/ppermute | solution.py:479
  18.2 0.0 collective-permute-done
  18.3 0.4 collective-permute-start.4
  18.7 2.8 %collective-permute-start.3 = (bf16[720,128]{1,0:T(8,128)(2,1)S(1)}, bf16[720,128]{1,0:T(8,128)(2,1)S(1)}, u32[]{:S(2)}, u32[]{:S(2)}) collective-permute-start(bf16[720,128]{1,0:T(8,128)(2,1)S(1)} %pad_maximum_fusion), channel_id=1, source_target_pairs={{0,8},{2,10},{4,12},{6,14},{8,0},{10,2},{12,4},{14,6},{1,9},{3,11}... | collective-permute-start | bytes 552968 | tf_op jit(solution)/shard_map/ppermute | solution.py:479
  21.5 2.6 %collective-permute-start.8 = (bf16[656,128]{1,0:T(8,128)(2,1)S(1)}, bf16[656,128]{1,0:T(8,128)(2,1)S(1)}, u32[]{:S(2)}, u32[]{:S(2)}) collective-permute-start(bf16[656,128]{1,0:T(8,128)(2,1)S(1)} %pad_maximum_fusion.2), channel_id=1, source_target_pairs={{0,6},{2,4},{4,2},{6,0},{8,14},{10,12},{12,10},{14,8},{1,7},{3,5},... | collective-permute-start | bytes 503816 | tf_op jit(solution)/shard_map/ppermute | solution.py:479
  24.1 0.0 collective-permute-done.4
  24.2 7.0 %collective-permute-start.5 = (bf16[656,128]{1,0:T(8,128)(2,1)S(1)}, bf16[656,128]{1,0:T(8,128)(2,1)S(1)}, u32[]{:S(2)}, u32[]{:S(2)}) collective-permute-start(bf16[656,128]{1,0:T(8,128)(2,1)S(1)} %pad_maximum_fusion.1), channel_id=1, source_target_pairs={{0,12},{2,14},{4,8},{6,10},{8,4},{10,6},{12,0},{14,2},{1,13},{3,15... | collective-permute-start | bytes 503816 | tf_op jit(solution)/shard_map/ppermute | solution.py:479
  31.2 0.0 collective-permute-start.7
  31.2 1.3 %collective-permute-done.3.refs_1_ = bf16[720,128]{1,0:T(8,128)(2,1)S(1)} collective-permute-done((bf16[720,128]{1,0:T(8,128)(2,1)S(1)}, bf16[720,128]{1,0:T(8,128)(2,1)S(1)}, u32[]{:S(2)}, u32[]{:S(2)}) %collective-permute-start.3) | collective-permute-done | bytes 184352 | tf_op jit(solution)/shard_map/ppermute | solution.py:479
  32.5 3.2 %collective-permute-done.5.refs_2_ = bf16[656,128]{1,0:T(8,128)(2,1)S(1)} collective-permute-done((bf16[656,128]{1,0:T(8,128)(2,1)S(1)}, bf16[656,128]{1,0:T(8,128)(2,1)S(1)}, u32[]{:S(2)}, u32[]{:S(2)}) %collective-permute-start.5) | collective-permute-done | bytes 167968 | tf_op jit(solution)/shard_map/ppermute | solution.py:479
  35.7 0.8 %collective-permute-done.6.refs_3_ = bf16[624,128]{1,0:T(8,128)(2,1)S(1)} collective-permute-done((bf16[624,128]{1,0:T(8,128)(2,1)S(1)}, bf16[624,128]{1,0:T(8,128)(2,1)S(1)}, u32[]{:S(2)}, u32[]{:S(2)}) %collective-permute-start.6) | collective-permute-done | bytes 159776 | tf_op jit(solution)/shard_map/ppermute | solution.py:479
  36.5 0.8 %collective-permute-done.7.refs_4_ = bf16[624,128]{1,0:T(8,128)(2,1)S(1)} collective-permute-done((bf16[624,128]{1,0:T(8,128)(2,1)S(1)}, bf16[624,128]{1,0:T(8,128)(2,1)S(1)}, u32[]{:S(2)}, u32[]{:S(2)}) %collective-permute-start.7) | collective-permute-done | bytes 159776 | tf_op jit(solution)/shard_map/ppermute | solution.py:479
  37.3 0.8 %statistics.1 = (bf16[256,128]{1,0:T(8,128)(2,1)S(1)}, bf16[256,128]{1,0:T(8,128)(2,1)S(1)}, f32[8,256]{1,0:T(8,128)S(1)}) custom-call(bf16[624,128]{1,0:T(8,128)(2,1)S(1)} %get-tuple-element.26.refs_0_, bf16[720,128]{1,0:T(8,128)(2,1)S(1)} %collective-permute-done.3.refs_1_, bf16[656,128]{1,0:T(8,128)(2,1)S(1)} %collective-permute-done.5.refs_2_, ...), custom_call_target="tpu_custom_call" | custom-call | tf_op jit(solution)/shard_map/statistics/pallas_call | solution.py:360
  38.1 0.5 %collective-permute-start.9 = (f32[8,256]{1,0:T(8,128)S(1)}, f32[8,256]{1,0:T(8,128)S(1)}, u32[]{:S(2)}, u32[]{:S(2)}) collective-permute-start(f32[8,256]{1,0:T(8,128)S(1)} %get-tuple-element.45.lag_ref), channel_id=1, source_target_pairs={{0,1},{1,0},{2,3},{3,2},{4,5},{5,4},{6,7},{7,6},{8,9},{9,8},{10,11... | collective-permute-start | bytes 24584 | tf_op jit(solution)/shard_map/ppermute | solution.py:530
  38.6 0.8 %collective-permute-done.9.lag_got_ref = f32[8,256]{1,0:T(8,128)S(1)} collective-permute-done((f32[8,256]{1,0:T(8,128)S(1)}, f32[8,256]{1,0:T(8,128)S(1)}, u32[]{:S(2)}, u32[]{:S(2)}) %collective-permute-start.9) | collective-permute-done | bytes 8224 | tf_op jit(solution)/shard_map/ppermute | solution.py:530
  39.5 2.1 %subtract.1 = (bf16[2,16,64,256]{3,2,1,0:T(8,128)(2,1)}, f32[2,33]{1,0:T(2,128)}) custom-call(f32[8,256]{1,0:T(8,128)S(1)} %get-tuple-element.45.lag_ref, f32[8,256]{1,0:T(8,128)S(1)} %collective-permute-done.9.lag_got_ref, f32[2,33]{1,0:T(2,128)S(1)} %bitcast.8, f32[2,80,256]{2,1,0:T(8,128)S(1)} %copy-done.1, ...), custom_call_target="tpu_custom_call" | custom-call | tf_op jit(solution)/shard_map/subtract/pallas_call | solution.py:445
  (21 shorter events, 0.2 us)
Async XLA Ops:
  0.6 11.7 %copy-start.1 = (f32[2,80,256]{2,1,0:T(8,128)S(1)}, f32[2,80,256]{2,1,0:T(8,128)}, u32[]{:S(2)}) copy-start(f32[2,80,256]{2,1,0:T(8,128)} %constant.2.clone.t_ref.refs_8_.table_ref) | copy-start | bytes 491524
  0.6 11.7 %copy-start = (bf16[1,1,32,64,256]{4,3,2,1,0:T(8,128)(2,1)S(1)}, bf16[1,1,32,64,256]{4,3,2,1,0:T(8,128)(2,1)}, u32[]{:S(2)}) copy-start(bf16[1,1,32,64,256]{4,3,2,1,0:T(8,128)(2,1)} %param.5) | copy-start | bytes 3145732
  0.7 38.8 %copy-start.2 = (f32[1,1,1,2,33]{4,3,2,1,0:T(2,128)S(1)}, f32[1,1,1,2,33]{4,3,2,1,0:T(2,128)}, u32[]{:S(2)}) copy-start(f32[1,1,1,2,33]{4,3,2,1,0:T(2,128)} %param.6) | copy-start | bytes 796
  9.3 8.9 %collective-permute-start = (bf16[624,128]{1,0:T(8,128)(2,1)S(1)}, bf16[624,128]{1,0:T(8,128)(2,1)S(1)}, u32[]{:S(2)}, u32[]{:S(2)}) collective-permute-start(bf16[624,128]{1,0:T(8,128)(2,1)S(1)} %get-tuple-element.28), channel_id=1, source_target_pairs={{0,2},{2,0},{4,6},{6,4},{8,10},{10,8},{12,14},{14,12},{1,3},{3,1},... | collective-permute-start | bytes 479240 | tf_op jit(solution)/shard_map/ppermute | solution.py:479
  12.8 1.4 %collective-permute-start.1 = (f32[16,16,128]{2,1,0:T(8,128)S(1)}, f32[16,16,128]{2,1,0:T(8,128)S(1)}, u32[]{:S(2)}, u32[]{:S(2)}) collective-permute-start(f32[16,16,128]{2,1,0:T(8,128)S(1)} %get-tuple-element.32), channel_id=1, source_target_pairs={{0,1},{1,0},{2,3},{3,2},{4,5},{5,4},{6,7},{7,6},{8,9},{9,8},{10,11... | collective-permute-start | bytes 393224 | tf_op jit(solution)/shard_map/ppermute | solution.py:491
  14.4 3.8 %collective-permute-start.2 = (f32[32,128]{1,0:T(8,128)S(1)}, f32[32,128]{1,0:T(8,128)S(1)}, u32[]{:S(2)}, u32[]{:S(2)}) collective-permute-start(f32[32,128]{1,0:T(8,128)S(1)} %get-tuple-element.34), channel_id=1, source_target_pairs={{0,2},{2,0},{4,6},{6,4},{8,10},{10,8},{12,14},{14,12},{1,3},{3,1},... | collective-permute-start | bytes 49160 | tf_op jit(solution)/shard_map/ppermute | solution.py:479
  18.3 5.8 %collective-permute-start.4 = (bf16[624,128]{1,0:T(8,128)(2,1)S(1)}, bf16[624,128]{1,0:T(8,128)(2,1)S(1)}, u32[]{:S(2)}, u32[]{:S(2)}) collective-permute-start(bf16[624,128]{1,0:T(8,128)(2,1)S(1)} %get-tuple-element.38), channel_id=1, source_target_pairs={{0,2},{2,0},{4,6},{6,4},{8,10},{10,8},{12,14},{14,12},{1,3},{3,1},... | collective-permute-start | bytes 479240 | tf_op jit(solution)/shard_map/ppermute | solution.py:479
  18.7 13.8 %collective-permute-start.3 = (bf16[720,128]{1,0:T(8,128)(2,1)S(1)}, bf16[720,128]{1,0:T(8,128)(2,1)S(1)}, u32[]{:S(2)}, u32[]{:S(2)}) collective-permute-start(bf16[720,128]{1,0:T(8,128)(2,1)S(1)} %pad_maximum_fusion), channel_id=1, source_target_pairs={{0,8},{2,10},{4,12},{6,14},{8,0},{10,2},{12,4},{14,6},{1,9},{3,11}... | collective-permute-start | bytes 552968 | tf_op jit(solution)/shard_map/ppermute | solution.py:479
  21.5 9.7 %collective-permute-start.8 = (bf16[656,128]{1,0:T(8,128)(2,1)S(1)}, bf16[656,128]{1,0:T(8,128)(2,1)S(1)}, u32[]{:S(2)}, u32[]{:S(2)}) collective-permute-start(bf16[656,128]{1,0:T(8,128)(2,1)S(1)} %pad_maximum_fusion.2), channel_id=1, source_target_pairs={{0,6},{2,4},{4,2},{6,0},{8,14},{10,12},{12,10},{14,8},{1,7},{3,5},... | collective-permute-start | bytes 503816 | tf_op jit(solution)/shard_map/ppermute | solution.py:479
  24.2 11.5 %collective-permute-start.5 = (bf16[656,128]{1,0:T(8,128)(2,1)S(1)}, bf16[656,128]{1,0:T(8,128)(2,1)S(1)}, u32[]{:S(2)}, u32[]{:S(2)}) collective-permute-start(bf16[656,128]{1,0:T(8,128)(2,1)S(1)} %pad_maximum_fusion.1), channel_id=1, source_target_pairs={{0,12},{2,14},{4,8},{6,10},{8,4},{10,6},{12,0},{14,2},{1,13},{3,15... | collective-permute-start | bytes 503816 | tf_op jit(solution)/shard_map/ppermute | solution.py:479
  31.2 5.3 %collective-permute-start.6 = (bf16[624,128]{1,0:T(8,128)(2,1)S(1)}, bf16[624,128]{1,0:T(8,128)(2,1)S(1)}, u32[]{:S(2)}, u32[]{:S(2)}) collective-permute-start(bf16[624,128]{1,0:T(8,128)(2,1)S(1)} %get-tuple-element.41), channel_id=1, source_target_pairs={{0,2},{2,0},{4,6},{6,4},{8,10},{10,8},{12,14},{14,12},{1,3},{3,1},... | collective-permute-start | bytes 479240 | tf_op jit(solution)/shard_map/ppermute | solution.py:479
  31.2 6.1 %collective-permute-start.7 = (bf16[624,128]{1,0:T(8,128)(2,1)S(1)}, bf16[624,128]{1,0:T(8,128)(2,1)S(1)}, u32[]{:S(2)}, u32[]{:S(2)}) collective-permute-start(bf16[624,128]{1,0:T(8,128)(2,1)S(1)} %get-tuple-element.42), channel_id=1, source_target_pairs={{0,4},{2,6},{4,0},{6,2},{8,12},{10,14},{12,8},{14,10},{1,5},{3,7},... | collective-permute-start | bytes 479240 | tf_op jit(solution)/shard_map/ppermute | solution.py:479
  38.1 1.4 %collective-permute-start.10 = (bf16[256,128]{1,0:T(8,128)(2,1)S(1)}, bf16[256,128]{1,0:T(8,128)(2,1)S(1)}, u32[]{:S(2)}, u32[]{:S(2)}) collective-permute-start(bf16[256,128]{1,0:T(8,128)(2,1)S(1)} %get-tuple-element.47), channel_id=1, source_target_pairs={{0,1},{1,0},{2,3},{3,2},{4,5},{5,4},{6,7},{7,6},{8,9},{9,8},{10,11... | collective-permute-start | bytes 196616 | tf_op jit(solution)/shard_map/ppermute | solution.py:529
  38.1 1.4 %collective-permute-start.9 = (f32[8,256]{1,0:T(8,128)S(1)}, f32[8,256]{1,0:T(8,128)S(1)}, u32[]{:S(2)}, u32[]{:S(2)}) collective-permute-start(f32[8,256]{1,0:T(8,128)S(1)} %get-tuple-element.45.lag_ref), channel_id=1, source_target_pairs={{0,1},{1,0},{2,3},{3,2},{4,5},{5,4},{6,7},{7,6},{8,9},{9,8},{10,11... | collective-permute-start | bytes 24584 | tf_op jit(solution)/shard_map/ppermute | solution.py:530

commit v5 on v4

--- a/solution.py
+++ b/solution.py
@@ -435,7 +435,7 @@
 
 
 def subtract(lag, lag_got, start, table, own, got, recorded):
-    steps = 2
+    steps = 1
     half = WC // 2
     each = half // steps
     recorded = recorded.reshape(2, half, 64, NT)
@@ -504,8 +504,7 @@
     totals += [parcel(add(kept[n], came[n]), far[n]) for n in range(1, len(far))]
     got = [swap(x, k) for x, k in zip(totals, far)]
     own, *close = close
-    (close[0], close[1]), _ = after(((close[0], close[1]), totals[1]))
-    close[2], _ = after((close[2], totals[0]))
+    close, _ = after((close, totals[0]))
     close = [swap(parcel(x, k), k) for k, x in enumerate(close, 1)]
     size = own.shape[0]
     if rows == 2:

time: 41.7 us -> 41.6 us (level)
  no operation moved by 1% of the time
where the time goes in v5:
time: 41.6 us; the launch traced here: 41.5 us
  starting transfers between devices  16.5 us (40%)
  Pallas kernels  12.1 us (29%)
  waiting for transfers between devices  12 us (29%)
  between operations  0.73 us (2%)
    ppermute x8, starting transfers between devices, swap(): return lax.ppermute(x, 'refl', [(i, i ^ k) for i in range(refl)])  15.9 us
    ppermute x8, waiting for transfers between devices, swap(): return lax.ppermute(x, 'refl', [(i, i ^ k) for i in range(refl)])  9.8 us
    pallas_call x1, Pallas kernels, block_terms(): pl.pallas_call(functools.partial(terms_kernel, rows), in_specs=[pl.BlockS...  8.64 us
    pallas_call x1, Pallas kernels, subtract(): pl.pallas_call(functools.partial(subtract_kernel, steps), grid=(steps,),...  2.01 us
    ppermute x1, waiting for transfers between devices, body(): other = lax.ppermute(send, 'freq', core_swap)  1.33 us
  transfers between devices with their start and end apart: 11, of which 7 were waited for; matrix products, arithmetic and copies ran while one was open for 0% of the time, Pallas kernels for 2%

profile of v5, /device:TPU:0, one launch (start us, length us, event | category | flops | bytes accessed | tf_op | source)
XLA Modules:
  0.0 41.5 jit_solution(12046335799066655854)
XLA Ops:
  0.6 0.0 copy-start.1
  0.7 8.6 %block_terms.1 = (bf16[624,128]{1,0:T(8,128)(2,1)S(1)}, bf16[624,128]{1,0:T(8,128)(2,1)S(1)}, bf16[624,128]{1,0:T(8,128)(2,1)S(1)}, bf16[624,128]{1,0:T(8,128)(2...) custom-call(bf16[2,8,512,1024]{3,2,1,0:T(8,128)(2,1)} %s_hbm.1), custom_call_target="tpu_custom_call" | custom-call | tf_op jit(solution)/shard_map/block_terms/pallas_call | solution.py:170
  9.3 3.0 %collective-permute-start = (bf16[624,128]{1,0:T(8,128)(2,1)S(1)}, bf16[624,128]{1,0:T(8,128)(2,1)S(1)}, u32[]{:S(2)}, u32[]{:S(2)}) collective-permute-start(bf16[624,128]{1,0:T(8,128)(2,1)S(1)} %get-tuple-element.28), channel_id=1, source_target_pairs={{0,2},{2,0},{4,6},{6,4},{8,10},{10,8},{12,14},{14,12},{1,3},{3,1},... | collective-permute-start | bytes 479240 | tf_op jit(solution)/shard_map/ppermute | solution.py:479
  12.4 0.4 %project.1 = (f32[16,16,128]{2,1,0:T(8,128)S(1)}, f32[16,16,128]{2,1,0:T(8,128)S(1)}) custom-call(bf16[32,64,256]{2,1,0:T(8,128)(2,1)S(1)} %bitcast.5, f32[2,80,256]{2,1,0:T(8,128)S(1)} %copy-done.1), custom_call_target="tpu_custom_call" | custom-call | tf_op jit(solution)/shard_map/project/pallas_call | solution.py:199
  12.8 0.0 collective-permute-start.1
  12.9 1.3 %collective-permute-done.1.other_ref.refs_7_ = f32[16,16,128]{2,1,0:T(8,128)S(1)} collective-permute-done((f32[16,16,128]{2,1,0:T(8,128)S(1)}, f32[16,16,128]{2,1,0:T(8,128)S(1)}, u32[]{:S(2)}, u32[]{:S(2)}) %collective-permute-start.1) | collective-permute-done | bytes 131104 | tf_op jit(solution)/shard_map/ppermute | solution.py:491
  14.2 0.2 edge_projections.1
  14.4 0.1 collective-permute-start.2
  14.5 3.7 %collective-permute-done.2.refs_10_ = f32[32,128]{1,0:T(8,128)S(1)} collective-permute-done((f32[32,128]{1,0:T(8,128)S(1)}, f32[32,128]{1,0:T(8,128)S(1)}, u32[]{:S(2)}, u32[]{:S(2)}) %collective-permute-start.2) | collective-permute-done | bytes 16416 | tf_op jit(solution)/shard_map/ppermute | solution.py:479
  18.2 0.0 collective-permute-done
  18.3 0.4 collective-permute-start.4
  18.7 2.8 %collective-permute-start.3 = (bf16[720,128]{1,0:T(8,128)(2,1)S(1)}, bf16[720,128]{1,0:T(8,128)(2,1)S(1)}, u32[]{:S(2)}, u32[]{:S(2)}) collective-permute-start(bf16[720,128]{1,0:T(8,128)(2,1)S(1)} %pad_maximum_fusion), channel_id=1, source_target_pairs={{0,8},{2,10},{4,12},{6,14},{8,0},{10,2},{12,4},{14,6},{1,9},{3,11}... | collective-permute-start | bytes 552968 | tf_op jit(solution)/shard_map/ppermute | solution.py:479
  21.5 2.6 %collective-permute-start.8 = (bf16[656,128]{1,0:T(8,128)(2,1)S(1)}, bf16[656,128]{1,0:T(8,128)(2,1)S(1)}, u32[]{:S(2)}, u32[]{:S(2)}) collective-permute-start(bf16[656,128]{1,0:T(8,128)(2,1)S(1)} %pad_maximum_fusion.2), channel_id=1, source_target_pairs={{0,6},{2,4},{4,2},{6,0},{8,14},{10,12},{12,10},{14,8},{1,7},{3,5},... | collective-permute-start | bytes 503816 | tf_op jit(solution)/shard_map/ppermute | solution.py:479
  24.1 0.0 collective-permute-done.4
  24.2 7.0 %collective-permute-start.5 = (bf16[656,128]{1,0:T(8,128)(2,1)S(1)}, bf16[656,128]{1,0:T(8,128)(2,1)S(1)}, u32[]{:S(2)}, u32[]{:S(2)}) collective-permute-start(bf16[656,128]{1,0:T(8,128)(2,1)S(1)} %pad_maximum_fusion.1), channel_id=1, source_target_pairs={{0,12},{2,14},{4,8},{6,10},{8,4},{10,6},{12,0},{14,2},{1,13},{3,15... | collective-permute-start | bytes 503816 | tf_op jit(solution)/shard_map/ppermute | solution.py:479
  31.2 1.3 %collective-permute-done.3.refs_1_ = bf16[720,128]{1,0:T(8,128)(2,1)S(1)} collective-permute-done((bf16[720,128]{1,0:T(8,128)(2,1)S(1)}, bf16[720,128]{1,0:T(8,128)(2,1)S(1)}, u32[]{:S(2)}, u32[]{:S(2)}) %collective-permute-start.3) | collective-permute-done | bytes 184352 | tf_op jit(solution)/shard_map/ppermute | solution.py:479
  32.5 3.2 %collective-permute-done.5.refs_2_ = bf16[656,128]{1,0:T(8,128)(2,1)S(1)} collective-permute-done((bf16[656,128]{1,0:T(8,128)(2,1)S(1)}, bf16[656,128]{1,0:T(8,128)(2,1)S(1)}, u32[]{:S(2)}, u32[]{:S(2)}) %collective-permute-start.5) | collective-permute-done | bytes 167968 | tf_op jit(solution)/shard_map/ppermute | solution.py:479
  35.7 0.8 %collective-permute-done.6.refs_3_ = bf16[624,128]{1,0:T(8,128)(2,1)S(1)} collective-permute-done((bf16[624,128]{1,0:T(8,128)(2,1)S(1)}, bf16[624,128]{1,0:T(8,128)(2,1)S(1)}, u32[]{:S(2)}, u32[]{:S(2)}) %collective-permute-start.6) | collective-permute-done | bytes 159776 | tf_op jit(solution)/shard_map/ppermute | solution.py:479
  36.5 0.8 %collective-permute-done.7.refs_4_ = bf16[624,128]{1,0:T(8,128)(2,1)S(1)} collective-permute-done((bf16[624,128]{1,0:T(8,128)(2,1)S(1)}, bf16[624,128]{1,0:T(8,128)(2,1)S(1)}, u32[]{:S(2)}, u32[]{:S(2)}) %collective-permute-start.7) | collective-permute-done | bytes 159776 | tf_op jit(solution)/shard_map/ppermute | solution.py:479
  37.3 0.8 %statistics.1 = (bf16[256,128]{1,0:T(8,128)(2,1)S(1)}, bf16[256,128]{1,0:T(8,128)(2,1)S(1)}, f32[8,256]{1,0:T(8,128)S(1)}) custom-call(bf16[624,128]{1,0:T(8,128)(2,1)S(1)} %get-tuple-element.26.refs_0_, bf16[720,128]{1,0:T(8,128)(2,1)S(1)} %collective-permute-done.3.refs_1_, bf16[656,128]{1,0:T(8,128)(2,1)S(1)} %collective-permute-done.5.refs_2_, ...), custom_call_target="tpu_custom_call" | custom-call | tf_op jit(solution)/shard_map/statistics/pallas_call | solution.py:360
  38.1 0.0 collective-permute-start.10
  38.1 0.5 %collective-permute-start.9 = (f32[8,256]{1,0:T(8,128)S(1)}, f32[8,256]{1,0:T(8,128)S(1)}, u32[]{:S(2)}, u32[]{:S(2)}) collective-permute-start(f32[8,256]{1,0:T(8,128)S(1)} %get-tuple-element.45.lag_ref), channel_id=1, source_target_pairs={{0,1},{1,0},{2,3},{3,2},{4,5},{5,4},{6,7},{7,6},{8,9},{9,8},{10,11... | collective-permute-start | bytes 24584 | tf_op jit(solution)/shard_map/ppermute | solution.py:529
  38.6 0.8 %collective-permute-done.9.lag_got_ref = f32[8,256]{1,0:T(8,128)S(1)} collective-permute-done((f32[8,256]{1,0:T(8,128)S(1)}, f32[8,256]{1,0:T(8,128)S(1)}, u32[]{:S(2)}, u32[]{:S(2)}) %collective-permute-start.9) | collective-permute-done | bytes 8224 | tf_op jit(solution)/shard_map/ppermute | solution.py:529
  39.5 2.0 %subtract.1 = (bf16[2,16,64,256]{3,2,1,0:T(8,128)(2,1)}, f32[2,33]{1,0:T(2,128)}) custom-call(f32[8,256]{1,0:T(8,128)S(1)} %get-tuple-element.45.lag_ref, f32[8,256]{1,0:T(8,128)S(1)} %collective-permute-done.9.lag_got_ref, f32[2,33]{1,0:T(2,128)S(1)} %bitcast.8, f32[2,80,256]{2,1,0:T(8,128)S(1)} %copy-done.1, ...), custom_call_target="tpu_custom_call" | custom-call | tf_op jit(solution)/shard_map/subtract/pallas_call | solution.py:445
  (21 shorter events, 0.2 us)
Async XLA Ops:
  0.6 11.7 %copy-start.1 = (f32[2,80,256]{2,1,0:T(8,128)S(1)}, f32[2,80,256]{2,1,0:T(8,128)}, u32[]{:S(2)}) copy-start(f32[2,80,256]{2,1,0:T(8,128)} %constant.2.clone.t_ref.refs_8_.table_ref) | copy-start | bytes 491524
  0.6 11.7 %copy-start = (bf16[1,1,32,64,256]{4,3,2,1,0:T(8,128)(2,1)S(1)}, bf16[1,1,32,64,256]{4,3,2,1,0:T(8,128)(2,1)}, u32[]{:S(2)}) copy-start(bf16[1,1,32,64,256]{4,3,2,1,0:T(8,128)(2,1)} %param.5) | copy-start | bytes 3145732
  0.7 38.8 %copy-start.2 = (f32[1,1,1,2,33]{4,3,2,1,0:T(2,128)S(1)}, f32[1,1,1,2,33]{4,3,2,1,0:T(2,128)}, u32[]{:S(2)}) copy-start(f32[1,1,1,2,33]{4,3,2,1,0:T(2,128)} %param.6) | copy-start | bytes 796
  9.3 8.9 %collective-permute-start = (bf16[624,128]{1,0:T(8,128)(2,1)S(1)}, bf16[624,128]{1,0:T(8,128)(2,1)S(1)}, u32[]{:S(2)}, u32[]{:S(2)}) collective-permute-start(bf16[624,128]{1,0:T(8,128)(2,1)S(1)} %get-tuple-element.28), channel_id=1, source_target_pairs={{0,2},{2,0},{4,6},{6,4},{8,10},{10,8},{12,14},{14,12},{1,3},{3,1},... | collective-permute-start | bytes 479240 | tf_op jit(solution)/shard_map/ppermute | solution.py:479
  12.8 1.4 %collective-permute-start.1 = (f32[16,16,128]{2,1,0:T(8,128)S(1)}, f32[16,16,128]{2,1,0:T(8,128)S(1)}, u32[]{:S(2)}, u32[]{:S(2)}) collective-permute-start(f32[16,16,128]{2,1,0:T(8,128)S(1)} %get-tuple-element.32), channel_id=1, source_target_pairs={{0,1},{1,0},{2,3},{3,2},{4,5},{5,4},{6,7},{7,6},{8,9},{9,8},{10,11... | collective-permute-start | bytes 393224 | tf_op jit(solution)/shard_map/ppermute | solution.py:491
  14.4 3.8 %collective-permute-start.2 = (f32[32,128]{1,0:T(8,128)S(1)}, f32[32,128]{1,0:T(8,128)S(1)}, u32[]{:S(2)}, u32[]{:S(2)}) collective-permute-start(f32[32,128]{1,0:T(8,128)S(1)} %get-tuple-element.34), channel_id=1, source_target_pairs={{0,2},{2,0},{4,6},{6,4},{8,10},{10,8},{12,14},{14,12},{1,3},{3,1},... | collective-permute-start | bytes 49160 | tf_op jit(solution)/shard_map/ppermute | solution.py:479
  18.3 5.8 %collective-permute-start.4 = (bf16[624,128]{1,0:T(8,128)(2,1)S(1)}, bf16[624,128]{1,0:T(8,128)(2,1)S(1)}, u32[]{:S(2)}, u32[]{:S(2)}) collective-permute-start(bf16[624,128]{1,0:T(8,128)(2,1)S(1)} %get-tuple-element.38), channel_id=1, source_target_pairs={{0,2},{2,0},{4,6},{6,4},{8,10},{10,8},{12,14},{14,12},{1,3},{3,1},... | collective-permute-start | bytes 479240 | tf_op jit(solution)/shard_map/ppermute | solution.py:479
  18.7 13.8 %collective-permute-start.3 = (bf16[720,128]{1,0:T(8,128)(2,1)S(1)}, bf16[720,128]{1,0:T(8,128)(2,1)S(1)}, u32[]{:S(2)}, u32[]{:S(2)}) collective-permute-start(bf16[720,128]{1,0:T(8,128)(2,1)S(1)} %pad_maximum_fusion), channel_id=1, source_target_pairs={{0,8},{2,10},{4,12},{6,14},{8,0},{10,2},{12,4},{14,6},{1,9},{3,11}... | collective-permute-start | bytes 552968 | tf_op jit(solution)/shard_map/ppermute | solution.py:479
  21.5 9.7 %collective-permute-start.8 = (bf16[656,128]{1,0:T(8,128)(2,1)S(1)}, bf16[656,128]{1,0:T(8,128)(2,1)S(1)}, u32[]{:S(2)}, u32[]{:S(2)}) collective-permute-start(bf16[656,128]{1,0:T(8,128)(2,1)S(1)} %pad_maximum_fusion.2), channel_id=1, source_target_pairs={{0,6},{2,4},{4,2},{6,0},{8,14},{10,12},{12,10},{14,8},{1,7},{3,5},... | collective-permute-start | bytes 503816 | tf_op jit(solution)/shard_map/ppermute | solution.py:479
  24.2 11.5 %collective-permute-start.5 = (bf16[656,128]{1,0:T(8,128)(2,1)S(1)}, bf16[656,128]{1,0:T(8,128)(2,1)S(1)}, u32[]{:S(2)}, u32[]{:S(2)}) collective-permute-start(bf16[656,128]{1,0:T(8,128)(2,1)S(1)} %pad_maximum_fusion.1), channel_id=1, source_target_pairs={{0,12},{2,14},{4,8},{6,10},{8,4},{10,6},{12,0},{14,2},{1,13},{3,15... | collective-permute-start | bytes 503816 | tf_op jit(solution)/shard_map/ppermute | solution.py:479
  31.2 5.3 %collective-permute-start.6 = (bf16[624,128]{1,0:T(8,128)(2,1)S(1)}, bf16[624,128]{1,0:T(8,128)(2,1)S(1)}, u32[]{:S(2)}, u32[]{:S(2)}) collective-permute-start(bf16[624,128]{1,0:T(8,128)(2,1)S(1)} %get-tuple-element.42), channel_id=1, source_target_pairs={{0,2},{2,0},{4,6},{6,4},{8,10},{10,8},{12,14},{14,12},{1,3},{3,1},... | collective-permute-start | bytes 479240 | tf_op jit(solution)/shard_map/ppermute | solution.py:479
  31.2 6.1 %collective-permute-start.7 = (bf16[624,128]{1,0:T(8,128)(2,1)S(1)}, bf16[624,128]{1,0:T(8,128)(2,1)S(1)}, u32[]{:S(2)}, u32[]{:S(2)}) collective-permute-start(bf16[624,128]{1,0:T(8,128)(2,1)S(1)} %get-tuple-element.43), channel_id=1, source_target_pairs={{0,4},{2,6},{4,0},{6,2},{8,12},{10,14},{12,8},{14,10},{1,5},{3,7},... | collective-permute-start | bytes 479240 | tf_op jit(solution)/shard_map/ppermute | solution.py:479
  38.1 1.4 %collective-permute-start.10 = (bf16[256,128]{1,0:T(8,128)(2,1)S(1)}, bf16[256,128]{1,0:T(8,128)(2,1)S(1)}, u32[]{:S(2)}, u32[]{:S(2)}) collective-permute-start(bf16[256,128]{1,0:T(8,128)(2,1)S(1)} %get-tuple-element.47), channel_id=1, source_target_pairs={{0,1},{1,0},{2,3},{3,2},{4,5},{5,4},{6,7},{7,6},{8,9},{9,8},{10,11... | collective-permute-start | bytes 196616 | tf_op jit(solution)/shard_map/ppermute | solution.py:528
  38.1 1.4 %collective-permute-start.9 = (f32[8,256]{1,0:T(8,128)S(1)}, f32[8,256]{1,0:T(8,128)S(1)}, u32[]{:S(2)}, u32[]{:S(2)}) collective-permute-start(f32[8,256]{1,0:T(8,128)S(1)} %get-tuple-element.45.lag_ref), channel_id=1, source_target_pairs={{0,1},{1,0},{2,3},{3,2},{4,5},{5,4},{6,7},{7,6},{8,9},{9,8},{10,11... | collective-permute-start | bytes 24584 | tf_op jit(solution)/shard_map/ppermute | solution.py:529

commit v6 on v5

--- a/solution.py
+++ b/solution.py
@@ -293,7 +293,7 @@
     here = pl.multiple_of(j * count, count)
     there = pl.multiple_of((1 - j) * count, count)
     own_ref[...] = spectrum[pl.ds(here, count), :].astype(BF16)
-    send_ref[...] = spectrum[pl.ds(there, count), :].astype(BF16)
+    send_ref[:count, :] = spectrum[pl.ds(there, count), :]
     sums = []
     for at, q_ref in ((here, keep_ref), (there, other_ref)):
         power = in_phase = turned = jnp.zeros((HF, LANES), F32)
@@ -352,7 +352,10 @@
         z = jnp.where(at_side, jnp.broadcast_to(z, (8, LANES)), 0.0)
         to = (column == n * HF + row // 16).astype(F32)
         stats = stats + dot(z, to, (((1,), (0,)), ((), ())))
-    lag_ref[...] = dot(stats, lags_ref[j, LAGS], (((1,), (0,)), ((), ())))
+    lag = dot(stats, lags_ref[j, LAGS], (((1,), (0,)), ((), ())))
+    lag_ref[...] = lag
+    send_ref[count : count + 8, :] = lag[:, :LANES]
+    send_ref[count + 8 :, :] = lag[:, LANES:]
 
 
 def statistics(blocks, keep, other, table, bands, nears, fars, rows):
@@ -361,7 +364,7 @@
         functools.partial(statistics_kernel, rows),
         out_shape=[
             jax.ShapeDtypeStruct((count, LANES), BF16),
-            jax.ShapeDtypeStruct((count, LANES), BF16),
+            jax.ShapeDtypeStruct((count + 16, LANES), F32),
             jax.ShapeDtypeStruct((8, 2 * LANES), F32),
         ],
         scratch_shapes=[pltpu.VMEM((2 * count, LANES), F32)],
@@ -373,7 +376,6 @@
 def subtract_kernel(
     steps,
     lag_ref,
-    lag_got_ref,
     start_ref,
     table_ref,
     own_ref,
@@ -390,8 +392,9 @@
 
     @pl.when(step == 0)
     def _():
-        total = lag_ref[0:2, :] + lag_got_ref[2:4, :]
-        lag, target = total[:, :LANES], total[:, LANES:]
+        at = half * 16
+        lag = lag_ref[0:2, :LANES] + got_ref[at + 2 : at + 4, :]
+        target = lag_ref[0:2, LANES:] + got_ref[at + 10 : at + 12, :]
         lane = lanes_of(2)
         held = lane < TAPS
         magnitude = jnp.where(held, jnp.abs(lag), 0.0)
@@ -425,7 +428,7 @@
     first = (lane % 64) < WC
     zero = jnp.zeros((32, LANES), BF16)
     for s in range(half // steps):
-        x = jnp.concatenate([own_ref[s * 16 : s * 16 + 16, :], got_ref[s * 16 : s * 16 + 16, :]], 0)
+        x = jnp.concatenate([own_ref[s * 16 : s * 16 + 16, :], got_ref[s * 16 : s * 16 + 16, :].astype(BF16)], 0)
         both = jnp.concatenate([jnp.where(first, x, zero), jnp.where(first, zero, x)], 0)
         predicted = lax.dot_general(
             both, table, (((0,), (0,)), ((), ())), preferred_element_type=F32
@@ -434,13 +437,13 @@
         clean_ref[1, s] = (r_high_ref[0, s].astype(F32) - predicted[64:]).astype(BF16)
 
 
-def subtract(lag, lag_got, start, table, own, got, recorded):
+def subtract(lag, start, table, own, got, recorded):
     steps = 1
     half = WC // 2
     each = half // steps
     recorded = recorded.reshape(2, half, 64, NT)
     whole = lambda x: pl.BlockSpec(x.shape, lambda i: (0,) * x.ndim)
-    small = (lag, lag_got, start, table)
+    small = (lag, start, table)
     rows_spec = pl.BlockSpec((each * 16, LANES), lambda i: (i, 0))
     return pl.pallas_call(
         functools.partial(subtract_kernel, steps),
@@ -448,7 +451,7 @@
         in_specs=[whole(x) for x in small]
         + [
             rows_spec,
-            rows_spec,
+            whole(got),
             pl.BlockSpec((1, each, 64, NT), lambda i: (0, i, 0, 0)),
             pl.BlockSpec((1, each, 64, NT), lambda i: (1, i, 0, 0)),
         ],
@@ -526,10 +529,8 @@
         fars = [shift(sides, rise, (None, 2, 1, None)) for rise in (0, 1, -1)]
     own, away, lag = statistics([own] + got + close, keep, other, table, bands, nears, fars, rows)
     away_got = lax.ppermute(away, "freq", core_swap)
-    lag_got = lax.ppermute(lag, "freq", core_swap)
     clean, filters = subtract(
         lag,
-        lag_got,
         initial_filters.reshape(2, TAPS),
         table,
         own,

time: 41.6 us -> 41.6 us (level)
  starting transfers between devices: 16.5 us -> 16 us
  waiting for transfers between devices: 12 us -> 12.5 us
    ppermute x1, waiting for transfers between devices: 0.01 us -> 1.37 us  [body(): away_got = lax.ppermute(away, 'freq', core_swap)]
    ppermute x1 -> x0, waiting for transfers between devices: 0.83 us -> none  [body(): lag_got = lax.ppermute(lag, 'freq', core_swap)]
    ppermute x1 -> x0, starting transfers between devices: 0.52 us -> none  [body(): lag_got = lax.ppermute(lag, 'freq', core_swap)]
  transfers between devices with their start and end apart: 11 -> 10, of which waited for: 7 -> 7; matrix products, arithmetic and copies ran while one was open for 0% -> 0% of each run, Pallas kernels for 2% -> 2%
where the time goes in v6:
time: 41.6 us; the launch traced here: 41.5 us
  starting transfers between devices  16 us (38%)
  waiting for transfers between devices  12.5 us (30%)
  Pallas kernels  12.1 us (29%)
  between operations  0.73 us (2%)
    ppermute x8, starting transfers between devices, swap(): return lax.ppermute(x, 'refl', [(i, i ^ k) for i in range(refl)])  15.9 us
    ppermute x8, waiting for transfers between devices, swap(): return lax.ppermute(x, 'refl', [(i, i ^ k) for i in range(refl)])  9.8 us
    pallas_call x1, Pallas kernels, block_terms(): pl.pallas_call(functools.partial(terms_kernel, rows), in_specs=[pl.BlockS...  8.64 us
    pallas_call x1, Pallas kernels, subtract(): pl.pallas_call(functools.partial(subtract_kernel, steps), grid=(steps,),...  2.01 us
    ppermute x1, waiting for transfers between devices, body(): away_got = lax.ppermute(away, 'freq', core_swap)  1.37 us
    ppermute x1, waiting for transfers between devices, body(): other = lax.ppermute(send, 'freq', core_swap)  1.33 us
  transfers between devices with their start and end apart: 10, of which 7 were waited for; matrix products, arithmetic and copies ran while one was open for 0% of the time, Pallas kernels for 2%

profile of v6, /device:TPU:0, one launch (start us, length us, event | category | flops | bytes accessed | tf_op | source)
XLA Modules:
  0.0 41.5 jit_solution(14366405075230517853)
XLA Ops:
  0.6 0.0 copy-start.1
  0.7 8.6 %block_terms.1 = (bf16[624,128]{1,0:T(8,128)(2,1)S(1)}, bf16[624,128]{1,0:T(8,128)(2,1)S(1)}, bf16[624,128]{1,0:T(8,128)(2,1)S(1)}, bf16[624,128]{1,0:T(8,128)(2...) custom-call(bf16[2,8,512,1024]{3,2,1,0:T(8,128)(2,1)} %s_hbm.1), custom_call_target="tpu_custom_call" | custom-call | tf_op jit(solution)/shard_map/block_terms/pallas_call | solution.py:170
  9.3 3.0 %collective-permute-start = (bf16[624,128]{1,0:T(8,128)(2,1)S(1)}, bf16[624,128]{1,0:T(8,128)(2,1)S(1)}, u32[]{:S(2)}, u32[]{:S(2)}) collective-permute-start(bf16[624,128]{1,0:T(8,128)(2,1)S(1)} %get-tuple-element.28), channel_id=1, source_target_pairs={{0,2},{2,0},{4,6},{6,4},{8,10},{10,8},{12,14},{14,12},{1,3},{3,1},... | collective-permute-start | bytes 479240 | tf_op jit(solution)/shard_map/ppermute | solution.py:482
  12.4 0.4 %project.1 = (f32[16,16,128]{2,1,0:T(8,128)S(1)}, f32[16,16,128]{2,1,0:T(8,128)S(1)}) custom-call(bf16[32,64,256]{2,1,0:T(8,128)(2,1)S(1)} %bitcast.5, f32[2,80,256]{2,1,0:T(8,128)S(1)} %copy-done.1), custom_call_target="tpu_custom_call" | custom-call | tf_op jit(solution)/shard_map/project/pallas_call | solution.py:199
  12.8 0.0 collective-permute-start.1
  12.9 1.3 %collective-permute-done.1.other_ref.refs_7_ = f32[16,16,128]{2,1,0:T(8,128)S(1)} collective-permute-done((f32[16,16,128]{2,1,0:T(8,128)S(1)}, f32[16,16,128]{2,1,0:T(8,128)S(1)}, u32[]{:S(2)}, u32[]{:S(2)}) %collective-permute-start.1) | collective-permute-done | bytes 131104 | tf_op jit(solution)/shard_map/ppermute | solution.py:494
  14.2 0.2 edge_projections.1
  14.4 0.1 collective-permute-start.2
  14.5 3.7 %collective-permute-done.2.refs_10_ = f32[32,128]{1,0:T(8,128)S(1)} collective-permute-done((f32[32,128]{1,0:T(8,128)S(1)}, f32[32,128]{1,0:T(8,128)S(1)}, u32[]{:S(2)}, u32[]{:S(2)}) %collective-permute-start.2) | collective-permute-done | bytes 16416 | tf_op jit(solution)/shard_map/ppermute | solution.py:482
  18.2 0.0 collective-permute-done
  18.3 0.4 collective-permute-start.4
  18.7 2.8 %collective-permute-start.3 = (bf16[720,128]{1,0:T(8,128)(2,1)S(1)}, bf16[720,128]{1,0:T(8,128)(2,1)S(1)}, u32[]{:S(2)}, u32[]{:S(2)}) collective-permute-start(bf16[720,128]{1,0:T(8,128)(2,1)S(1)} %pad_maximum_fusion), channel_id=1, source_target_pairs={{0,8},{2,10},{4,12},{6,14},{8,0},{10,2},{12,4},{14,6},{1,9},{3,11}... | collective-permute-start | bytes 552968 | tf_op jit(solution)/shard_map/ppermute | solution.py:482
  21.5 2.6 %collective-permute-start.8 = (bf16[656,128]{1,0:T(8,128)(2,1)S(1)}, bf16[656,128]{1,0:T(8,128)(2,1)S(1)}, u32[]{:S(2)}, u32[]{:S(2)}) collective-permute-start(bf16[656,128]{1,0:T(8,128)(2,1)S(1)} %pad_maximum_fusion.2), channel_id=1, source_target_pairs={{0,6},{2,4},{4,2},{6,0},{8,14},{10,12},{12,10},{14,8},{1,7},{3,5},... | collective-permute-start | bytes 503816 | tf_op jit(solution)/shard_map/ppermute | solution.py:482
  24.1 0.0 collective-permute-done.4
  24.2 7.0 %collective-permute-start.5 = (bf16[656,128]{1,0:T(8,128)(2,1)S(1)}, bf16[656,128]{1,0:T(8,128)(2,1)S(1)}, u32[]{:S(2)}, u32[]{:S(2)}) collective-permute-start(bf16[656,128]{1,0:T(8,128)(2,1)S(1)} %pad_maximum_fusion.1), channel_id=1, source_target_pairs={{0,12},{2,14},{4,8},{6,10},{8,4},{10,6},{12,0},{14,2},{1,13},{3,15... | collective-permute-start | bytes 503816 | tf_op jit(solution)/shard_map/ppermute | solution.py:482
  31.2 0.0 collective-permute-start.6
  31.2 0.0 collective-permute-start.7
  31.2 1.3 %collective-permute-done.3.refs_1_ = bf16[720,128]{1,0:T(8,128)(2,1)S(1)} collective-permute-done((bf16[720,128]{1,0:T(8,128)(2,1)S(1)}, bf16[720,128]{1,0:T(8,128)(2,1)S(1)}, u32[]{:S(2)}, u32[]{:S(2)}) %collective-permute-start.3) | collective-permute-done | bytes 184352 | tf_op jit(solution)/shard_map/ppermute | solution.py:482
  32.5 3.2 %collective-permute-done.5.refs_2_ = bf16[656,128]{1,0:T(8,128)(2,1)S(1)} collective-permute-done((bf16[656,128]{1,0:T(8,128)(2,1)S(1)}, bf16[656,128]{1,0:T(8,128)(2,1)S(1)}, u32[]{:S(2)}, u32[]{:S(2)}) %collective-permute-start.5) | collective-permute-done | bytes 167968 | tf_op jit(solution)/shard_map/ppermute | solution.py:482
  35.7 0.8 %collective-permute-done.6.refs_3_ = bf16[624,128]{1,0:T(8,128)(2,1)S(1)} collective-permute-done((bf16[624,128]{1,0:T(8,128)(2,1)S(1)}, bf16[624,128]{1,0:T(8,128)(2,1)S(1)}, u32[]{:S(2)}, u32[]{:S(2)}) %collective-permute-start.6) | collective-permute-done | bytes 159776 | tf_op jit(solution)/shard_map/ppermute | solution.py:482
  36.5 0.8 %collective-permute-done.7.refs_4_ = bf16[624,128]{1,0:T(8,128)(2,1)S(1)} collective-permute-done((bf16[624,128]{1,0:T(8,128)(2,1)S(1)}, bf16[624,128]{1,0:T(8,128)(2,1)S(1)}, u32[]{:S(2)}, u32[]{:S(2)}) %collective-permute-start.7) | collective-permute-done | bytes 159776 | tf_op jit(solution)/shard_map/ppermute | solution.py:482
  37.3 0.8 %statistics.1 = (bf16[256,128]{1,0:T(8,128)(2,1)S(1)}, f32[272,128]{1,0:T(8,128)S(1)}, f32[8,256]{1,0:T(8,128)S(1)}) custom-call(bf16[624,128]{1,0:T(8,128)(2,1)S(1)} %get-tuple-element.26.refs_0_, bf16[720,128]{1,0:T(8,128)(2,1)S(1)} %collective-permute-done.3.refs_1_, bf16[656,128]{1,0:T(8,128)(2,1)S(1)} %collective-permute-done.5.refs_2_, ...), custom_call_target="tpu_custom_call" | custom-call | tf_op jit(solution)/shard_map/statistics/pallas_call | solution.py:363
  38.1 1.4 %collective-permute-done.9.got_ref = f32[272,128]{1,0:T(8,128)S(1)} collective-permute-done((f32[272,128]{1,0:T(8,128)S(1)}, f32[272,128]{1,0:T(8,128)S(1)}, u32[]{:S(2)}, u32[]{:S(2)}) %collective-permute-start.9) | collective-permute-done | bytes 139296 | tf_op jit(solution)/shard_map/ppermute | solution.py:531
  39.5 2.0 %subtract.1 = (bf16[2,16,64,256]{3,2,1,0:T(8,128)(2,1)}, f32[2,33]{1,0:T(2,128)}) custom-call(f32[8,256]{1,0:T(8,128)S(1)} %get-tuple-element.45.lag_ref, f32[2,33]{1,0:T(2,128)S(1)} %bitcast.8, f32[2,80,256]{2,1,0:T(8,128)S(1)} %copy-done.1, bf16[256,128]{1,0:T(8,128)(2,1)S(1)} %get-tuple-element.46.own_ref, f32[272,128]{1,0:T(8,128)S(1)} %collective-permute-done.9.got_ref, ...), custom_call_target="tpu_custom_call" | custom-call | tf_op jit(solution)/shard_map/subtract/pallas_call | solution.py:448
  (19 shorter events, 0.2 us)
Async XLA Ops:
  0.6 11.7 %copy-start.1 = (f32[2,80,256]{2,1,0:T(8,128)S(1)}, f32[2,80,256]{2,1,0:T(8,128)}, u32[]{:S(2)}) copy-start(f32[2,80,256]{2,1,0:T(8,128)} %constant.2.clone.t_ref.refs_8_.table_ref) | copy-start | bytes 491524
  0.6 11.7 %copy-start = (bf16[1,1,32,64,256]{4,3,2,1,0:T(8,128)(2,1)S(1)}, bf16[1,1,32,64,256]{4,3,2,1,0:T(8,128)(2,1)}, u32[]{:S(2)}) copy-start(bf16[1,1,32,64,256]{4,3,2,1,0:T(8,128)(2,1)} %param.5) | copy-start | bytes 3145732
  0.7 38.8 %copy-start.2 = (f32[1,1,1,2,33]{4,3,2,1,0:T(2,128)S(1)}, f32[1,1,1,2,33]{4,3,2,1,0:T(2,128)}, u32[]{:S(2)}) copy-start(f32[1,1,1,2,33]{4,3,2,1,0:T(2,128)} %param.6) | copy-start | bytes 796
  9.3 8.9 %collective-permute-start = (bf16[624,128]{1,0:T(8,128)(2,1)S(1)}, bf16[624,128]{1,0:T(8,128)(2,1)S(1)}, u32[]{:S(2)}, u32[]{:S(2)}) collective-permute-start(bf16[624,128]{1,0:T(8,128)(2,1)S(1)} %get-tuple-element.28), channel_id=1, source_target_pairs={{0,2},{2,0},{4,6},{6,4},{8,10},{10,8},{12,14},{14,12},{1,3},{3,1},... | collective-permute-start | bytes 479240 | tf_op jit(solution)/shard_map/ppermute | solution.py:482
  12.8 1.4 %collective-permute-start.1 = (f32[16,16,128]{2,1,0:T(8,128)S(1)}, f32[16,16,128]{2,1,0:T(8,128)S(1)}, u32[]{:S(2)}, u32[]{:S(2)}) collective-permute-start(f32[16,16,128]{2,1,0:T(8,128)S(1)} %get-tuple-element.32), channel_id=1, source_target_pairs={{0,1},{1,0},{2,3},{3,2},{4,5},{5,4},{6,7},{7,6},{8,9},{9,8},{10,11... | collective-permute-start | bytes 393224 | tf_op jit(solution)/shard_map/ppermute | solution.py:494
  14.4 3.8 %collective-permute-start.2 = (f32[32,128]{1,0:T(8,128)S(1)}, f32[32,128]{1,0:T(8,128)S(1)}, u32[]{:S(2)}, u32[]{:S(2)}) collective-permute-start(f32[32,128]{1,0:T(8,128)S(1)} %get-tuple-element.34), channel_id=1, source_target_pairs={{0,2},{2,0},{4,6},{6,4},{8,10},{10,8},{12,14},{14,12},{1,3},{3,1},... | collective-permute-start | bytes 49160 | tf_op jit(solution)/shard_map/ppermute | solution.py:482
  18.3 5.8 %collective-permute-start.4 = (bf16[624,128]{1,0:T(8,128)(2,1)S(1)}, bf16[624,128]{1,0:T(8,128)(2,1)S(1)}, u32[]{:S(2)}, u32[]{:S(2)}) collective-permute-start(bf16[624,128]{1,0:T(8,128)(2,1)S(1)} %get-tuple-element.38), channel_id=1, source_target_pairs={{0,2},{2,0},{4,6},{6,4},{8,10},{10,8},{12,14},{14,12},{1,3},{3,1},... | collective-permute-start | bytes 479240 | tf_op jit(solution)/shard_map/ppermute | solution.py:482
  18.7 13.8 %collective-permute-start.3 = (bf16[720,128]{1,0:T(8,128)(2,1)S(1)}, bf16[720,128]{1,0:T(8,128)(2,1)S(1)}, u32[]{:S(2)}, u32[]{:S(2)}) collective-permute-start(bf16[720,128]{1,0:T(8,128)(2,1)S(1)} %pad_maximum_fusion), channel_id=1, source_target_pairs={{0,8},{2,10},{4,12},{6,14},{8,0},{10,2},{12,4},{14,6},{1,9},{3,11}... | collective-permute-start | bytes 552968 | tf_op jit(solution)/shard_map/ppermute | solution.py:482
  21.5 9.7 %collective-permute-start.8 = (bf16[656,128]{1,0:T(8,128)(2,1)S(1)}, bf16[656,128]{1,0:T(8,128)(2,1)S(1)}, u32[]{:S(2)}, u32[]{:S(2)}) collective-permute-start(bf16[656,128]{1,0:T(8,128)(2,1)S(1)} %pad_maximum_fusion.2), channel_id=1, source_target_pairs={{0,6},{2,4},{4,2},{6,0},{8,14},{10,12},{12,10},{14,8},{1,7},{3,5},... | collective-permute-start | bytes 503816 | tf_op jit(solution)/shard_map/ppermute | solution.py:482
  24.2 11.5 %collective-permute-start.5 = (bf16[656,128]{1,0:T(8,128)(2,1)S(1)}, bf16[656,128]{1,0:T(8,128)(2,1)S(1)}, u32[]{:S(2)}, u32[]{:S(2)}) collective-permute-start(bf16[656,128]{1,0:T(8,128)(2,1)S(1)} %pad_maximum_fusion.1), channel_id=1, source_target_pairs={{0,12},{2,14},{4,8},{6,10},{8,4},{10,6},{12,0},{14,2},{1,13},{3,15... | collective-permute-start | bytes 503816 | tf_op jit(solution)/shard_map/ppermute | solution.py:482
  31.2 5.3 %collective-permute-start.6 = (bf16[624,128]{1,0:T(8,128)(2,1)S(1)}, bf16[624,128]{1,0:T(8,128)(2,1)S(1)}, u32[]{:S(2)}, u32[]{:S(2)}) collective-permute-start(bf16[624,128]{1,0:T(8,128)(2,1)S(1)} %get-tuple-element.42), channel_id=1, source_target_pairs={{0,2},{2,0},{4,6},{6,4},{8,10},{10,8},{12,14},{14,12},{1,3},{3,1},... | collective-permute-start | bytes 479240 | tf_op jit(solution)/shard_map/ppermute | solution.py:482
  31.2 6.1 %collective-permute-start.7 = (bf16[624,128]{1,0:T(8,128)(2,1)S(1)}, bf16[624,128]{1,0:T(8,128)(2,1)S(1)}, u32[]{:S(2)}, u32[]{:S(2)}) collective-permute-start(bf16[624,128]{1,0:T(8,128)(2,1)S(1)} %get-tuple-element.43), channel_id=1, source_target_pairs={{0,4},{2,6},{4,0},{6,2},{8,12},{10,14},{12,8},{14,10},{1,5},{3,7},... | collective-permute-start | bytes 479240 | tf_op jit(solution)/shard_map/ppermute | solution.py:482
  38.1 1.4 %collective-permute-start.9 = (f32[272,128]{1,0:T(8,128)S(1)}, f32[272,128]{1,0:T(8,128)S(1)}, u32[]{:S(2)}, u32[]{:S(2)}) collective-permute-start(f32[272,128]{1,0:T(8,128)S(1)} %get-tuple-element.47), channel_id=1, source_target_pairs={{0,1},{1,0},{2,3},{3,2},{4,5},{5,4},{6,7},{7,6},{8,9},{9,8},{10,11... | collective-permute-start | bytes 417800 | tf_op jit(solution)/shard_map/ppermute | solution.py:531
